TPU v7x, 512 devices: a whole 4x8x8 slice. The times are simulated.
512 devices in a mesh: run: 16 (over z_lo, y), tile: 32 (over x, z_hi, core).
Axes of the slice: x: 4, y: 8, z: 8 (z_hi: 4, z_lo: 2; z = z_hi * 2 + z_lo), core: 2. Of those that a mesh axis runs over, the one named last changes fastest.
Arguments:
- state: float32 [16, 5, 8, 256, 128], P('run', None, None, 'tile'), as said below
- spacing_index: int32 [16], P('run'), may hold values from 1 to 3
- strength_index: int32 [16], P('run'), may hold values from 0 to 3
- obs_offsets: int32 [8, 2], replicated, may hold values from 0 to 1
Outputs:
- final_state: float32 [16, 5, 8, 256, 128], P('run', None, None, 'tile')
- misfit: float32 [16], P('run')
Inputs may be any that keep to these rules, and one draw needn't show every extreme that they name: `state`: components 0 and 4 (density and temperature) lie between 0.8 and 1.2; velocities are of order 0.1.
All inputs are finite; a program needn't handle non-finite values.
Results may differ from a plain program's by a relative error of at most 0.0003.
Values sent between devices are 32-bit elements; how exact they have to be, the bound alone decides.
No kernel may reach another device: no remote copies, remote signals or barrier semaphores. Data moves between devices by JAX's collectives and lax.ppermute only.
A program may use at most 64 MiB of HBM per device.

v0:
```python
import jax
import jax.numpy as jnp
from jax import lax
from jax.sharding import PartitionSpec as P

STEPS = 3


time_step = 0.05
viscosity = 0.05
conduction_coefficient = 0.05
adiabatic_index = 1.4
gravity = 0.5
hot_wall = 1.2
cold_wall = 0.8


def with_halo(block, sides, width):
    for axis, dim in sides:
        count = lax.axis_size(axis)
        forward = [(i, i + 1) for i in range(count - 1)]
        forward.append((count - 1, 0))
        backward = [(target, source) for source, target in forward]
        low = lax.ppermute(
            lax.slice_in_dim(block, block.shape[dim] - width, None, axis=dim), axis, forward
        )
        high = lax.ppermute(lax.slice_in_dim(block, 0, width, axis=dim), axis, backward)
        block = jnp.concatenate([low, block, high], axis=dim)
    return block


def from_root(x, axis, root):
    mine = lax.axis_index(axis) == root
    return lax.psum(jnp.where(mine, x, jnp.zeros_like(x)), axis)


def pad_vertical(fields):
    signs = jnp.array([1.0, 1.0, 1.0, -1.0, -1.0], jnp.float32).reshape(5, 1, 1, 1)
    bottom_add = jnp.array([0.0, 0.0, 0.0, 0.0, 2.0 * hot_wall], jnp.float32).reshape(5, 1, 1, 1)
    top_add = jnp.array([0.0, 0.0, 0.0, 0.0, 2.0 * cold_wall], jnp.float32).reshape(5, 1, 1, 1)
    bottom = signs * fields[:, :1] + bottom_add
    top = signs * fields[:, -1:] + top_add
    return jnp.concatenate([bottom, fields, top], axis=1)


def inner_domain(values):
    return values[..., 1:-1, 1:-1, :]


def deriv_x(values):
    return 0.5 * (values[..., 1:-1, 2:, :] - values[..., 1:-1, :-2, :])


def deriv_y(values):
    centre = inner_domain(values)
    return 0.5 * (jnp.roll(centre, -1, -1) - jnp.roll(centre, 1, -1))


def deriv_z(values):
    return 0.5 * (values[..., 2:, 1:-1, :] - values[..., :-2, 1:-1, :])


def second_derivative_sum(values):
    centre = inner_domain(values)
    total = values[..., 2:, 1:-1, :] + values[..., :-2, 1:-1, :]
    total = total + values[..., 1:-1, 2:, :] + values[..., 1:-1, :-2, :]
    total = total + jnp.roll(centre, -1, -1) + jnp.roll(centre, 1, -1)
    return total - 6.0 * centre


def tendency(xpadded):
    device_arrangement = pad_vertical(xpadded)
    matter_per_volume = device_arrangement[0]
    stream_speed_vector = device_arrangement[1:4]
    warmth_field = device_arrangement[4]
    mass_flux = (
        deriv_x(matter_per_volume * device_arrangement[1])
        + deriv_y(matter_per_volume * device_arrangement[2])
        + deriv_z(matter_per_volume * device_arrangement[3])
    )
    normal_stress_field = matter_per_volume * warmth_field
    centre_vel = inner_domain(stream_speed_vector)
    centre_den = inner_domain(matter_per_volume)
    middle_warmth_value = inner_domain(warmth_field)

    def transport_contribution(quantity):
        return (
            centre_vel[0] * deriv_x(quantity)
            + centre_vel[1] * deriv_y(quantity)
            + centre_vel[2] * deriv_z(quantity)
        )

    gradient = jnp.stack(
        [deriv_x(normal_stress_field), deriv_y(normal_stress_field), deriv_z(normal_stress_field)]
    )
    lift = jnp.array([0.0, 0.0, gravity], jnp.float32).reshape(3, 1, 1, 1)
    accel = (
        -transport_contribution(stream_speed_vector)
        - gradient / centre_den
        + viscosity * second_derivative_sum(stream_speed_vector)
        - lift
    )
    outflow_spread = (
        deriv_x(device_arrangement[1])
        + deriv_y(device_arrangement[2])
        + deriv_z(device_arrangement[3])
    )
    internal_warming = (
        -transport_contribution(warmth_field)
        - (adiabatic_index - 1.0) * middle_warmth_value * outflow_spread
        + conduction_coefficient * second_derivative_sum(warmth_field)
    )
    return jnp.concatenate([-mass_flux[None], accel, internal_warming[None]], axis=0)


def lattice(fields, offset_x, offset_y):
    count, planes, width_x, width_y = fields.shape
    partition_seeds = fields.reshape(count, planes, width_x // 2, 2, width_y // 2, 2)
    pick_x = offset_x.reshape(1, planes, 1, 1, 1)
    along_x = jnp.where(pick_x == 0, partition_seeds[:, :, :, 0], partition_seeds[:, :, :, 1])
    pick_y = offset_y.reshape(1, planes, 1, 1)
    return jnp.where(pick_y == 0, along_x[..., 0], along_x[..., 1])


def spread_blocks(points, spacing):
    count, planes, half_x, half_y = points.shape
    result = jnp.zeros((count, planes, 2 * half_x, 2 * half_y), jnp.float32)
    for stride in (2, 4, 8):
        half = stride // 2
        picked = points.reshape(count, planes, half_x // half, half, half_y // half, half)[
            :, :, :, 0, :, 0
        ]
        repeated = jnp.repeat(jnp.repeat(picked, stride, axis=2), stride, axis=3)
        result = jnp.where(spacing == stride, repeated, result)
    return result


def shards(state, spacing_index, strength_index, obs_offsets):
    fields = state[0]
    offset_x = obs_offsets[:, 0]
    offset_y = obs_offsets[:, 1]
    spacing = jnp.left_shift(jnp.ones_like(spacing_index[0]), spacing_index[0])
    is_nature = lax.axis_index("run") == 0
    strength = jnp.where(is_nature, 0.0, 0.5 * jnp.exp2(strength_index[0].astype(jnp.float32)))
    cells = fields.shape[1] * fields.shape[2] * lax.axis_size("tile") * fields.shape[3]
    observed = jnp.zeros((4,) + fields.shape[1:], jnp.float32)
    for iteration in range(STEPS):
        xpadded = with_halo(fields, (("tile", 2),), 1)
        nature_points = lattice(from_root(fields[1:5], "run", 0), offset_x, offset_y)
        observed = spread_blocks(lattice(fields[1:5], offset_x, offset_y) - nature_points, spacing)
        nudged = tendency(xpadded) - strength * jnp.pad(observed, ((1, 0), (0, 0), (0, 0), (0, 0)))
        fields = fields + time_step * nudged
    local_sum = jnp.sum(observed[3] * observed[3])
    total = lax.psum(local_sum, "tile")
    return (fields[None], (total / cells).reshape(1))


def solution(mesh):
    placed = (P("run", None, None, "tile", None), P("run"), P("run"), P())
    return jax.shard_map(
        shards,
        mesh=mesh,
        in_specs=placed,
        out_specs=(P("run", None, None, "tile", None), P("run")),
        check_vma=False,
    )
```

profile of v0, /device:TPU:1, one launch (start us, length us, event | category | flops | bytes accessed | tf_op | source)
XLA Modules:
  0.0 575.1 jit_solution(16546901599556299854)
XLA Ops:
  7.2 0.9 copy.853
  8.2 7.2 %collective-permute-start = (f32[5,8,1,128]{3,1,2,0:T(8,128)S(1)}, f32[5,8,1,128]{3,1,2,0:T(8,128)S(1)}, u32[]{:S(2)}, u32[]{:S(2)}) collective-permute-start(f32[5,8,1,128]{3,1,2,0:T(8,128)S(1)} %get-tuple-element.96), channel_id=1, source_target_pairs={{0,1},{1,2},{2,3},{3,4},{4,5},{5,6},{6,7},{7,8},{8,9},{9,10},{10,1... | collective-permute-start | bytes 61448 | tf_op jit(solution)/shard_map/ppermute | solution.py:24
  15.4 3.5 collective-permute-start.1
  18.9 0.9 fusion.133
  19.8 0.6 copy.768
  20.4 1.6 copy.769
  23.3 0.6 copy.762
  24.5 1.1 fusion.123
  25.9 0.8 copy.827
  29.7 0.7 fusion.73
  30.4 131.9 %all-reduce.7.cloned.1.call-done = f32[4,8,4,2,64,2]{1,4,2,0,5,3:T(8,128)} async-done(((f32[4,8,4,2,64,2]{1,4,2,0,5,3:T(8,128)}), f32[4,8,4,2,64,2]{1,4,2,0,5,3:T(8,128)}) %all-reduce.7.cloned.1.call-update) | async-done | bytes 131088 | tf_op jit(solution)/shard_map/psum | solution.py:34
  162.3 1.7 fusion.2
  164.7 0.9 fusion.19
  165.7 1.0 copy.773
  166.7 1.2 broadcast_in_dim.136
  168.5 1.4 fusion.11
  170.7 0.6 copy.777
  171.7 0.6 fusion.132
  172.3 0.7 fusion.130
  173.0 0.6 fusion.90
  174.2 1.6 copy.788
  176.6 1.2 fusion.118
  177.8 14.5 %collective-permute-start.2 = (f32[5,8,1,128]{3,1,2,0:T(8,128)S(1)}, f32[5,8,1,128]{3,1,2,0:T(8,128)S(1)}, u32[]{:S(2)}, u32[]{:S(2)}) collective-permute-start(f32[5,8,1,128]{3,1,2,0:T(8,128)S(1)} %copy-done.28), channel_id=1, source_target_pairs={{0,1},{1,2},{2,3},{3,4},{4,5},{5,6},{6,7},{7,8},{8,9},{9,10},{10,1... | collective-permute-start | bytes 61448 | tf_op jit(solution)/shard_map/ppermute | solution.py:24
  192.3 2.1 collective-permute-start.3
  194.5 3.8 collective-permute-done.3
  198.6 0.6 fusion.144
  199.2 0.7 fusion.145
  200.0 0.7 slice_bitcast_fusion.29
  200.7 0.6 fusion.62
  201.4 0.7 fusion.147
  202.1 0.7 fusion.148
  202.7 0.7 fusion.149
  203.4 0.7 fusion.150
  204.7 0.9 fusion.85
  205.5 1.6 fusion.57
  207.2 1.6 fusion.29
  208.7 0.9 fusion.66
  209.6 111.1 %all-reduce.9.cloned.1.call-done = f32[4,8,4,2,64,2]{1,4,2,0,5,3:T(8,128)} async-done(((f32[4,8,4,2,64,2]{1,4,2,0,5,3:T(8,128)}), f32[4,8,4,2,64,2]{1,4,2,0,5,3:T(8,128)}) %all-reduce.9.cloned.1.call-update) | async-done | bytes 131088 | tf_op jit(solution)/shard_map/psum | solution.py:34
  320.7 1.9 fusion.5
  325.7 1.4 fusion.20
  328.5 0.6 fusion.128
  329.1 0.6 fusion.126
  329.8 0.6 fusion.93
  331.0 1.6 copy.807
  333.3 1.2 fusion.117
  334.5 14.5 %collective-permute-start.4 = (f32[5,8,1,128]{3,1,2,0:T(8,128)S(1)}, f32[5,8,1,128]{3,1,2,0:T(8,128)S(1)}, u32[]{:S(2)}, u32[]{:S(2)}) collective-permute-start(f32[5,8,1,128]{3,1,2,0:T(8,128)S(1)} %copy-done.29), channel_id=1, source_target_pairs={{0,1},{1,2},{2,3},{3,4},{4,5},{5,6},{6,7},{7,8},{8,9},{9,10},{10,1... | collective-permute-start | bytes 61448 | tf_op jit(solution)/shard_map/ppermute | solution.py:24
  349.0 1.9 collective-permute-start.5
  351.1 4.0 collective-permute-done.5
  355.3 0.7 fusion.137
  356.0 0.7 fusion.138
  356.9 0.6 fusion.46
  357.5 0.7 fusion.140
  358.2 0.7 fusion.141
  358.9 0.7 fusion.142
  359.6 0.7 fusion.143
  360.9 1.6 fusion.41
  362.6 0.9 fusion.25
  363.5 0.9 fusion.50
  364.4 113.3 %all-reduce.11.cloned.1.call-done = f32[4,8,4,2,64,2]{1,4,2,0,5,3:T(8,128)} async-done(((f32[4,8,4,2,64,2]{1,4,2,0,5,3:T(8,128)}), f32[4,8,4,2,64,2]{1,4,2,0,5,3:T(8,128)}) %all-reduce.11.cloned.1.call-update) | async-done | bytes 131088 | tf_op jit(solution)/shard_map/psum | solution.py:34
  477.7 1.9 fusion.4
  482.6 1.4 fusion.21
  485.2 0.6 fusion.35
  485.9 0.7 copy.818
  486.6 80.2 %psum.31 = f32[]{:T(128)} all-reduce(f32[]{:T(128)} %fusion.35), channel_id=1, replica_groups=mesh['run'=16,'tile'=32] {'tile'}, use_global_device_ids=true, to_apply=%region_4.5 | all-reduce | flops 1 | bytes 8 | tf_op jit(solution)/shard_map/psum | solution.py:154
  (223 shorter events, 19.0 us)
Async XLA Ops:
  7.2 155.1 %all-reduce.7.cloned.1.call-start = ((), (), s32[]{:S(2)}) async-start(), calls=%async_computation | async-start | bytes 4194304 | tf_op jit(solution)/shard_map/psum | solution.py:34
  8.2 19.8 %collective-permute-start = (f32[5,8,1,128]{3,1,2,0:T(8,128)S(1)}, f32[5,8,1,128]{3,1,2,0:T(8,128)S(1)}, u32[]{:S(2)}, u32[]{:S(2)}) collective-permute-start(f32[5,8,1,128]{3,1,2,0:T(8,128)S(1)} %get-tuple-element.96), channel_id=1, source_target_pairs={{0,1},{1,2},{2,3},{3,4},{4,5},{5,6},{6,7},{7,8},{8,9},{9,10},{10,1... | collective-permute-start | bytes 61448 | tf_op jit(solution)/shard_map/ppermute | solution.py:24
  15.4 12.6 %collective-permute-start.1 = (f32[5,8,1,128]{3,1,2,0:T(8,128)S(1)}, f32[5,8,1,128]{3,1,2,0:T(8,128)S(1)}, u32[]{:S(2)}, u32[]{:S(2)}) collective-permute-start(f32[5,8,1,128]{3,1,2,0:T(8,128)S(1)} %get-tuple-element.97), channel_id=1, source_target_pairs={{1,0},{2,1},{3,2},{4,3},{5,4},{6,5},{7,6},{8,7},{9,8},{10,9},{11,1... | collective-permute-start | bytes 61448 | tf_op jit(solution)/shard_map/ppermute | solution.py:27
  22.1 0.7 copy-start.42
  22.1 298.6 %all-reduce.9.cloned.1.call-start = ((), (), s32[]{:S(2)}) async-start(), calls=%async_computation.1 | async-start | bytes 4194304 | tf_op jit(solution)/shard_map/psum | solution.py:34
  23.3 139.0 %copy-start.30 = (pred[8]{0:T(512)(128)(4,1)}, pred[8]{0:T(512)(128)(4,1)S(1)}, u32[]{:S(2)}) copy-start(pred[8]{0:T(512)(128)(4,1)S(1)} %get-tuple-element.154) | copy-start | bytes 28
  24.4 3.5 copy-start.34
  24.5 3.5 copy-start.36
  24.5 3.5 copy-start.39
  25.6 139.1 %copy-start.2 = (f32[4,8,4,64,1]{1,4,3,2,0:T(1,128)}, f32[4,8,4,64,1]{1,4,3,2,0:T(1,128)S(1)}, u32[]{:S(2)}) copy-start(f32[4,8,4,64,1]{1,4,3,2,0:T(1,128)S(1)} %get-tuple-element.30) | copy-start | bytes 98308
  25.6 139.1 %copy-start.3 = (f32[4,8,4,64,1]{1,4,3,2,0:T(1,128)}, f32[4,8,4,64,1]{1,4,3,2,0:T(1,128)S(1)}, u32[]{:S(2)}) copy-start(f32[4,8,4,64,1]{1,4,3,2,0:T(1,128)S(1)} %get-tuple-element.31) | copy-start | bytes 98308
  28.1 1.4 copy-start.32
  30.4 133.9 %copy-start.23 = (f32[4,8,1,1,16,1]{4,1,0,5,3,2:T(8,128)S(1)}, f32[4,8,1,1,16,1]{4,1,0,5,3,2:T(8,128)}, u32[]{:S(2)}) copy-start(f32[4,8,1,1,16,1]{4,1,0,5,3,2:T(8,128)} %copy.827) | copy-start | bytes 6148
  30.4 133.9 %copy-start.24 = (pred[8]{0:T(512)(128)(4,1)S(1)}, pred[8]{0:T(512)(128)(4,1)}, u32[]{:S(2)}) copy-start(pred[8]{0:T(512)(128)(4,1)} %get-tuple-element.155) | copy-start | bytes 28
  166.7 1.8 copy-start.25
  170.7 0.9 copy-start.4
  170.7 0.9 copy-start.22
  175.9 301.8 %all-reduce.11.cloned.1.call-start = ((), (), s32[]{:S(2)}) async-start(), calls=%async_computation.2 | async-start | bytes 4194304 | tf_op jit(solution)/shard_map/psum | solution.py:34
  176.5 1.2 copy-start.28
  176.5 21.8 %copy-start.35 = (f32[5]{0:T(128)S(1)}, f32[5]{0:T(128)}, u32[]{:S(2)}) copy-start(f32[5]{0:T(128)} %constant.55.clone) | copy-start | bytes 64
  176.6 21.8 %copy-start.37 = (f32[5]{0:T(128)S(1)}, f32[5]{0:T(128)}, u32[]{:S(2)}) copy-start(f32[5]{0:T(128)} %constant.56.clone) | copy-start | bytes 64
  176.6 21.8 %copy-start.40 = (f32[5]{0:T(128)S(1)}, f32[5]{0:T(128)}, u32[]{:S(2)}) copy-start(f32[5]{0:T(128)} %constant.57.clone) | copy-start | bytes 64
  177.8 16.7 %collective-permute-start.2 = (f32[5,8,1,128]{3,1,2,0:T(8,128)S(1)}, f32[5,8,1,128]{3,1,2,0:T(8,128)S(1)}, u32[]{:S(2)}, u32[]{:S(2)}) collective-permute-start(f32[5,8,1,128]{3,1,2,0:T(8,128)S(1)} %copy-done.28), channel_id=1, source_target_pairs={{0,1},{1,2},{2,3},{3,4},{4,5},{5,6},{6,7},{7,8},{8,9},{9,10},{10,1... | collective-permute-start | bytes 61448 | tf_op jit(solution)/shard_map/ppermute | solution.py:24
  192.3 6.0 %collective-permute-start.3 = (f32[5,8,1,128]{3,1,2,0:T(8,128)S(1)}, f32[5,8,1,128]{3,1,2,0:T(8,128)S(1)}, u32[]{:S(2)}, u32[]{:S(2)}) collective-permute-start(f32[5,8,1,128]{3,1,2,0:T(8,128)S(1)} %get-tuple-element.88), channel_id=1, source_target_pairs={{1,0},{2,1},{3,2},{4,3},{5,4},{6,5},{7,6},{8,7},{9,8},{10,9},{11,1... | collective-permute-start | bytes 61448 | tf_op jit(solution)/shard_map/ppermute | solution.py:27
  198.5 8.6 %copy-start.14 = (f32[3,8,8,127]{3,1,2,0:T(8,128)S(1)}, f32[3,8,8,127]{3,1,2,0:T(8,128)}, u32[]{:S(2)}) copy-start(f32[3,8,8,127]{3,1,2,0:T(8,128)} %get-tuple-element.83) | copy-start | bytes 292612
  198.5 8.6 %copy-start.15 = (f32[3,8,8,127]{3,1,2,0:T(8,128)S(1)}, f32[3,8,8,127]{3,1,2,0:T(8,128)}, u32[]{:S(2)}) copy-start(f32[3,8,8,127]{3,1,2,0:T(8,128)} %get-tuple-element.84) | copy-start | bytes 292612
  198.5 8.6 %copy-start.19 = (f32[8,8,128]{2,0,1:T(8,128)S(1)}, f32[8,8,128]{2,0,1:T(8,128)}, u32[]{:S(2)}) copy-start(f32[8,8,128]{2,0,1:T(8,128)} %get-tuple-element.82) | copy-start | bytes 98308
  198.6 8.6 %copy-start.33 = (f32[3]{0:T(128)S(1)}, f32[3]{0:T(128)}, u32[]{:S(2)}) copy-start(f32[3]{0:T(128)} %constant.68) | copy-start | bytes 40
  200.0 120.7 %copy-start.1 = (f32[4,8,4,1,64,2]{1,5,4,3,2,0:T(2,128)S(1)}, f32[4,8,4,1,64,2]{1,5,4,3,2,0:T(2,128)}, u32[]{:S(2)}) copy-start(f32[4,8,4,1,64,2]{1,5,4,3,2,0:T(2,128)} %get-tuple-element.21) | copy-start | bytes 196612
  200.0 120.7 %copy-start.31 = (pred[8]{0:T(512)(128)(4,1)S(1)}, pred[8]{0:T(512)(128)(4,1)}, u32[]{:S(2)}) copy-start(pred[8]{0:T(512)(128)(4,1)} %copy-done.30) | copy-start | bytes 28
  322.6 0.7 copy-start.26
  322.7 0.8 copy-start.7
  322.7 1.0 copy-start.8
  323.3 1.3 copy-start.11
  323.3 1.3 copy-start.12
  327.5 0.9 copy-start.16
  327.5 0.9 copy-start.21
  333.3 1.2 copy-start.29
  333.3 15.7 %copy-start.27 = (f32[5,8,1,128]{3,1,2,0:T(8,128)S(1)}, f32[5,8,1,128]{3,1,2,0:T(8,128)}, u32[]{:S(2)}) copy-start(f32[5,8,1,128]{3,1,2,0:T(8,128)} %get-tuple-element.77) | copy-start | bytes 61444
  333.3 21.8 %copy-start.38 = (f32[5]{0:T(128)S(1)}, f32[5]{0:T(128)}, u32[]{:S(2)}) copy-start(f32[5]{0:T(128)} %constant.56.clone) | copy-start | bytes 64
  333.3 21.8 %copy-start.41 = (f32[5]{0:T(128)S(1)}, f32[5]{0:T(128)}, u32[]{:S(2)}) copy-start(f32[5]{0:T(128)} %constant.57.clone) | copy-start | bytes 64
  334.5 16.5 %collective-permute-start.4 = (f32[5,8,1,128]{3,1,2,0:T(8,128)S(1)}, f32[5,8,1,128]{3,1,2,0:T(8,128)S(1)}, u32[]{:S(2)}, u32[]{:S(2)}) collective-permute-start(f32[5,8,1,128]{3,1,2,0:T(8,128)S(1)} %copy-done.29), channel_id=1, source_target_pairs={{0,1},{1,2},{2,3},{3,4},{4,5},{5,6},{6,7},{7,8},{8,9},{9,10},{10,1... | collective-permute-start | bytes 61448 | tf_op jit(solution)/shard_map/ppermute | solution.py:24
  349.0 6.0 %collective-permute-start.5 = (f32[5,8,1,128]{3,1,2,0:T(8,128)S(1)}, f32[5,8,1,128]{3,1,2,0:T(8,128)S(1)}, u32[]{:S(2)}, u32[]{:S(2)}) collective-permute-start(f32[5,8,1,128]{3,1,2,0:T(8,128)S(1)} %copy-done.27), channel_id=1, source_target_pairs={{1,0},{2,1},{3,2},{4,3},{5,4},{6,5},{7,6},{8,7},{9,8},{10,9},{11,1... | collective-permute-start | bytes 61448 | tf_op jit(solution)/shard_map/ppermute | solution.py:27
  355.3 7.3 %copy-start.13 = (f32[3,8,8,127]{3,1,2,0:T(8,128)S(1)}, f32[3,8,8,127]{3,1,2,0:T(8,128)}, u32[]{:S(2)}) copy-start(f32[3,8,8,127]{3,1,2,0:T(8,128)} %get-tuple-element.73) | copy-start | bytes 292612
  355.3 7.3 %copy-start.17 = (f32[8,8,128]{2,0,1:T(8,128)S(1)}, f32[8,8,128]{2,0,1:T(8,128)}, u32[]{:S(2)}) copy-start(f32[8,8,128]{2,0,1:T(8,128)} %get-tuple-element.69) | copy-start | bytes 98308
  355.3 7.3 %copy-start.18 = (f32[8,8,128]{2,0,1:T(8,128)S(1)}, f32[8,8,128]{2,0,1:T(8,128)}, u32[]{:S(2)}) copy-start(f32[8,8,128]{2,0,1:T(8,128)} %get-tuple-element.70) | copy-start | bytes 98308
  356.8 120.9 %copy-start = (f32[4,8,4,1,64,2]{1,5,4,3,2,0:T(2,128)S(1)}, f32[4,8,4,1,64,2]{1,5,4,3,2,0:T(2,128)}, u32[]{:S(2)}) copy-start(f32[4,8,4,1,64,2]{1,5,4,3,2,0:T(2,128)} %get-tuple-element.19) | copy-start | bytes 196612
  479.6 0.8 copy-start.5
  479.6 1.0 copy-start.6
  479.7 1.7 copy-start.9
  479.7 1.7 copy-start.10
  484.4 1.4 copy-start.20
Sparse Core Ops, SparseCore 0:
  22.2 140.0 all-reduce.6
  176.0 144.6 all-reduce.8
  332.8 144.8 all-reduce.10
where the time goes:
time: 576 us; the launch traced here: 575 us
  waiting for transfers between devices  364 us (63%)
  blocking collectives  80.2 us (14%)
  starting transfers between devices  43.9 us (8%)
  local copies, waits for them, and re-layouts  42.3 us (7%)
  other arithmetic  26.7 us (5%)
  between operations  18 us (3%)
    psum x3, waiting for transfers between devices, from_root(): return lax.psum(jnp.where(mine, x, jnp.zeros_like(x)), axis)  356 us
    psum x1, blocking collectives, shards(): total = lax.psum(local_sum, 'tile')  80.2 us
    ppermute x3, starting transfers between devices, with_halo(): lax.ppermute(lax.slice_in_dim(block, block.shape[dim] - width, None, axis...  36.2 us
  transfers between devices with their start and end apart: 9, of which 5 were waited for; matrix products, arithmetic and copies ran while one was open for 6% of the time, Pallas kernels for 0%

commit v1 on v0

v1 whole, which is shorter than its diff:
```python
import jax
import jax.numpy as jnp
from jax import lax
from jax.experimental import pallas as pl
from jax.experimental.pallas import tpu as pltpu
from jax.sharding import PartitionSpec as P

RUNS = 16
TILES = 32
PLANES = 8
CELLS = 8 * 256 * 128

DT = 0.05
VISC = 0.05
GAMMA1 = 0.4
GRAVITY = 0.5
HOT = 1.2
COLD = 0.8

ROWS = (8, 128)


def rolled(v, shift, axis):
    return pltpu.roll(v, shift % v.shape[axis], axis)


def sub_ids():
    return lax.broadcasted_iota(jnp.int32, ROWS, 0)


def lane_ids():
    return lax.broadcasted_iota(jnp.int32, ROWS, 1)


class Spread:
    def __init__(self, sp_ref, off_ref):
        sub, lane = sub_ids(), lane_ids()
        k = sp_ref[0]
        self.off = off_ref
        self.sub_odd = (sub & 1) == 1
        self.lane_odd = (lane & 1) == 1
        self.masks = []
        for ids in (sub, lane):
            self.masks.append(
                tuple(((ids & bit) != 0) & (k >= level) for bit, level in ((2, 2), (4, 3)))
            )
        self.sub1, self.lane1 = sub & 1, lane & 1

    def plane(self, z):
        return self.sub1 == self.off[z, 0], self.lane1 == self.off[z, 1]

    def __call__(self, e, keep):
        for axis in (0, 1):
            odd = (self.sub_odd, self.lane_odd)[axis]
            swapped = jnp.where(odd, rolled(e, 1, axis), rolled(e, -1, axis))
            e = jnp.where(keep[axis], e, swapped)
            for mask, shift in zip(self.masks[axis], (2, 4)):
                e = jnp.where(mask, rolled(e, shift, axis), e)
        return e


def ghosted(load):
    def get(c, z, t):
        if z < 0:
            edge = load(c, 0, t)
            return edge if c < 3 else -edge if c == 3 else 2.0 * HOT - edge
        if z >= PLANES:
            edge = load(c, PLANES - 1, t)
            return edge if c < 3 else -edge if c == 3 else 2.0 * COLD - edge
        return load(c, z, t)

    return get


def neighbours_x(a, b, sub):
    a1, b1 = rolled(a, -1, 0), rolled(b, -1, 0)
    a2, b2 = rolled(a, 1, 0), rolled(b, 1, 0)
    last, first = sub == 7, sub == 0
    return (
        (jnp.where(last, b1, a1), jnp.where(last, a1, b1)),
        (jnp.where(first, b2, a2), jnp.where(first, a2, b2)),
    )


def stepped(get, z, tiles, sub):
    centre = [[get(c, z, t) for t in (0, 1)] for c in range(5)]
    along_x = [neighbours_x(v[0], v[1], sub) for v in centre]
    result = []
    for t in tiles:
        c0 = [v[t] for v in centre]
        xn = [v[0][t] for v in along_x]
        xp = [v[1][t] for v in along_x]
        yn = [rolled(v, -1, 1) for v in c0]
        yp = [rolled(v, 1, 1) for v in c0]
        zn = [get(c, z + 1, t) for c in range(5)]
        zp = [get(c, z - 1, t) for c in range(5)]
        flux = (
            (xn[0] * xn[1] - xp[0] * xp[1])
            + (yn[0] * yn[2] - yp[0] * yp[2])
            + (zn[0] * zn[3] - zp[0] * zp[3])
        )
        scale = (0.5 * DT) / c0[0]
        grad = (
            xn[0] * xn[4] - xp[0] * xp[4],
            yn[0] * yn[4] - yp[0] * yp[4],
            zn[0] * zn[4] - zp[0] * zp[4],
        )
        new = [c0[0] - (0.5 * DT) * flux]
        div = None
        for q in range(1, 5):
            dx, dy, dz = xn[q] - xp[q], yn[q] - yp[q], zn[q] - zp[q]
            part = (None, dx, dy, dz, None)[q]
            if part is not None:
                div = part if div is None else div + part
            adv = c0[1] * dx + c0[2] * dy + c0[3] * dz
            six = ((xn[q] + xp[q]) + (yn[q] + yp[q])) + (zn[q] + zp[q])
            change = (DT * VISC) * (six - 6.0 * c0[q]) - (0.5 * DT) * adv
            if q < 4:
                change = change - grad[q - 1] * scale
                if q == 3:
                    change = change - DT * GRAVITY
            else:
                change = change - (0.5 * DT * GAMMA1) * (c0[4] * div)
            new.append(c0[q] + change)
        result.append(new)
    return result


def nudge_factor(st_ref):
    strength = 0.5 * lax.shift_left(jnp.int32(1), st_ref[0]).astype(jnp.float32)
    return jnp.where(lax.axis_index("run") == 0, 0.0, DT * strength)


def pack_kernel(sp_ref, off_ref, own_ref, y_ref, p_ref, q_ref, nat_ref, d_ref, near_ref, far_ref):
    spread = Spread(sp_ref, off_ref)
    sub = sub_ids()
    even = lax.rem(lax.axis_index("tile"), 2) == 0
    to_near = (sub >= 4) == even
    for z in range(PLANES):
        keep = spread.plane(z)
        for c in range(5):
            own = own_ref[c, z]
            nat = y_ref[c, z] + p_ref[c, z] + q_ref[c, z]
            nat_ref[c, z] = nat
            if c > 0:
                d = spread(own - nat, keep)
                d_ref[c - 1, z] = d
                own = jnp.where(sub == 5, rolled(d, -2, 0), own)
            other = rolled(nat, 4, 0)
            near_ref[c, z] = jnp.where(to_near, own, other)
            far_ref[c, z] = jnp.where(to_near, other, own)


def steps_kernel(
    sp_ref, st_ref, off_ref, own_ref, nat_ref, d_ref, near_ref, far_ref,
    own2_ref, beyond_ref, edge_ref, d2_ref, sum_ref, a_ref, b_ref, a1_ref, b1_ref, n2_ref,
):
    spread = Spread(sp_ref, off_ref)
    sub = sub_ids()
    even = lax.rem(lax.axis_index("tile"), 2) == 0
    from_near = (sub < 4) == even
    mu = nudge_factor(st_ref)
    for c in range(5):
        for z in range(PLANES):
            near, far = near_ref[c, z], far_ref[c, z]
            a_ref[c, z] = jnp.where(from_near, near, far)
            b_ref[c, z] = rolled(jnp.where(from_near, far, near), 4, 0)
    a = ghosted(lambda c, z, t: a_ref[c, z] if t else own_ref[c, z])
    b = ghosted(lambda c, z, t: b_ref[c, z] if t else nat_ref[c, z])
    for z in range(PLANES):
        keep = spread.plane(z)
        new_a = stepped(a, z, (0, 1), sub)
        new_b = stepped(b, z, (0, 1), sub)
        for t in (0, 1):
            for c in range(5):
                value = new_a[t][c]
                if c > 0:
                    if t == 0:
                        d = d_ref[c - 1, z]
                    else:
                        halo = a_ref[c, z]
                        d = spread(halo - b_ref[c, z], keep)
                        d = jnp.where(sub == 7, rolled(halo, 2, 0), d)
                    value = value - mu * d
                a1_ref[t, c, z] = value
                b1_ref[t, c, z] = new_b[t][c]
    a = ghosted(lambda c, z, t: a1_ref[t, c, z])
    b = ghosted(lambda c, z, t: b1_ref[t, c, z])
    total = jnp.zeros(ROWS, jnp.float32)
    for z in range(PLANES):
        keep = spread.plane(z)
        new_a = stepped(a, z, (0, 1), sub)
        new_b = stepped(b, z, (0,), sub)[0]
        for c in range(5):
            for t in (0, 1):
                value = new_a[t][c]
                if c > 0:
                    value = value - mu * spread(a1_ref[t, c, z] - b1_ref[t, c, z], keep)
                if t == 0:
                    own2_ref[c, z] = value
                    edge_ref[c, z : z + 1] = value[7:8]
                    if c > 0:
                        d = spread(value - new_b[c], keep)
                        d2_ref[c - 1, z] = d
                        if c == 4:
                            total = total + d * d
                else:
                    beyond_ref[c, z : z + 1] = value[0:1]
    sum_ref[...] = jnp.broadcast_to(jnp.sum(total, axis=0)[None, None], sum_ref.shape)


def last_kernel(st_ref, own_ref, beyond_ref, edge_ref, d_ref, sums_ref, out_ref, misfit_ref, h_ref):
    sub = sub_ids()
    mu = nudge_factor(st_ref)
    for c in range(5):
        for z in range(PLANES):
            h_ref[c, z] = jnp.where(
                sub == 0,
                jnp.broadcast_to(beyond_ref[c, z : z + 1], ROWS),
                jnp.broadcast_to(edge_ref[c, z : z + 1], ROWS),
            )
    a = ghosted(lambda c, z, t: h_ref[c, z] if t else own_ref[c, z])
    for z in range(PLANES):
        new = stepped(a, z, (0,), sub)[0]
        for c in range(5):
            value = new[c]
            if c > 0:
                value = value - mu * d_ref[c - 1, z]
            out_ref[c, z] = value
    misfit_ref[0] = jnp.sum(sums_ref[...]) * (1.0 / CELLS)


def f32(*shape):
    return jax.ShapeDtypeStruct(shape, jnp.float32)


VM = pl.BlockSpec(memory_space=pltpu.VMEM)
SM = pl.BlockSpec(memory_space=pltpu.SMEM)
PARAMS = pltpu.CompilerParams(vmem_limit_bytes=12 * 2**20)
BLOCK = (5, PLANES, 8, 128)
BLOCK4 = (4, PLANES, 8, 128)


def twice(pairs):
    return pairs + [(a + 8, b + 8) for a, b in pairs]


def shards(state, spacing_index, strength_index, obs_offsets):
    own = state[0]
    run = lax.axis_index("run")

    p = lax.ppermute(own, "run", [(0, 8)])
    y = jnp.where(run == 0, own, p)
    p = lax.ppermute(y, "run", twice([(0, 3)]))
    q = lax.ppermute(y, "run", twice([(0, 5)]))
    y = y + p + q
    p = lax.ppermute(y, "run", twice([(0, 1), (3, 4), (5, 6)]))
    q = lax.ppermute(y, "run", twice([(0, 7), (3, 2)]))

    nat, d, near, far = pl.pallas_call(
        pack_kernel,
        out_shape=(f32(*BLOCK), f32(*BLOCK4), f32(*BLOCK), f32(*BLOCK)),
        in_specs=[SM, SM, VM, VM, VM, VM],
        out_specs=(VM,) * 4,
        compiler_params=PARAMS,
        name="pack",
    )(spacing_index, obs_offsets, own, y, p, q)

    far = lax.ppermute(
        far, "tile", [(i, (i + 1) % TILES if i % 2 else (i - 1) % TILES) for i in range(TILES)]
    )
    near = lax.ppermute(near, "tile", [(i, i ^ 1) for i in range(TILES)])

    own2, beyond, edge, d2, sums = pl.pallas_call(
        steps_kernel,
        out_shape=(
            f32(*BLOCK), f32(5, PLANES, 128), f32(5, PLANES, 128), f32(*BLOCK4), f32(TILES, 1, 128)
        ),
        in_specs=[SM, SM, SM] + [VM] * 5,
        out_specs=(VM,) * 5,
        scratch_shapes=[
            pltpu.VMEM(BLOCK, jnp.float32),
            pltpu.VMEM(BLOCK, jnp.float32),
            pltpu.VMEM((2,) + BLOCK, jnp.float32),
            pltpu.VMEM((2,) + BLOCK, jnp.float32),
            pltpu.VMEM(BLOCK, jnp.float32),
        ],
        compiler_params=PARAMS,
        name="steps",
    )(spacing_index, strength_index, obs_offsets, own, nat, d, near, far)

    edge = lax.ppermute(edge, "tile", [(i, (i + 1) % TILES) for i in range(TILES)])
    sums = lax.all_to_all(sums, "tile", 0, 0)

    out, misfit = pl.pallas_call(
        last_kernel,
        out_shape=(f32(*BLOCK), f32(1)),
        in_specs=[SM] + [VM] * 5,
        out_specs=(VM, SM),
        scratch_shapes=[pltpu.VMEM(BLOCK, jnp.float32)],
        compiler_params=PARAMS,
        name="last",
    )(strength_index, own2, beyond, edge, d2, sums)
    return out[None], misfit


def solution(mesh):
    placed = (P("run", None, None, "tile", None), P("run"), P("run"), P())
    return jax.shard_map(
        shards,
        mesh=mesh,
        in_specs=placed,
        out_specs=(P("run", None, None, "tile", None), P("run")),
        check_vma=False,
    )
```

time: 576 us -> 74.9 us (0.13)
  waiting for transfers between devices: 364 us -> 16 us
  blocking collectives: 80.2 us -> 0 us
  local copies, waits for them, and re-layouts: 42.3 us -> 0.09 us
  other arithmetic: 26.7 us -> 0.96 us
  Pallas kernels: 0 us -> 17.8 us
  between operations: 18 us -> 2.05 us
  starting transfers between devices: 43.9 us -> 37 us
    psum x3 -> x0, waiting for transfers between devices: 356 us -> none  [from_root(): return lax.psum(jnp.where(mine, x, jnp.zeros_like(x)), axis)]
    psum x1 -> x0, blocking collectives: 80.2 us -> none  [shards(): total = lax.psum(local_sum, 'tile')]
    ppermute x6 -> x8, starting transfers between devices: 43.7 us -> 24.6 us  [the longest x1 6.99 us: shards(): near = lax.ppermute(near, 'tile', [(i, i ^ 1) for i in range(TILES)])]
    slice x64 -> x0, local copies, waits for them, and re-layouts: 18.7 us -> none  [the longest x31 11.3 us: deriv_y(): return 0.5 * (jnp.roll(centre, -1, -1) - jnp.roll(centre, 1, -1))]
    pallas_call x0 -> x3, Pallas kernels: none -> 17.8 us  [the longest x1 16 us: shards(): pl.pallas_call(steps_kernel, out_shape=(f32(*BLOCK), f32(5, PLANES, 128),...]
    all_to_all x0 -> x1, starting transfers between devices: none -> 12.5 us  [shards(): sums = lax.all_to_all(sums, 'tile', 0, 0)]
    reshape x9 -> x0, local copies, waits for them, and re-layouts: 8.23 us -> none  [the longest x3 4.89 us: lattice(): fields.reshape(count, planes, width_x // 2, 2, width_y // 2, 2)]
    select_n x10 -> x1, other arithmetic: 7.77 us -> 0.94 us  [shards(): y = jnp.where(run == 0, own, p)]
  transfers between devices with their start and end apart: 9 -> 9, of which waited for: 5 -> 8; matrix products, arithmetic and copies ran while one was open for 6% -> 0% of each run, Pallas kernels for 0% -> 0%
where the time goes in v1:
time: 74.9 us; the launch traced here: 73.9 us
  starting transfers between devices  37 us (49%)
  Pallas kernels  17.8 us (24%)
  waiting for transfers between devices  16 us (21%)
  between operations  2.05 us (3%)
  other arithmetic  0.96 us (1%)
    pallas_call x1, Pallas kernels, shards(): pl.pallas_call(steps_kernel, out_shape=(f32(*BLOCK), f32(5, PLANES, 128),...  16 us
    all_to_all x1, starting transfers between devices, shards(): sums = lax.all_to_all(sums, 'tile', 0, 0)  12.5 us
    ppermute x1, starting transfers between devices, shards(): near = lax.ppermute(near, 'tile', [(i, i ^ 1) for i in range(TILES)])  6.99 us
    ppermute x1, starting transfers between devices, shards(): p = lax.ppermute(own, 'run', [(0, 8)])  4.84 us
    ppermute x1, starting transfers between devices, shards(): lax.ppermute(edge, 'tile', [(i, (i + 1) % TILES) for i in range(TILES)])  4.44 us
    all_to_all x1, waiting for transfers between devices, shards(): sums = lax.all_to_all(sums, 'tile', 0, 0)  3.94 us
    ppermute x1, waiting for transfers between devices, shards(): lax.ppermute(far, 'tile', [(i, (i + 1) % TILES if i % 2 else (i - 1) % TI...  3.9 us
    ppermute x1, starting transfers between devices, shards(): lax.ppermute(far, 'tile', [(i, (i + 1) % TILES if i % 2 else (i - 1) % TI...  2.97 us
  transfers between devices with their start and end apart: 9, of which 8 were waited for; matrix products, arithmetic and copies ran while one was open for 0% of the time, Pallas kernels for 0%

profile of v1, /device:TPU:1, one launch (start us, length us, event | category | flops | bytes accessed | tf_op | source)
XLA Modules:
  0.0 73.9 jit_solution(4627341373935759597)
XLA Ops:
  0.6 4.8 %collective-permute-start = (f32[5,8,8,128]{3,2,1,0:T(8,128)}, f32[5,8,8,128]{3,2,1,0:T(8,128)S(1)}, u32[]{:S(2)}, u32[]{:S(2)}) collective-permute-start(f32[5,8,8,128]{3,2,1,0:T(8,128)} %bitcast.3), channel_id=1, source_target_pairs={{0,256},{1,257},{2,258},{3,259},{4,260},{5,261},{6,262},{7,263},{8... | collective-permute-start | bytes 491528 | tf_op jit(solution)/shard_map/ppermute | solution.py:252
  5.5 2.5 %collective-permute-done = f32[5,8,8,128]{3,2,1,0:T(8,128)S(1)} collective-permute-done((f32[5,8,8,128]{3,2,1,0:T(8,128)}, f32[5,8,8,128]{3,2,1,0:T(8,128)S(1)}, u32[]{:S(2)}, u32[]{:S(2)}) %collective-permute-start) | collective-permute-done | bytes 163872 | tf_op jit(solution)/shard_map/ppermute | solution.py:252
  8.0 0.9 %broadcast_select_fusion = f32[5,8,8,128]{3,2,1,0:T(8,128)S(1)} fusion(f32[5,8,8,128]{3,2,1,0:T(8,128)S(1)} %collective-permute-done, pred[]{:T(512)S(6)} %eq.3, f32[1,5,8,8,128]{4,3,2,1,0:T(8,128)} %param.4), kind=kLoop, calls=%fused_computation.1 | loop fusion | flops 40960 | bytes 491521 | tf_op jit(solution)/shard_map/jit(_where)/select_n | solution.py:253
  9.0 0.0 copy-start.1
  9.0 0.0 copy-start
  9.0 1.4 %collective-permute-start.1 = (f32[5,8,8,128]{3,2,1,0:T(8,128)S(1)}, f32[5,8,8,128]{3,2,1,0:T(8,128)S(1)}, u32[]{:S(2)}, u32[]{:S(2)}) collective-permute-start(f32[5,8,8,128]{3,2,1,0:T(8,128)S(1)} %broadcast_select_fusion), channel_id=1, source_target_pairs={{0,96},{256,352},{1,97},{257,353},{2,98},{258,354},{3,99},{259,355... | collective-permute-start | bytes 491528 | tf_op jit(solution)/shard_map/ppermute | solution.py:254
  10.4 1.3 %collective-permute-start.2 = (f32[5,8,8,128]{3,2,1,0:T(8,128)S(1)}, f32[5,8,8,128]{3,2,1,0:T(8,128)S(1)}, u32[]{:S(2)}, u32[]{:S(2)}) collective-permute-start(f32[5,8,8,128]{3,2,1,0:T(8,128)S(1)} %broadcast_select_fusion), channel_id=1, source_target_pairs={{0,160},{256,416},{1,161},{257,417},{2,162},{258,418},{3,163},{259... | collective-permute-start | bytes 491528 | tf_op jit(solution)/shard_map/ppermute | solution.py:255
  11.7 0.9 %collective-permute-done.1 = f32[5,8,8,128]{3,2,1,0:T(8,128)S(1)} collective-permute-done((f32[5,8,8,128]{3,2,1,0:T(8,128)S(1)}, f32[5,8,8,128]{3,2,1,0:T(8,128)S(1)}, u32[]{:S(2)}, u32[]{:S(2)}) %collective-permute-start.1) | collective-permute-done | bytes 163872 | tf_op jit(solution)/shard_map/ppermute | solution.py:254
  12.7 1.3 %collective-permute-done.2 = f32[5,8,8,128]{3,2,1,0:T(8,128)S(1)} collective-permute-done((f32[5,8,8,128]{3,2,1,0:T(8,128)S(1)}, f32[5,8,8,128]{3,2,1,0:T(8,128)S(1)}, u32[]{:S(2)}, u32[]{:S(2)}) %collective-permute-start.2) | collective-permute-done | bytes 163872 | tf_op jit(solution)/shard_map/ppermute | solution.py:255
  14.0 1.3 %collective-permute-start.3 = (f32[5,8,8,128]{3,2,1,0:T(8,128)S(1)}, f32[5,8,8,128]{3,2,1,0:T(8,128)S(1)}, u32[]{:S(2)}, u32[]{:S(2)}) collective-permute-start(f32[5,8,8,128]{3,2,1,0:T(8,128)S(1)} %add_add_fusion.y_ref), channel_id=1, source_target_pairs={{0,32},{96,128},{160,192},{256,288},{352,384},{416,448},{1,33},{97... | collective-permute-start | bytes 491528 | tf_op jit(solution)/shard_map/ppermute | solution.py:257
  15.3 1.3 %collective-permute-start.4 = (f32[5,8,8,128]{3,2,1,0:T(8,128)S(1)}, f32[5,8,8,128]{3,2,1,0:T(8,128)S(1)}, u32[]{:S(2)}, u32[]{:S(2)}) collective-permute-start(f32[5,8,8,128]{3,2,1,0:T(8,128)S(1)} %add_add_fusion.y_ref), channel_id=1, source_target_pairs={{0,224},{96,64},{256,480},{352,320},{1,225},{97,65},{257,481},{353... | collective-permute-start | bytes 491528 | tf_op jit(solution)/shard_map/ppermute | solution.py:258
  16.6 0.0 copy-done.1
  16.6 0.1 copy.7.off_ref
  17.4 1.2 %collective-permute-done.3.p_ref = f32[5,8,8,128]{3,2,1,0:T(8,128)S(1)} collective-permute-done((f32[5,8,8,128]{3,2,1,0:T(8,128)S(1)}, f32[5,8,8,128]{3,2,1,0:T(8,128)S(1)}, u32[]{:S(2)}, u32[]{:S(2)}) %collective-permute-start.3) | collective-permute-done | bytes 163872 | tf_op jit(solution)/shard_map/ppermute | solution.py:257
  18.5 1.3 %collective-permute-done.4.q_ref = f32[5,8,8,128]{3,2,1,0:T(8,128)S(1)} collective-permute-done((f32[5,8,8,128]{3,2,1,0:T(8,128)S(1)}, f32[5,8,8,128]{3,2,1,0:T(8,128)S(1)}, u32[]{:S(2)}, u32[]{:S(2)}) %collective-permute-start.4) | collective-permute-done | bytes 163872 | tf_op jit(solution)/shard_map/ppermute | solution.py:258
  19.8 0.0 copy-done
  19.8 0.9 %pack.1 = (f32[5,8,8,128]{3,2,1,0:T(8,128)S(1)}, f32[4,8,8,128]{3,2,1,0:T(8,128)S(1)}, f32[5,8,8,128]{3,2,1,0:T(8,128)S(1)}, f32[5,8,8,128]{3,2,1,0:T(8,128)S(1)}) custom-call(s32[1]{0:T(128)S(6)} %copy.8.sp_ref, s32[8,2]{1,0:T(8,128)S(1)} %copy.7.off_ref, f32[5,8,8,128]{3,2,1,0:T(8,128)S(1)} %bitcast.4, f32[5,8,8,128]{3,2,1,0:T(8,128)S(1)} %add_add_fusion.y_ref, ...), custom_call_target="tpu_custom_call" | custom-call | tf_op jit(solution)/shard_map/pack/pallas_call | solution.py:260
  20.7 7.0 %collective-permute-start.5 = (f32[5,8,8,128]{3,2,1,0:T(8,128)S(1)}, f32[5,8,8,128]{3,2,1,0:T(8,128)S(1)}, u32[]{:S(2)}, u32[]{:S(2)}) collective-permute-start(f32[5,8,8,128]{3,2,1,0:T(8,128)S(1)} %get-tuple-element.15), channel_id=1, source_target_pairs={{0,1},{1,0},{2,3},{3,2},{4,5},{5,4},{6,7},{7,6},{8,9},{9,8},{10,11... | collective-permute-start | bytes 491528 | tf_op jit(solution)/shard_map/ppermute | solution.py:272
  27.7 3.0 %collective-permute-start.6 = (f32[5,8,8,128]{3,2,1,0:T(8,128)S(1)}, f32[5,8,8,128]{3,2,1,0:T(8,128)S(1)}, u32[]{:S(2)}, u32[]{:S(2)}) collective-permute-start(f32[5,8,8,128]{3,2,1,0:T(8,128)S(1)} %get-tuple-element.16), channel_id=1, source_target_pairs={{0,31},{1,2},{2,1},{3,4},{4,3},{5,6},{6,5},{7,8},{8,7},{9,10},{10,... | collective-permute-start | bytes 491528 | tf_op jit(solution)/shard_map/ppermute | solution.py:269
  31.4 0.0 collective-permute-done.5.near_ref
  31.4 3.9 %collective-permute-done.6.far_ref = f32[5,8,8,128]{3,2,1,0:T(8,128)S(1)} collective-permute-done((f32[5,8,8,128]{3,2,1,0:T(8,128)S(1)}, f32[5,8,8,128]{3,2,1,0:T(8,128)S(1)}, u32[]{:S(2)}, u32[]{:S(2)}) %collective-permute-start.6) | collective-permute-done | bytes 163872 | tf_op jit(solution)/shard_map/ppermute | solution.py:269
  35.3 16.0 %steps.1 = (f32[5,8,8,128]{3,2,1,0:T(8,128)S(1)}, f32[5,8,128]{2,1,0:T(8,128)S(1)}, f32[5,8,128]{2,1,0:T(8,128)S(1)}, f32[4,8,8,128]{3,2,1,0:T(8,128)S(1)}, f32[32,1,128]{2,1,0:T(1,128)}) custom-call(s32[1]{0:T(128)S(6)} %copy.8.sp_ref, s32[1]{0:T(128)S(6)} %copy.9.st_ref, s32[8,2]{1,0:T(8,128)S(1)} %copy.7.off_ref, f32[5,8,8,128]{3,2,1,0:T(8,128)S(1)} %bitcast.5, ...), custom_call_target="tpu_custom_call" | custom-call | tf_op jit(solution)/shard_map/steps/pallas_call | solution.py:274
  51.3 12.5 %all-to-all-start = ((f32[32,1,128]{2,1,0:T(1,128)}), f32[32,1,128]{2,1,0:T(1,128)S(1)}, u32[]{:S(2)}, u32[]{:S(2)}) async-start(f32[32,1,128]{2,1,0:T(1,128)} %get-tuple-element.21), calls=%async_computation | async-start | bytes 32768 | tf_op jit(solution)/shard_map/all_to_all | solution.py:293
  63.8 4.4 %collective-permute-start.7 = (f32[5,8,128]{2,1,0:T(8,128)S(1)}, f32[5,8,128]{2,1,0:T(8,128)S(1)}, u32[]{:S(2)}, u32[]{:S(2)}) collective-permute-start(f32[5,8,128]{2,1,0:T(8,128)S(1)} %get-tuple-element.19), channel_id=1, source_target_pairs={{0,1},{1,2},{2,3},{3,4},{4,5},{5,6},{6,7},{7,8},{8,9},{9,10},{10,1... | collective-permute-start | bytes 61448 | tf_op jit(solution)/shard_map/ppermute | solution.py:292
  68.2 0.9 %collective-permute-done.7.edge_ref = f32[5,8,128]{2,1,0:T(8,128)S(1)} collective-permute-done((f32[5,8,128]{2,1,0:T(8,128)S(1)}, f32[5,8,128]{2,1,0:T(8,128)S(1)}, u32[]{:S(2)}, u32[]{:S(2)}) %collective-permute-start.7) | collective-permute-done | bytes 20512 | tf_op jit(solution)/shard_map/ppermute | solution.py:292
  69.1 3.9 %all-to-all-done.sums_ref = f32[32,1,128]{2,1,0:T(1,128)S(1)} async-done(((f32[32,1,128]{2,1,0:T(1,128)}), f32[32,1,128]{2,1,0:T(1,128)S(1)}, u32[]{:S(2)}, u32[]{:S(2)}) %all-to-all-start) | async-done | bytes 16416 | tf_op jit(solution)/shard_map/all_to_all | solution.py:293
  73.0 0.9 %last.1 = (f32[5,8,8,128]{3,2,1,0:T(8,128)}, f32[1]{0:T(128)}) custom-call(s32[1]{0:T(128)S(6)} %copy.9.st_ref, f32[5,8,8,128]{3,2,1,0:T(8,128)S(1)} %get-tuple-element.17.own_ref, f32[5,8,128]{2,1,0:T(8,128)S(1)} %get-tuple-element.18.beyond_ref, f32[5,8,128]{2,1,0:T(8,128)S(1)} %collective-permute-done.7.edge_ref, ...), custom_call_target="tpu_custom_call" | custom-call | tf_op jit(solution)/shard_map/last/pallas_call | solution.py:295
  (1 shorter events, 0.0 us)
Async XLA Ops:
  0.6 7.4 %collective-permute-start = (f32[5,8,8,128]{3,2,1,0:T(8,128)}, f32[5,8,8,128]{3,2,1,0:T(8,128)S(1)}, u32[]{:S(2)}, u32[]{:S(2)}) collective-permute-start(f32[5,8,8,128]{3,2,1,0:T(8,128)} %bitcast.3), channel_id=1, source_target_pairs={{0,256},{1,257},{2,258},{3,259},{4,260},{5,261},{6,262},{7,263},{8... | collective-permute-start | bytes 491528 | tf_op jit(solution)/shard_map/ppermute | solution.py:252
  9.0 7.7 %copy-start.1 = (s32[8,2]{0,1:T(2,128)S(1)}, s32[8,2]{0,1:T(2,128)}, u32[]{:S(2)}) copy-start(s32[8,2]{0,1:T(2,128)} %param.7) | copy-start | bytes 196
  9.0 10.8 %copy-start = (f32[1,5,8,8,128]{4,3,2,1,0:T(8,128)S(1)}, f32[1,5,8,8,128]{4,3,2,1,0:T(8,128)}, u32[]{:S(2)}) copy-start(f32[1,5,8,8,128]{4,3,2,1,0:T(8,128)} %param.4) | copy-start | bytes 491524
  9.0 3.7 %collective-permute-start.1 = (f32[5,8,8,128]{3,2,1,0:T(8,128)S(1)}, f32[5,8,8,128]{3,2,1,0:T(8,128)S(1)}, u32[]{:S(2)}, u32[]{:S(2)}) collective-permute-start(f32[5,8,8,128]{3,2,1,0:T(8,128)S(1)} %broadcast_select_fusion), channel_id=1, source_target_pairs={{0,96},{256,352},{1,97},{257,353},{2,98},{258,354},{3,99},{259,355... | collective-permute-start | bytes 491528 | tf_op jit(solution)/shard_map/ppermute | solution.py:254
  10.4 3.5 %collective-permute-start.2 = (f32[5,8,8,128]{3,2,1,0:T(8,128)S(1)}, f32[5,8,8,128]{3,2,1,0:T(8,128)S(1)}, u32[]{:S(2)}, u32[]{:S(2)}) collective-permute-start(f32[5,8,8,128]{3,2,1,0:T(8,128)S(1)} %broadcast_select_fusion), channel_id=1, source_target_pairs={{0,160},{256,416},{1,161},{257,417},{2,162},{258,418},{3,163},{259... | collective-permute-start | bytes 491528 | tf_op jit(solution)/shard_map/ppermute | solution.py:255
  14.0 4.5 %collective-permute-start.3 = (f32[5,8,8,128]{3,2,1,0:T(8,128)S(1)}, f32[5,8,8,128]{3,2,1,0:T(8,128)S(1)}, u32[]{:S(2)}, u32[]{:S(2)}) collective-permute-start(f32[5,8,8,128]{3,2,1,0:T(8,128)S(1)} %add_add_fusion.y_ref), channel_id=1, source_target_pairs={{0,32},{96,128},{160,192},{256,288},{352,384},{416,448},{1,33},{97... | collective-permute-start | bytes 491528 | tf_op jit(solution)/shard_map/ppermute | solution.py:257
  15.3 4.5 %collective-permute-start.4 = (f32[5,8,8,128]{3,2,1,0:T(8,128)S(1)}, f32[5,8,8,128]{3,2,1,0:T(8,128)S(1)}, u32[]{:S(2)}, u32[]{:S(2)}) collective-permute-start(f32[5,8,8,128]{3,2,1,0:T(8,128)S(1)} %add_add_fusion.y_ref), channel_id=1, source_target_pairs={{0,224},{96,64},{256,480},{352,320},{1,225},{97,65},{257,481},{353... | collective-permute-start | bytes 491528 | tf_op jit(solution)/shard_map/ppermute | solution.py:258
  20.7 10.6 %collective-permute-start.5 = (f32[5,8,8,128]{3,2,1,0:T(8,128)S(1)}, f32[5,8,8,128]{3,2,1,0:T(8,128)S(1)}, u32[]{:S(2)}, u32[]{:S(2)}) collective-permute-start(f32[5,8,8,128]{3,2,1,0:T(8,128)S(1)} %get-tuple-element.15), channel_id=1, source_target_pairs={{0,1},{1,0},{2,3},{3,2},{4,5},{5,4},{6,7},{7,6},{8,9},{9,8},{10,11... | collective-permute-start | bytes 491528 | tf_op jit(solution)/shard_map/ppermute | solution.py:272
  27.7 7.5 %collective-permute-start.6 = (f32[5,8,8,128]{3,2,1,0:T(8,128)S(1)}, f32[5,8,8,128]{3,2,1,0:T(8,128)S(1)}, u32[]{:S(2)}, u32[]{:S(2)}) collective-permute-start(f32[5,8,8,128]{3,2,1,0:T(8,128)S(1)} %get-tuple-element.16), channel_id=1, source_target_pairs={{0,31},{1,2},{2,1},{3,4},{4,3},{5,6},{6,5},{7,8},{8,7},{9,10},{10,... | collective-permute-start | bytes 491528 | tf_op jit(solution)/shard_map/ppermute | solution.py:269
  51.3 21.7 %all-to-all-start = ((f32[32,1,128]{2,1,0:T(1,128)}), f32[32,1,128]{2,1,0:T(1,128)S(1)}, u32[]{:S(2)}, u32[]{:S(2)}) async-start(f32[32,1,128]{2,1,0:T(1,128)} %get-tuple-element.21), calls=%async_computation | async-start | bytes 32768 | tf_op jit(solution)/shard_map/all_to_all | solution.py:293
  63.8 5.3 %collective-permute-start.7 = (f32[5,8,128]{2,1,0:T(8,128)S(1)}, f32[5,8,128]{2,1,0:T(8,128)S(1)}, u32[]{:S(2)}, u32[]{:S(2)}) collective-permute-start(f32[5,8,128]{2,1,0:T(8,128)S(1)} %get-tuple-element.19), channel_id=1, source_target_pairs={{0,1},{1,2},{2,3},{3,4},{4,5},{5,6},{6,7},{7,8},{8,9},{9,10},{10,1... | collective-permute-start | bytes 61448 | tf_op jit(solution)/shard_map/ppermute | solution.py:292

commit v2 on v1

--- a/solution.py
+++ b/solution.py
@@ -18,6 +18,7 @@
 COLD = 0.8
 
 ROWS = (8, 128)
+UNROLL = 2
 
 
 def rolled(v, shift, axis):
@@ -151,26 +152,44 @@
             far_ref[c, z] = jnp.where(to_near, other, own)
 
 
+def set_ghosts(ref):
+    for c in range(5):
+        for t in (0, 1):
+            low, high = ref[c, 1, t], ref[c, PLANES, t]
+            if c == 3:
+                low, high = -low, -high
+            elif c == 4:
+                low, high = 2.0 * HOT - low, 2.0 * COLD - high
+            ref[c, 0, t] = low
+            ref[c, PLANES + 1, t] = high
+
+
 def steps_kernel(
     sp_ref, st_ref, off_ref, own_ref, nat_ref, d_ref, near_ref, far_ref,
-    own2_ref, beyond_ref, edge_ref, d2_ref, sum_ref, a_ref, b_ref, a1_ref, b1_ref, n2_ref,
+    own2_ref, beyond_ref, edge_ref, d2_ref, sum_ref, a_ref, b_ref, a1_ref, b1_ref, far2_ref, total_ref,
 ):
     spread = Spread(sp_ref, off_ref)
     sub = sub_ids()
     even = lax.rem(lax.axis_index("tile"), 2) == 0
     from_near = (sub < 4) == even
     mu = nudge_factor(st_ref)
-    for c in range(5):
-        for z in range(PLANES):
+    for z in range(PLANES):
+        for c in range(5):
             near, far = near_ref[c, z], far_ref[c, z]
-            a_ref[c, z] = jnp.where(from_near, near, far)
-            b_ref[c, z] = rolled(jnp.where(from_near, far, near), 4, 0)
-    a = ghosted(lambda c, z, t: a_ref[c, z] if t else own_ref[c, z])
-    b = ghosted(lambda c, z, t: b_ref[c, z] if t else nat_ref[c, z])
-    for z in range(PLANES):
+            a_ref[c, z + 1, 0] = own_ref[c, z]
+            b_ref[c, z + 1, 0] = nat_ref[c, z]
+            a_ref[c, z + 1, 1] = jnp.where(from_near, near, far)
+            b_ref[c, z + 1, 1] = rolled(jnp.where(from_near, far, near), 4, 0)
+    set_ghosts(a_ref)
+    set_ghosts(b_ref)
+
+    def getter(ref):
+        return lambda c, z, t: ref[c, z + 1, t]
+
+    def first(z):
         keep = spread.plane(z)
-        new_a = stepped(a, z, (0, 1), sub)
-        new_b = stepped(b, z, (0, 1), sub)
+        new_a = stepped(getter(a_ref), z, (0, 1), sub)
+        new_b = stepped(getter(b_ref), z, (0, 1), sub)
         for t in (0, 1):
             for c in range(5):
                 value = new_a[t][c]
@@ -178,35 +197,51 @@
                     if t == 0:
                         d = d_ref[c - 1, z]
                     else:
-                        halo = a_ref[c, z]
-                        d = spread(halo - b_ref[c, z], keep)
+                        halo = a_ref[c, z + 1, 1]
+                        d = spread(halo - b_ref[c, z + 1, 1], keep)
                         d = jnp.where(sub == 7, rolled(halo, 2, 0), d)
                     value = value - mu * d
-                a1_ref[t, c, z] = value
-                b1_ref[t, c, z] = new_b[t][c]
-    a = ghosted(lambda c, z, t: a1_ref[t, c, z])
-    b = ghosted(lambda c, z, t: b1_ref[t, c, z])
-    total = jnp.zeros(ROWS, jnp.float32)
-    for z in range(PLANES):
+                a1_ref[c, z + 1, t] = value
+                b1_ref[c, z + 1, t] = new_b[t][c]
+
+    def second(z):
         keep = spread.plane(z)
-        new_a = stepped(a, z, (0, 1), sub)
-        new_b = stepped(b, z, (0,), sub)[0]
+        new_a = stepped(getter(a1_ref), z, (0, 1), sub)
+        new_b = stepped(getter(b1_ref), z, (0,), sub)[0]
         for c in range(5):
             for t in (0, 1):
                 value = new_a[t][c]
                 if c > 0:
-                    value = value - mu * spread(a1_ref[t, c, z] - b1_ref[t, c, z], keep)
+                    value = value - mu * spread(a1_ref[c, z + 1, t] - b1_ref[c, z + 1, t], keep)
                 if t == 0:
                     own2_ref[c, z] = value
-                    edge_ref[c, z : z + 1] = value[7:8]
                     if c > 0:
                         d = spread(value - new_b[c], keep)
                         d2_ref[c - 1, z] = d
                         if c == 4:
-                            total = total + d * d
+                            total_ref[...] += d * d
                 else:
-                    beyond_ref[c, z : z + 1] = value[0:1]
-    sum_ref[...] = jnp.broadcast_to(jnp.sum(total, axis=0)[None, None], sum_ref.shape)
+                    far2_ref[c, z] = value
+
+    def planes(body):
+        def several(i, carry):
+            for k in range(UNROLL):
+                body(i * UNROLL + k)
+            return carry
+
+        lax.fori_loop(0, PLANES // UNROLL, several, 0)
+
+    total_ref[...] = jnp.zeros(ROWS, jnp.float32)
+    planes(first)
+    set_ghosts(a1_ref)
+    set_ghosts(b1_ref)
+    planes(second)
+    for c in range(5):
+        for z in range(PLANES):
+            edge_ref[c, z : z + 1] = own2_ref[c, z, 7:8]
+            beyond_ref[c, z : z + 1] = far2_ref[c, z, 0:1]
+    total = jnp.sum(total_ref[...], axis=0)
+    sum_ref[...] = jnp.broadcast_to(total[None, None], sum_ref.shape)
 
 
 def last_kernel(st_ref, own_ref, beyond_ref, edge_ref, d_ref, sums_ref, out_ref, misfit_ref, h_ref):
@@ -239,6 +274,7 @@
 PARAMS = pltpu.CompilerParams(vmem_limit_bytes=12 * 2**20)
 BLOCK = (5, PLANES, 8, 128)
 BLOCK4 = (4, PLANES, 8, 128)
+EXTENDED = (5, PLANES + 2, 2, 8, 128)
 
 
 def twice(pairs):
@@ -279,11 +315,9 @@
         in_specs=[SM, SM, SM] + [VM] * 5,
         out_specs=(VM,) * 5,
         scratch_shapes=[
+            *[pltpu.VMEM(EXTENDED, jnp.float32)] * 4,
             pltpu.VMEM(BLOCK, jnp.float32),
-            pltpu.VMEM(BLOCK, jnp.float32),
-            pltpu.VMEM((2,) + BLOCK, jnp.float32),
-            pltpu.VMEM((2,) + BLOCK, jnp.float32),
-            pltpu.VMEM(BLOCK, jnp.float32),
+            pltpu.VMEM(ROWS, jnp.float32),
         ],
         compiler_params=PARAMS,
         name="steps",

time: 74.9 us -> 62.9 us (0.84)
  Pallas kernels: 17.8 us -> 5.85 us
    pallas_call x1, Pallas kernels: 16 us -> 4.07 us  [shards(): pl.pallas_call(steps_kernel, out_shape=(f32(*BLOCK), f32(5, PLANES, 128),...]
where the time goes in v2:
time: 62.9 us; the launch traced here: 62 us
  starting transfers between devices  37 us (59%)
  waiting for transfers between devices  16 us (25%)
  Pallas kernels  5.85 us (9%)
  between operations  2.05 us (3%)
  other arithmetic  0.96 us (2%)
    all_to_all x1, starting transfers between devices, shards(): sums = lax.all_to_all(sums, 'tile', 0, 0)  12.5 us
    ppermute x1, starting transfers between devices, shards(): near = lax.ppermute(near, 'tile', [(i, i ^ 1) for i in range(TILES)])  6.99 us
    ppermute x1, starting transfers between devices, shards(): p = lax.ppermute(own, 'run', [(0, 8)])  4.84 us
    ppermute x1, starting transfers between devices, shards(): lax.ppermute(edge, 'tile', [(i, (i + 1) % TILES) for i in range(TILES)])  4.44 us
    pallas_call x1, Pallas kernels, shards(): pl.pallas_call(steps_kernel, out_shape=(f32(*BLOCK), f32(5, PLANES, 128),...  4.07 us
    all_to_all x1, waiting for transfers between devices, shards(): sums = lax.all_to_all(sums, 'tile', 0, 0)  3.94 us
    ppermute x1, waiting for transfers between devices, shards(): lax.ppermute(far, 'tile', [(i, (i + 1) % TILES if i % 2 else (i - 1) % TI...  3.9 us
    ppermute x1, starting transfers between devices, shards(): lax.ppermute(far, 'tile', [(i, (i + 1) % TILES if i % 2 else (i - 1) % TI...  2.97 us
  transfers between devices with their start and end apart: 9, of which 8 were waited for; matrix products, arithmetic and copies ran while one was open for 0% of the time, Pallas kernels for 0%

profile of v2, /device:TPU:1, one launch (start us, length us, event | category | flops | bytes accessed | tf_op | source)
XLA Modules:
  0.0 62.0 jit_solution(4098543826232373033)
XLA Ops:
  0.6 4.8 %collective-permute-start = (f32[5,8,8,128]{3,2,1,0:T(8,128)}, f32[5,8,8,128]{3,2,1,0:T(8,128)S(1)}, u32[]{:S(2)}, u32[]{:S(2)}) collective-permute-start(f32[5,8,8,128]{3,2,1,0:T(8,128)} %bitcast.3), channel_id=1, source_target_pairs={{0,256},{1,257},{2,258},{3,259},{4,260},{5,261},{6,262},{7,263},{8... | collective-permute-start | bytes 491528 | tf_op jit(solution)/shard_map/ppermute | solution.py:288
  5.5 2.5 %collective-permute-done = f32[5,8,8,128]{3,2,1,0:T(8,128)S(1)} collective-permute-done((f32[5,8,8,128]{3,2,1,0:T(8,128)}, f32[5,8,8,128]{3,2,1,0:T(8,128)S(1)}, u32[]{:S(2)}, u32[]{:S(2)}) %collective-permute-start) | collective-permute-done | bytes 163872 | tf_op jit(solution)/shard_map/ppermute | solution.py:288
  8.0 0.9 %broadcast_select_fusion = f32[5,8,8,128]{3,2,1,0:T(8,128)S(1)} fusion(f32[5,8,8,128]{3,2,1,0:T(8,128)S(1)} %collective-permute-done, pred[]{:T(512)S(6)} %eq.3, f32[1,5,8,8,128]{4,3,2,1,0:T(8,128)} %param.4), kind=kLoop, calls=%fused_computation.1 | loop fusion | flops 40960 | bytes 491521 | tf_op jit(solution)/shard_map/jit(_where)/select_n | solution.py:289
  9.0 0.0 copy-start.1
  9.0 0.0 copy-start
  9.0 1.4 %collective-permute-start.1 = (f32[5,8,8,128]{3,2,1,0:T(8,128)S(1)}, f32[5,8,8,128]{3,2,1,0:T(8,128)S(1)}, u32[]{:S(2)}, u32[]{:S(2)}) collective-permute-start(f32[5,8,8,128]{3,2,1,0:T(8,128)S(1)} %broadcast_select_fusion), channel_id=1, source_target_pairs={{0,96},{256,352},{1,97},{257,353},{2,98},{258,354},{3,99},{259,355... | collective-permute-start | bytes 491528 | tf_op jit(solution)/shard_map/ppermute | solution.py:290
  10.4 1.3 %collective-permute-start.2 = (f32[5,8,8,128]{3,2,1,0:T(8,128)S(1)}, f32[5,8,8,128]{3,2,1,0:T(8,128)S(1)}, u32[]{:S(2)}, u32[]{:S(2)}) collective-permute-start(f32[5,8,8,128]{3,2,1,0:T(8,128)S(1)} %broadcast_select_fusion), channel_id=1, source_target_pairs={{0,160},{256,416},{1,161},{257,417},{2,162},{258,418},{3,163},{259... | collective-permute-start | bytes 491528 | tf_op jit(solution)/shard_map/ppermute | solution.py:291
  11.7 0.9 %collective-permute-done.1 = f32[5,8,8,128]{3,2,1,0:T(8,128)S(1)} collective-permute-done((f32[5,8,8,128]{3,2,1,0:T(8,128)S(1)}, f32[5,8,8,128]{3,2,1,0:T(8,128)S(1)}, u32[]{:S(2)}, u32[]{:S(2)}) %collective-permute-start.1) | collective-permute-done | bytes 163872 | tf_op jit(solution)/shard_map/ppermute | solution.py:290
  12.7 1.3 %collective-permute-done.2 = f32[5,8,8,128]{3,2,1,0:T(8,128)S(1)} collective-permute-done((f32[5,8,8,128]{3,2,1,0:T(8,128)S(1)}, f32[5,8,8,128]{3,2,1,0:T(8,128)S(1)}, u32[]{:S(2)}, u32[]{:S(2)}) %collective-permute-start.2) | collective-permute-done | bytes 163872 | tf_op jit(solution)/shard_map/ppermute | solution.py:291
  14.0 1.3 %collective-permute-start.3 = (f32[5,8,8,128]{3,2,1,0:T(8,128)S(1)}, f32[5,8,8,128]{3,2,1,0:T(8,128)S(1)}, u32[]{:S(2)}, u32[]{:S(2)}) collective-permute-start(f32[5,8,8,128]{3,2,1,0:T(8,128)S(1)} %add_add_fusion.y_ref), channel_id=1, source_target_pairs={{0,32},{96,128},{160,192},{256,288},{352,384},{416,448},{1,33},{97... | collective-permute-start | bytes 491528 | tf_op jit(solution)/shard_map/ppermute | solution.py:293
  15.3 1.3 %collective-permute-start.4 = (f32[5,8,8,128]{3,2,1,0:T(8,128)S(1)}, f32[5,8,8,128]{3,2,1,0:T(8,128)S(1)}, u32[]{:S(2)}, u32[]{:S(2)}) collective-permute-start(f32[5,8,8,128]{3,2,1,0:T(8,128)S(1)} %add_add_fusion.y_ref), channel_id=1, source_target_pairs={{0,224},{96,64},{256,480},{352,320},{1,225},{97,65},{257,481},{353... | collective-permute-start | bytes 491528 | tf_op jit(solution)/shard_map/ppermute | solution.py:294
  16.6 0.0 copy-done.1
  16.6 0.1 copy.7.off_ref
  17.4 1.2 %collective-permute-done.3.p_ref = f32[5,8,8,128]{3,2,1,0:T(8,128)S(1)} collective-permute-done((f32[5,8,8,128]{3,2,1,0:T(8,128)S(1)}, f32[5,8,8,128]{3,2,1,0:T(8,128)S(1)}, u32[]{:S(2)}, u32[]{:S(2)}) %collective-permute-start.3) | collective-permute-done | bytes 163872 | tf_op jit(solution)/shard_map/ppermute | solution.py:293
  18.5 1.3 %collective-permute-done.4.q_ref = f32[5,8,8,128]{3,2,1,0:T(8,128)S(1)} collective-permute-done((f32[5,8,8,128]{3,2,1,0:T(8,128)S(1)}, f32[5,8,8,128]{3,2,1,0:T(8,128)S(1)}, u32[]{:S(2)}, u32[]{:S(2)}) %collective-permute-start.4) | collective-permute-done | bytes 163872 | tf_op jit(solution)/shard_map/ppermute | solution.py:294
  19.8 0.0 copy-done
  19.8 0.9 %pack.1 = (f32[5,8,8,128]{3,2,1,0:T(8,128)S(1)}, f32[4,8,8,128]{3,2,1,0:T(8,128)S(1)}, f32[5,8,8,128]{3,2,1,0:T(8,128)S(1)}, f32[5,8,8,128]{3,2,1,0:T(8,128)S(1)}) custom-call(s32[1]{0:T(128)S(6)} %copy.8.sp_ref, s32[8,2]{1,0:T(8,128)S(1)} %copy.7.off_ref, f32[5,8,8,128]{3,2,1,0:T(8,128)S(1)} %bitcast.4, f32[5,8,8,128]{3,2,1,0:T(8,128)S(1)} %add_add_fusion.y_ref, ...), custom_call_target="tpu_custom_call" | custom-call | tf_op jit(solution)/shard_map/pack/pallas_call | solution.py:296
  20.7 7.0 %collective-permute-start.5 = (f32[5,8,8,128]{3,2,1,0:T(8,128)S(1)}, f32[5,8,8,128]{3,2,1,0:T(8,128)S(1)}, u32[]{:S(2)}, u32[]{:S(2)}) collective-permute-start(f32[5,8,8,128]{3,2,1,0:T(8,128)S(1)} %get-tuple-element.15), channel_id=1, source_target_pairs={{0,1},{1,0},{2,3},{3,2},{4,5},{5,4},{6,7},{7,6},{8,9},{9,8},{10,11... | collective-permute-start | bytes 491528 | tf_op jit(solution)/shard_map/ppermute | solution.py:308
  27.7 3.0 %collective-permute-start.6 = (f32[5,8,8,128]{3,2,1,0:T(8,128)S(1)}, f32[5,8,8,128]{3,2,1,0:T(8,128)S(1)}, u32[]{:S(2)}, u32[]{:S(2)}) collective-permute-start(f32[5,8,8,128]{3,2,1,0:T(8,128)S(1)} %get-tuple-element.16), channel_id=1, source_target_pairs={{0,31},{1,2},{2,1},{3,4},{4,3},{5,6},{6,5},{7,8},{8,7},{9,10},{10,... | collective-permute-start | bytes 491528 | tf_op jit(solution)/shard_map/ppermute | solution.py:305
  31.4 0.0 collective-permute-done.5.near_ref
  31.4 3.9 %collective-permute-done.6.far_ref = f32[5,8,8,128]{3,2,1,0:T(8,128)S(1)} collective-permute-done((f32[5,8,8,128]{3,2,1,0:T(8,128)S(1)}, f32[5,8,8,128]{3,2,1,0:T(8,128)S(1)}, u32[]{:S(2)}, u32[]{:S(2)}) %collective-permute-start.6) | collective-permute-done | bytes 163872 | tf_op jit(solution)/shard_map/ppermute | solution.py:305
  35.3 4.1 %steps.1 = (f32[5,8,8,128]{3,2,1,0:T(8,128)S(1)}, f32[5,8,128]{2,1,0:T(8,128)S(1)}, f32[5,8,128]{2,1,0:T(8,128)S(1)}, f32[4,8,8,128]{3,2,1,0:T(8,128)S(1)}, f32[32,1,128]{2,1,0:T(1,128)}) custom-call(s32[1]{0:T(128)S(6)} %copy.8.sp_ref, s32[1]{0:T(128)S(6)} %copy.9.st_ref, s32[8,2]{1,0:T(8,128)S(1)} %copy.7.off_ref, f32[5,8,8,128]{3,2,1,0:T(8,128)S(1)} %bitcast.5, ...), custom_call_target="tpu_custom_call" | custom-call | tf_op jit(solution)/shard_map/steps/pallas_call | solution.py:310
  39.3 12.5 %all-to-all-start = ((f32[32,1,128]{2,1,0:T(1,128)}), f32[32,1,128]{2,1,0:T(1,128)S(1)}, u32[]{:S(2)}, u32[]{:S(2)}) async-start(f32[32,1,128]{2,1,0:T(1,128)} %get-tuple-element.21), calls=%async_computation | async-start | bytes 32768 | tf_op jit(solution)/shard_map/all_to_all | solution.py:327
  51.8 4.4 %collective-permute-start.7 = (f32[5,8,128]{2,1,0:T(8,128)S(1)}, f32[5,8,128]{2,1,0:T(8,128)S(1)}, u32[]{:S(2)}, u32[]{:S(2)}) collective-permute-start(f32[5,8,128]{2,1,0:T(8,128)S(1)} %get-tuple-element.19), channel_id=1, source_target_pairs={{0,1},{1,2},{2,3},{3,4},{4,5},{5,6},{6,7},{7,8},{8,9},{9,10},{10,1... | collective-permute-start | bytes 61448 | tf_op jit(solution)/shard_map/ppermute | solution.py:326
  56.2 0.9 %collective-permute-done.7.edge_ref = f32[5,8,128]{2,1,0:T(8,128)S(1)} collective-permute-done((f32[5,8,128]{2,1,0:T(8,128)S(1)}, f32[5,8,128]{2,1,0:T(8,128)S(1)}, u32[]{:S(2)}, u32[]{:S(2)}) %collective-permute-start.7) | collective-permute-done | bytes 20512 | tf_op jit(solution)/shard_map/ppermute | solution.py:326
  57.1 3.9 %all-to-all-done.sums_ref = f32[32,1,128]{2,1,0:T(1,128)S(1)} async-done(((f32[32,1,128]{2,1,0:T(1,128)}), f32[32,1,128]{2,1,0:T(1,128)S(1)}, u32[]{:S(2)}, u32[]{:S(2)}) %all-to-all-start) | async-done | bytes 16416 | tf_op jit(solution)/shard_map/all_to_all | solution.py:327
  61.1 0.9 %last.1 = (f32[5,8,8,128]{3,2,1,0:T(8,128)}, f32[1]{0:T(128)}) custom-call(s32[1]{0:T(128)S(6)} %copy.9.st_ref, f32[5,8,8,128]{3,2,1,0:T(8,128)S(1)} %get-tuple-element.17.own_ref, f32[5,8,128]{2,1,0:T(8,128)S(1)} %get-tuple-element.18.beyond_ref, f32[5,8,128]{2,1,0:T(8,128)S(1)} %collective-permute-done.7.edge_ref, ...), custom_call_target="tpu_custom_call" | custom-call | tf_op jit(solution)/shard_map/last/pallas_call | solution.py:329
  (1 shorter events, 0.0 us)
Async XLA Ops:
  0.6 7.4 %collective-permute-start = (f32[5,8,8,128]{3,2,1,0:T(8,128)}, f32[5,8,8,128]{3,2,1,0:T(8,128)S(1)}, u32[]{:S(2)}, u32[]{:S(2)}) collective-permute-start(f32[5,8,8,128]{3,2,1,0:T(8,128)} %bitcast.3), channel_id=1, source_target_pairs={{0,256},{1,257},{2,258},{3,259},{4,260},{5,261},{6,262},{7,263},{8... | collective-permute-start | bytes 491528 | tf_op jit(solution)/shard_map/ppermute | solution.py:288
  9.0 7.7 %copy-start.1 = (s32[8,2]{0,1:T(2,128)S(1)}, s32[8,2]{0,1:T(2,128)}, u32[]{:S(2)}) copy-start(s32[8,2]{0,1:T(2,128)} %param.7) | copy-start | bytes 196
  9.0 10.8 %copy-start = (f32[1,5,8,8,128]{4,3,2,1,0:T(8,128)S(1)}, f32[1,5,8,8,128]{4,3,2,1,0:T(8,128)}, u32[]{:S(2)}) copy-start(f32[1,5,8,8,128]{4,3,2,1,0:T(8,128)} %param.4) | copy-start | bytes 491524
  9.0 3.7 %collective-permute-start.1 = (f32[5,8,8,128]{3,2,1,0:T(8,128)S(1)}, f32[5,8,8,128]{3,2,1,0:T(8,128)S(1)}, u32[]{:S(2)}, u32[]{:S(2)}) collective-permute-start(f32[5,8,8,128]{3,2,1,0:T(8,128)S(1)} %broadcast_select_fusion), channel_id=1, source_target_pairs={{0,96},{256,352},{1,97},{257,353},{2,98},{258,354},{3,99},{259,355... | collective-permute-start | bytes 491528 | tf_op jit(solution)/shard_map/ppermute | solution.py:290
  10.4 3.5 %collective-permute-start.2 = (f32[5,8,8,128]{3,2,1,0:T(8,128)S(1)}, f32[5,8,8,128]{3,2,1,0:T(8,128)S(1)}, u32[]{:S(2)}, u32[]{:S(2)}) collective-permute-start(f32[5,8,8,128]{3,2,1,0:T(8,128)S(1)} %broadcast_select_fusion), channel_id=1, source_target_pairs={{0,160},{256,416},{1,161},{257,417},{2,162},{258,418},{3,163},{259... | collective-permute-start | bytes 491528 | tf_op jit(solution)/shard_map/ppermute | solution.py:291
  14.0 4.5 %collective-permute-start.3 = (f32[5,8,8,128]{3,2,1,0:T(8,128)S(1)}, f32[5,8,8,128]{3,2,1,0:T(8,128)S(1)}, u32[]{:S(2)}, u32[]{:S(2)}) collective-permute-start(f32[5,8,8,128]{3,2,1,0:T(8,128)S(1)} %add_add_fusion.y_ref), channel_id=1, source_target_pairs={{0,32},{96,128},{160,192},{256,288},{352,384},{416,448},{1,33},{97... | collective-permute-start | bytes 491528 | tf_op jit(solution)/shard_map/ppermute | solution.py:293
  15.3 4.5 %collective-permute-start.4 = (f32[5,8,8,128]{3,2,1,0:T(8,128)S(1)}, f32[5,8,8,128]{3,2,1,0:T(8,128)S(1)}, u32[]{:S(2)}, u32[]{:S(2)}) collective-permute-start(f32[5,8,8,128]{3,2,1,0:T(8,128)S(1)} %add_add_fusion.y_ref), channel_id=1, source_target_pairs={{0,224},{96,64},{256,480},{352,320},{1,225},{97,65},{257,481},{353... | collective-permute-start | bytes 491528 | tf_op jit(solution)/shard_map/ppermute | solution.py:294
  20.7 10.6 %collective-permute-start.5 = (f32[5,8,8,128]{3,2,1,0:T(8,128)S(1)}, f32[5,8,8,128]{3,2,1,0:T(8,128)S(1)}, u32[]{:S(2)}, u32[]{:S(2)}) collective-permute-start(f32[5,8,8,128]{3,2,1,0:T(8,128)S(1)} %get-tuple-element.15), channel_id=1, source_target_pairs={{0,1},{1,0},{2,3},{3,2},{4,5},{5,4},{6,7},{7,6},{8,9},{9,8},{10,11... | collective-permute-start | bytes 491528 | tf_op jit(solution)/shard_map/ppermute | solution.py:308
  27.7 7.5 %collective-permute-start.6 = (f32[5,8,8,128]{3,2,1,0:T(8,128)S(1)}, f32[5,8,8,128]{3,2,1,0:T(8,128)S(1)}, u32[]{:S(2)}, u32[]{:S(2)}) collective-permute-start(f32[5,8,8,128]{3,2,1,0:T(8,128)S(1)} %get-tuple-element.16), channel_id=1, source_target_pairs={{0,31},{1,2},{2,1},{3,4},{4,3},{5,6},{6,5},{7,8},{8,7},{9,10},{10,... | collective-permute-start | bytes 491528 | tf_op jit(solution)/shard_map/ppermute | solution.py:305
  39.3 21.7 %all-to-all-start = ((f32[32,1,128]{2,1,0:T(1,128)}), f32[32,1,128]{2,1,0:T(1,128)S(1)}, u32[]{:S(2)}, u32[]{:S(2)}) async-start(f32[32,1,128]{2,1,0:T(1,128)} %get-tuple-element.21), calls=%async_computation | async-start | bytes 32768 | tf_op jit(solution)/shard_map/all_to_all | solution.py:327
  51.8 5.3 %collective-permute-start.7 = (f32[5,8,128]{2,1,0:T(8,128)S(1)}, f32[5,8,128]{2,1,0:T(8,128)S(1)}, u32[]{:S(2)}, u32[]{:S(2)}) collective-permute-start(f32[5,8,128]{2,1,0:T(8,128)S(1)} %get-tuple-element.19), channel_id=1, source_target_pairs={{0,1},{1,2},{2,3},{3,4},{4,5},{5,6},{6,7},{7,8},{8,9},{9,10},{10,1... | collective-permute-start | bytes 61448 | tf_op jit(solution)/shard_map/ppermute | solution.py:326

commit v3 on v2

v3 whole, which is shorter than its diff:
```python
import jax
import jax.numpy as jnp
from jax import lax
from jax.experimental import pallas as pl
from jax.experimental.pallas import tpu as pltpu
from jax.sharding import PartitionSpec as P

RUNS = 16
TILES = 32
PLANES = 8
CELLS = 8 * 256 * 128

DT = 0.05
VISC = 0.05
GAMMA1 = 0.4
GRAVITY = 0.5
HOT = 1.2
COLD = 0.8

ROWS = (8, 128)
UNROLL = 2


def rolled(v, shift, axis):
    return pltpu.roll(v, shift % v.shape[axis], axis)


def sub_ids():
    return lax.broadcasted_iota(jnp.int32, ROWS, 0)


def lane_ids():
    return lax.broadcasted_iota(jnp.int32, ROWS, 1)


class Spread:
    def __init__(self, sp_ref, off_ref):
        k = sp_ref[0]
        self.off = off_ref
        self.base = [lax.shift_left(lax.shift_right_logical(ids, k), k) for ids in (sub_ids(), lane_ids())]

    def plane(self, z):
        return self.base[0] + self.off[z, 0], self.base[1] + self.off[z, 1]

    def __call__(self, e, index):
        for axis in (0, 1):
            e = jnp.take_along_axis(e, index[axis], axis=axis, mode="promise_in_bounds")
        return e


def put(ref, c, z, t, value):
    ref[c, z + 1, 8 + 8 * t : 16 + 8 * t] = value
    if t == 0:
        ref[c, z + 1, 24:25] = value[0:1]
    else:
        ref[c, z + 1, 7:8] = value[7:8]


def get(ref, c, z, t, shift=0):
    first = 8 + 8 * t + shift
    return ref[c, z + 1, first : first + 8]


def set_ghosts(ref, tiles=(0, 1)):
    for c in range(5):
        for t in tiles:
            low, high = get(ref, c, 0, t), get(ref, c, PLANES - 1, t)
            if c == 3:
                low, high = -low, -high
            elif c == 4:
                low, high = 2.0 * HOT - low, 2.0 * COLD - high
            ref[c, 0, 8 + 8 * t : 16 + 8 * t] = low
            ref[c, PLANES + 1, 8 + 8 * t : 16 + 8 * t] = high


def stepped(ref, z, t):
    c0, xn, xp, zn, zp = (
        [get(ref, c, z + dz, t, dx) for c in range(5)]
        for dz, dx in ((0, 0), (0, 1), (0, -1), (1, 0), (-1, 0))
    )
    yn = [rolled(v, -1, 1) for v in c0]
    yp = [rolled(v, 1, 1) for v in c0]
    flux = (
        (xn[0] * xn[1] - xp[0] * xp[1])
        + (yn[0] * yn[2] - yp[0] * yp[2])
        + (zn[0] * zn[3] - zp[0] * zp[3])
    )
    scale = (0.5 * DT) / c0[0]
    grad = (
        xn[0] * xn[4] - xp[0] * xp[4],
        yn[0] * yn[4] - yp[0] * yp[4],
        zn[0] * zn[4] - zp[0] * zp[4],
    )
    new = [c0[0] - (0.5 * DT) * flux]
    div = None
    for q in range(1, 5):
        dx, dy, dz = xn[q] - xp[q], yn[q] - yp[q], zn[q] - zp[q]
        part = (None, dx, dy, dz, None)[q]
        if part is not None:
            div = part if div is None else div + part
        adv = c0[1] * dx + c0[2] * dy + c0[3] * dz
        six = ((xn[q] + xp[q]) + (yn[q] + yp[q])) + (zn[q] + zp[q])
        change = (DT * VISC) * (six - 6.0 * c0[q]) - (0.5 * DT) * adv
        if q < 4:
            change = change - grad[q - 1] * scale
            if q == 3:
                change = change - DT * GRAVITY
        else:
            change = change - (0.5 * DT * GAMMA1) * (c0[4] * div)
        new.append(c0[q] + change)
    return new


def nudge_factor(st_ref):
    strength = 0.5 * lax.shift_left(jnp.int32(1), st_ref[0]).astype(jnp.float32)
    return jnp.where(lax.axis_index("run") == 0, 0.0, DT * strength)


def pack_kernel(sp_ref, off_ref, own_ref, y_ref, p_ref, q_ref, nat_ref, d_ref, near_ref, far_ref):
    spread = Spread(sp_ref, off_ref)
    sub = sub_ids()
    even = lax.rem(lax.axis_index("tile"), 2) == 0
    to_near = (sub >= 4) == even
    for z in range(PLANES):
        keep = spread.plane(z)
        for c in range(5):
            own = own_ref[c, z]
            nat = y_ref[c, z] + p_ref[c, z] + q_ref[c, z]
            nat_ref[c, z] = nat
            if c > 0:
                d = spread(own - nat, keep)
                d_ref[c - 1, z] = d
                own = jnp.where(sub == 5, rolled(d, -2, 0), own)
            other = rolled(nat, 4, 0)
            near_ref[c, z] = jnp.where(to_near, own, other)
            far_ref[c, z] = jnp.where(to_near, other, own)


def steps_kernel(
    sp_ref, st_ref, off_ref, own_ref, nat_ref, d_ref, far_ref, near_ref,
    own2_ref, beyond_ref, edge_ref, d2_ref, sum_ref, a_ref, b_ref, a1_ref, b1_ref, far2_ref, total_ref,
):
    spread = Spread(sp_ref, off_ref)
    sub = sub_ids()
    even = lax.rem(lax.axis_index("tile"), 2) == 0
    from_near = (sub < 4) == even
    mu = nudge_factor(st_ref)
    for z in range(PLANES):
        for c in range(5):
            near, far = near_ref[c, z], far_ref[c, z]
            put(a_ref, c, z, 0, own_ref[c, z])
            put(b_ref, c, z, 0, nat_ref[c, z])
            put(a_ref, c, z, 1, jnp.where(from_near, near, far))
            put(b_ref, c, z, 1, rolled(jnp.where(from_near, far, near), 4, 0))
    set_ghosts(a_ref)
    set_ghosts(b_ref)

    def first(z):
        index = spread.plane(z)
        for t in (0, 1):
            new_a = stepped(a_ref, z, t)
            new_b = stepped(b_ref, z, t)
            for c in range(5):
                value = new_a[c]
                if c > 0:
                    if t == 0:
                        d = d_ref[c - 1, z]
                    else:
                        halo = get(a_ref, c, z, 1)
                        d = spread(halo - get(b_ref, c, z, 1), index)
                        d = jnp.where(sub == 7, rolled(halo, 2, 0), d)
                    value = value - mu * d
                put(a1_ref, c, z, t, value)
                put(b1_ref, c, z, t, new_b[c])

    def second(z):
        index = spread.plane(z)
        new_b = stepped(b1_ref, z, 0)
        for t in (0, 1):
            new_a = stepped(a1_ref, z, t)
            for c in range(5):
                value = new_a[c]
                if c > 0:
                    value = value - mu * spread(get(a1_ref, c, z, t) - get(b1_ref, c, z, t), index)
                if t == 0:
                    own2_ref[c, z] = value
                    if c > 0:
                        d = spread(value - new_b[c], index)
                        d2_ref[c - 1, z] = d
                        if c == 4:
                            total_ref[...] += d * d
                else:
                    far2_ref[c, z] = value

    def planes(body):
        def several(i, carry):
            for k in range(UNROLL):
                body(i * UNROLL + k)
            return carry

        lax.fori_loop(0, PLANES // UNROLL, several, 0)

    total_ref[...] = jnp.zeros(ROWS, jnp.float32)
    planes(first)
    set_ghosts(a1_ref)
    set_ghosts(b1_ref, (0,))
    planes(second)
    for c in range(5):
        for z in range(PLANES):
            edge_ref[c, z : z + 1] = own2_ref[c, z, 7:8]
            beyond_ref[c, z : z + 1] = far2_ref[c, z, 0:1]
    total = jnp.sum(total_ref[...], axis=0)
    sum_ref[...] = jnp.broadcast_to(total[None, None], sum_ref.shape)


def last_kernel(st_ref, own_ref, beyond_ref, edge_ref, d_ref, sums_ref, out_ref, misfit_ref, a_ref):
    mu = nudge_factor(st_ref)
    for c in range(5):
        for z in range(PLANES):
            a_ref[c, z + 1, 8:16] = own_ref[c, z]
            a_ref[c, z + 1, 7:8] = edge_ref[c, z : z + 1]
            a_ref[c, z + 1, 16:17] = beyond_ref[c, z : z + 1]
    set_ghosts(a_ref, (0,))
    for z in range(PLANES):
        new = stepped(a_ref, z, 0)
        for c in range(5):
            value = new[c]
            if c > 0:
                value = value - mu * d_ref[c - 1, z]
            out_ref[c, z] = value
    misfit_ref[0] = jnp.sum(sums_ref[...]) * (1.0 / CELLS)


def f32(*shape):
    return jax.ShapeDtypeStruct(shape, jnp.float32)


VM = pl.BlockSpec(memory_space=pltpu.VMEM)
SM = pl.BlockSpec(memory_space=pltpu.SMEM)
PARAMS = pltpu.CompilerParams(vmem_limit_bytes=12 * 2**20)
BLOCK = (5, PLANES, 8, 128)
BLOCK4 = (4, PLANES, 8, 128)
EXTENDED = (5, PLANES + 2, 32, 128)


def twice(pairs):
    return pairs + [(a + 8, b + 8) for a, b in pairs]


def shards(state, spacing_index, strength_index, obs_offsets):
    own = state[0]
    run = lax.axis_index("run")

    p = lax.ppermute(own, "run", [(0, 8)])
    y = jnp.where(run == 0, own, p)
    p = lax.ppermute(y, "run", twice([(0, 3)]))
    q = lax.ppermute(y, "run", twice([(0, 5)]))
    y = y + p + q
    p = lax.ppermute(y, "run", twice([(0, 1), (3, 4), (5, 6)]))
    q = lax.ppermute(y, "run", twice([(0, 7), (3, 2)]))

    nat, d, near, far = pl.pallas_call(
        pack_kernel,
        out_shape=(f32(*BLOCK), f32(*BLOCK4), f32(*BLOCK), f32(*BLOCK)),
        in_specs=[SM, SM, VM, VM, VM, VM],
        out_specs=(VM,) * 4,
        compiler_params=PARAMS,
        name="pack",
    )(spacing_index, obs_offsets, own, y, p, q)

    far = lax.ppermute(
        far, "tile", [(i, (i + 1) % TILES if i % 2 else (i - 1) % TILES) for i in range(TILES)]
    )
    near = lax.ppermute(near, "tile", [(i, i ^ 1) for i in range(TILES)])

    own2, beyond, edge, d2, sums = pl.pallas_call(
        steps_kernel,
        out_shape=(
            f32(*BLOCK), f32(5, PLANES, 128), f32(5, PLANES, 128), f32(*BLOCK4), f32(TILES, 1, 128)
        ),
        in_specs=[SM, SM, SM] + [VM] * 5,
        out_specs=(VM,) * 5,
        scratch_shapes=[
            *[pltpu.VMEM(EXTENDED, jnp.float32)] * 4,
            pltpu.VMEM(BLOCK, jnp.float32),
            pltpu.VMEM(ROWS, jnp.float32),
        ],
        compiler_params=PARAMS,
        name="steps",
    )(spacing_index, strength_index, obs_offsets, own, nat, d, far, near)

    edge = lax.ppermute(edge, "tile", [(i, (i + 1) % TILES) for i in range(TILES)])
    sums = lax.all_to_all(sums, "tile", 0, 0)

    out, misfit = pl.pallas_call(
        last_kernel,
        out_shape=(f32(*BLOCK), f32(1)),
        in_specs=[SM] + [VM] * 5,
        out_specs=(VM, SM),
        scratch_shapes=[pltpu.VMEM(EXTENDED, jnp.float32)],
        compiler_params=PARAMS,
        name="last",
    )(strength_index, own2, beyond, edge, d2, sums)
    return out[None], misfit


def solution(mesh):
    placed = (P("run", None, None, "tile", None), P("run"), P("run"), P())
    return jax.shard_map(
        shards,
        mesh=mesh,
        in_specs=placed,
        out_specs=(P("run", None, None, "tile", None), P("run")),
        check_vma=False,
    )
```

time: 62.9 us -> 59.5 us (0.946)
  waiting for transfers between devices: 16 us -> 12.4 us
  Pallas kernels: 5.85 us -> 4.63 us
  starting transfers between devices: 37 us -> 38.2 us
    ppermute x1, starting transfers between devices: 2.97 us -> 8.05 us  [shards(): lax.ppermute(far, 'tile', [(i, (i + 1) % TILES if i % 2 else (i - 1) % TI...]
    ppermute x1, waiting for transfers between devices: 3.9 us -> 0.01 us  [shards(): lax.ppermute(far, 'tile', [(i, (i + 1) % TILES if i % 2 else (i - 1) % TI...]
    all_to_all x1, starting transfers between devices: 12.5 us -> 9.68 us  [shards(): sums = lax.all_to_all(sums, 'tile', 0, 0)]
    ppermute x1, starting transfers between devices: 6.99 us -> 5.84 us  [shards(): near = lax.ppermute(near, 'tile', [(i, i ^ 1) for i in range(TILES)])]
    pallas_call x1, Pallas kernels: 4.07 us -> 3 us  [shards(): pl.pallas_call(steps_kernel, out_shape=(f32(*BLOCK), f32(5, PLANES, 128),...]
where the time goes in v3:
time: 59.5 us; the launch traced here: 58.3 us
  starting transfers between devices  38.2 us (64%)
  waiting for transfers between devices  12.4 us (21%)
  Pallas kernels  4.63 us (8%)
  between operations  2.06 us (3%)
  other arithmetic  0.96 us (2%)
    all_to_all x1, starting transfers between devices, shards(): sums = lax.all_to_all(sums, 'tile', 0, 0)  9.68 us
    ppermute x1, starting transfers between devices, shards(): lax.ppermute(far, 'tile', [(i, (i + 1) % TILES if i % 2 else (i - 1) % TI...  8.05 us
    ppermute x1, starting transfers between devices, shards(): near = lax.ppermute(near, 'tile', [(i, i ^ 1) for i in range(TILES)])  5.84 us
    ppermute x1, starting transfers between devices, shards(): p = lax.ppermute(own, 'run', [(0, 8)])  4.84 us
    ppermute x1, starting transfers between devices, shards(): lax.ppermute(edge, 'tile', [(i, (i + 1) % TILES) for i in range(TILES)])  4.44 us
    all_to_all x1, waiting for transfers between devices, shards(): sums = lax.all_to_all(sums, 'tile', 0, 0)  3.94 us
    pallas_call x1, Pallas kernels, shards(): pl.pallas_call(steps_kernel, out_shape=(f32(*BLOCK), f32(5, PLANES, 128),...  3 us
    ppermute x1, waiting for transfers between devices, shards(): p = lax.ppermute(own, 'run', [(0, 8)])  2.55 us
  transfers between devices with their start and end apart: 9, of which 8 were waited for; matrix products, arithmetic and copies ran while one was open for 0% of the time, Pallas kernels for 0%

profile of v3, /device:TPU:1, one launch (start us, length us, event | category | flops | bytes accessed | tf_op | source)
XLA Modules:
  0.0 58.3 jit_solution(8070815320388402491)
XLA Ops:
  0.6 4.8 %collective-permute-start = (f32[5,8,8,128]{3,2,1,0:T(8,128)}, f32[5,8,8,128]{3,2,1,0:T(8,128)S(1)}, u32[]{:S(2)}, u32[]{:S(2)}) collective-permute-start(f32[5,8,8,128]{3,2,1,0:T(8,128)} %bitcast.3), channel_id=1, source_target_pairs={{0,256},{1,257},{2,258},{3,259},{4,260},{5,261},{6,262},{7,263},{8... | collective-permute-start | bytes 491528 | tf_op jit(solution)/shard_map/ppermute | solution.py:254
  5.5 2.5 %collective-permute-done = f32[5,8,8,128]{3,2,1,0:T(8,128)S(1)} collective-permute-done((f32[5,8,8,128]{3,2,1,0:T(8,128)}, f32[5,8,8,128]{3,2,1,0:T(8,128)S(1)}, u32[]{:S(2)}, u32[]{:S(2)}) %collective-permute-start) | collective-permute-done | bytes 163872 | tf_op jit(solution)/shard_map/ppermute | solution.py:254
  8.0 0.9 %broadcast_select_fusion = f32[5,8,8,128]{3,2,1,0:T(8,128)S(1)} fusion(f32[5,8,8,128]{3,2,1,0:T(8,128)S(1)} %collective-permute-done, pred[]{:T(512)S(6)} %eq.3, f32[1,5,8,8,128]{4,3,2,1,0:T(8,128)} %param.4), kind=kLoop, calls=%fused_computation.1 | loop fusion | flops 40960 | bytes 491521 | tf_op jit(solution)/shard_map/jit(_where)/select_n | solution.py:255
  9.0 0.0 copy-start.1
  9.0 0.0 copy-start
  9.0 1.4 %collective-permute-start.1 = (f32[5,8,8,128]{3,2,1,0:T(8,128)S(1)}, f32[5,8,8,128]{3,2,1,0:T(8,128)S(1)}, u32[]{:S(2)}, u32[]{:S(2)}) collective-permute-start(f32[5,8,8,128]{3,2,1,0:T(8,128)S(1)} %broadcast_select_fusion), channel_id=1, source_target_pairs={{0,96},{256,352},{1,97},{257,353},{2,98},{258,354},{3,99},{259,355... | collective-permute-start | bytes 491528 | tf_op jit(solution)/shard_map/ppermute | solution.py:256
  10.4 1.3 %collective-permute-start.2 = (f32[5,8,8,128]{3,2,1,0:T(8,128)S(1)}, f32[5,8,8,128]{3,2,1,0:T(8,128)S(1)}, u32[]{:S(2)}, u32[]{:S(2)}) collective-permute-start(f32[5,8,8,128]{3,2,1,0:T(8,128)S(1)} %broadcast_select_fusion), channel_id=1, source_target_pairs={{0,160},{256,416},{1,161},{257,417},{2,162},{258,418},{3,163},{259... | collective-permute-start | bytes 491528 | tf_op jit(solution)/shard_map/ppermute | solution.py:257
  11.7 0.9 %collective-permute-done.1 = f32[5,8,8,128]{3,2,1,0:T(8,128)S(1)} collective-permute-done((f32[5,8,8,128]{3,2,1,0:T(8,128)S(1)}, f32[5,8,8,128]{3,2,1,0:T(8,128)S(1)}, u32[]{:S(2)}, u32[]{:S(2)}) %collective-permute-start.1) | collective-permute-done | bytes 163872 | tf_op jit(solution)/shard_map/ppermute | solution.py:256
  12.7 1.3 %collective-permute-done.2 = f32[5,8,8,128]{3,2,1,0:T(8,128)S(1)} collective-permute-done((f32[5,8,8,128]{3,2,1,0:T(8,128)S(1)}, f32[5,8,8,128]{3,2,1,0:T(8,128)S(1)}, u32[]{:S(2)}, u32[]{:S(2)}) %collective-permute-start.2) | collective-permute-done | bytes 163872 | tf_op jit(solution)/shard_map/ppermute | solution.py:257
  14.0 1.3 %collective-permute-start.3 = (f32[5,8,8,128]{3,2,1,0:T(8,128)S(1)}, f32[5,8,8,128]{3,2,1,0:T(8,128)S(1)}, u32[]{:S(2)}, u32[]{:S(2)}) collective-permute-start(f32[5,8,8,128]{3,2,1,0:T(8,128)S(1)} %add_add_fusion.y_ref), channel_id=1, source_target_pairs={{0,32},{96,128},{160,192},{256,288},{352,384},{416,448},{1,33},{97... | collective-permute-start | bytes 491528 | tf_op jit(solution)/shard_map/ppermute | solution.py:259
  15.3 1.3 %collective-permute-start.4 = (f32[5,8,8,128]{3,2,1,0:T(8,128)S(1)}, f32[5,8,8,128]{3,2,1,0:T(8,128)S(1)}, u32[]{:S(2)}, u32[]{:S(2)}) collective-permute-start(f32[5,8,8,128]{3,2,1,0:T(8,128)S(1)} %add_add_fusion.y_ref), channel_id=1, source_target_pairs={{0,224},{96,64},{256,480},{352,320},{1,225},{97,65},{257,481},{353... | collective-permute-start | bytes 491528 | tf_op jit(solution)/shard_map/ppermute | solution.py:260
  16.6 0.0 copy-done.1
  16.6 0.1 copy.7.off_ref
  17.4 1.2 %collective-permute-done.3.p_ref = f32[5,8,8,128]{3,2,1,0:T(8,128)S(1)} collective-permute-done((f32[5,8,8,128]{3,2,1,0:T(8,128)S(1)}, f32[5,8,8,128]{3,2,1,0:T(8,128)S(1)}, u32[]{:S(2)}, u32[]{:S(2)}) %collective-permute-start.3) | collective-permute-done | bytes 163872 | tf_op jit(solution)/shard_map/ppermute | solution.py:259
  18.5 1.3 %collective-permute-done.4.q_ref = f32[5,8,8,128]{3,2,1,0:T(8,128)S(1)} collective-permute-done((f32[5,8,8,128]{3,2,1,0:T(8,128)S(1)}, f32[5,8,8,128]{3,2,1,0:T(8,128)S(1)}, u32[]{:S(2)}, u32[]{:S(2)}) %collective-permute-start.4) | collective-permute-done | bytes 163872 | tf_op jit(solution)/shard_map/ppermute | solution.py:260
  19.8 0.0 copy-done
  19.8 0.7 %pack.1 = (f32[5,8,8,128]{3,2,1,0:T(8,128)S(1)}, f32[4,8,8,128]{3,2,1,0:T(8,128)S(1)}, f32[5,8,8,128]{3,2,1,0:T(8,128)S(1)}, f32[5,8,8,128]{3,2,1,0:T(8,128)S(1)}) custom-call(s32[1]{0:T(128)S(6)} %copy.8.sp_ref, s32[8,2]{1,0:T(8,128)S(1)} %copy.7.off_ref, f32[5,8,8,128]{3,2,1,0:T(8,128)S(1)} %bitcast.4, f32[5,8,8,128]{3,2,1,0:T(8,128)S(1)} %add_add_fusion.y_ref, ...), custom_call_target="tpu_custom_call" | custom-call | tf_op jit(solution)/shard_map/pack/pallas_call | solution.py:262
  20.6 8.1 %collective-permute-start.5 = (f32[5,8,8,128]{3,2,1,0:T(8,128)S(1)}, f32[5,8,8,128]{3,2,1,0:T(8,128)S(1)}, u32[]{:S(2)}, u32[]{:S(2)}) collective-permute-start(f32[5,8,8,128]{3,2,1,0:T(8,128)S(1)} %get-tuple-element.15), channel_id=1, source_target_pairs={{0,31},{1,2},{2,1},{3,4},{4,3},{5,6},{6,5},{7,8},{8,7},{9,10},{10,... | collective-permute-start | bytes 491528 | tf_op jit(solution)/shard_map/ppermute | solution.py:271
  28.6 5.8 %collective-permute-start.6 = (f32[5,8,8,128]{3,2,1,0:T(8,128)S(1)}, f32[5,8,8,128]{3,2,1,0:T(8,128)S(1)}, u32[]{:S(2)}, u32[]{:S(2)}) collective-permute-start(f32[5,8,8,128]{3,2,1,0:T(8,128)S(1)} %get-tuple-element.16), channel_id=1, source_target_pairs={{0,1},{1,0},{2,3},{3,2},{4,5},{5,4},{6,7},{7,6},{8,9},{9,8},{10,11... | collective-permute-start | bytes 491528 | tf_op jit(solution)/shard_map/ppermute | solution.py:274
  35.1 0.0 collective-permute-done.5.far_ref
  35.1 0.3 collective-permute-done.6.near_ref
  35.5 3.0 %steps.1 = (f32[5,8,8,128]{3,2,1,0:T(8,128)S(1)}, f32[5,8,128]{2,1,0:T(8,128)S(1)}, f32[5,8,128]{2,1,0:T(8,128)S(1)}, f32[4,8,8,128]{3,2,1,0:T(8,128)S(1)}, f32[32,1,128]{2,1,0:T(1,128)}) custom-call(s32[1]{0:T(128)S(6)} %copy.8.sp_ref, s32[1]{0:T(128)S(6)} %copy.9.st_ref, s32[8,2]{1,0:T(8,128)S(1)} %copy.7.off_ref, f32[5,8,8,128]{3,2,1,0:T(8,128)S(1)} %bitcast.5, ...), custom_call_target="tpu_custom_call" | custom-call | tf_op jit(solution)/shard_map/steps/pallas_call | solution.py:276
  38.5 9.7 %all-to-all-start = ((f32[32,1,128]{2,1,0:T(1,128)}), f32[32,1,128]{2,1,0:T(1,128)S(1)}, u32[]{:S(2)}, u32[]{:S(2)}) async-start(f32[32,1,128]{2,1,0:T(1,128)} %get-tuple-element.21), calls=%async_computation | async-start | bytes 32768 | tf_op jit(solution)/shard_map/all_to_all | solution.py:293
  48.2 4.4 %collective-permute-start.7 = (f32[5,8,128]{2,1,0:T(8,128)S(1)}, f32[5,8,128]{2,1,0:T(8,128)S(1)}, u32[]{:S(2)}, u32[]{:S(2)}) collective-permute-start(f32[5,8,128]{2,1,0:T(8,128)S(1)} %get-tuple-element.19), channel_id=1, source_target_pairs={{0,1},{1,2},{2,3},{3,4},{4,5},{5,6},{6,7},{7,8},{8,9},{9,10},{10,1... | collective-permute-start | bytes 61448 | tf_op jit(solution)/shard_map/ppermute | solution.py:292
  52.6 0.9 %collective-permute-done.7.edge_ref = f32[5,8,128]{2,1,0:T(8,128)S(1)} collective-permute-done((f32[5,8,128]{2,1,0:T(8,128)S(1)}, f32[5,8,128]{2,1,0:T(8,128)S(1)}, u32[]{:S(2)}, u32[]{:S(2)}) %collective-permute-start.7) | collective-permute-done | bytes 20512 | tf_op jit(solution)/shard_map/ppermute | solution.py:292
  53.5 3.9 %all-to-all-done.sums_ref = f32[32,1,128]{2,1,0:T(1,128)S(1)} async-done(((f32[32,1,128]{2,1,0:T(1,128)}), f32[32,1,128]{2,1,0:T(1,128)S(1)}, u32[]{:S(2)}, u32[]{:S(2)}) %all-to-all-start) | async-done | bytes 16416 | tf_op jit(solution)/shard_map/all_to_all | solution.py:293
  57.4 0.9 %last.1 = (f32[5,8,8,128]{3,2,1,0:T(8,128)}, f32[1]{0:T(128)}) custom-call(s32[1]{0:T(128)S(6)} %copy.9.st_ref, f32[5,8,8,128]{3,2,1,0:T(8,128)S(1)} %get-tuple-element.17.own_ref, f32[5,8,128]{2,1,0:T(8,128)S(1)} %get-tuple-element.18.beyond_ref, f32[5,8,128]{2,1,0:T(8,128)S(1)} %collective-permute-done.7.edge_ref, ...), custom_call_target="tpu_custom_call" | custom-call | tf_op jit(solution)/shard_map/last/pallas_call | solution.py:295
  (1 shorter events, 0.0 us)
Async XLA Ops:
  0.6 7.4 %collective-permute-start = (f32[5,8,8,128]{3,2,1,0:T(8,128)}, f32[5,8,8,128]{3,2,1,0:T(8,128)S(1)}, u32[]{:S(2)}, u32[]{:S(2)}) collective-permute-start(f32[5,8,8,128]{3,2,1,0:T(8,128)} %bitcast.3), channel_id=1, source_target_pairs={{0,256},{1,257},{2,258},{3,259},{4,260},{5,261},{6,262},{7,263},{8... | collective-permute-start | bytes 491528 | tf_op jit(solution)/shard_map/ppermute | solution.py:254
  9.0 7.7 %copy-start.1 = (s32[8,2]{0,1:T(2,128)S(1)}, s32[8,2]{0,1:T(2,128)}, u32[]{:S(2)}) copy-start(s32[8,2]{0,1:T(2,128)} %param.7) | copy-start | bytes 196
  9.0 10.8 %copy-start = (f32[1,5,8,8,128]{4,3,2,1,0:T(8,128)S(1)}, f32[1,5,8,8,128]{4,3,2,1,0:T(8,128)}, u32[]{:S(2)}) copy-start(f32[1,5,8,8,128]{4,3,2,1,0:T(8,128)} %param.4) | copy-start | bytes 491524
  9.0 3.7 %collective-permute-start.1 = (f32[5,8,8,128]{3,2,1,0:T(8,128)S(1)}, f32[5,8,8,128]{3,2,1,0:T(8,128)S(1)}, u32[]{:S(2)}, u32[]{:S(2)}) collective-permute-start(f32[5,8,8,128]{3,2,1,0:T(8,128)S(1)} %broadcast_select_fusion), channel_id=1, source_target_pairs={{0,96},{256,352},{1,97},{257,353},{2,98},{258,354},{3,99},{259,355... | collective-permute-start | bytes 491528 | tf_op jit(solution)/shard_map/ppermute | solution.py:256
  10.4 3.5 %collective-permute-start.2 = (f32[5,8,8,128]{3,2,1,0:T(8,128)S(1)}, f32[5,8,8,128]{3,2,1,0:T(8,128)S(1)}, u32[]{:S(2)}, u32[]{:S(2)}) collective-permute-start(f32[5,8,8,128]{3,2,1,0:T(8,128)S(1)} %broadcast_select_fusion), channel_id=1, source_target_pairs={{0,160},{256,416},{1,161},{257,417},{2,162},{258,418},{3,163},{259... | collective-permute-start | bytes 491528 | tf_op jit(solution)/shard_map/ppermute | solution.py:257
  14.0 4.5 %collective-permute-start.3 = (f32[5,8,8,128]{3,2,1,0:T(8,128)S(1)}, f32[5,8,8,128]{3,2,1,0:T(8,128)S(1)}, u32[]{:S(2)}, u32[]{:S(2)}) collective-permute-start(f32[5,8,8,128]{3,2,1,0:T(8,128)S(1)} %add_add_fusion.y_ref), channel_id=1, source_target_pairs={{0,32},{96,128},{160,192},{256,288},{352,384},{416,448},{1,33},{97... | collective-permute-start | bytes 491528 | tf_op jit(solution)/shard_map/ppermute | solution.py:259
  15.3 4.5 %collective-permute-start.4 = (f32[5,8,8,128]{3,2,1,0:T(8,128)S(1)}, f32[5,8,8,128]{3,2,1,0:T(8,128)S(1)}, u32[]{:S(2)}, u32[]{:S(2)}) collective-permute-start(f32[5,8,8,128]{3,2,1,0:T(8,128)S(1)} %add_add_fusion.y_ref), channel_id=1, source_target_pairs={{0,224},{96,64},{256,480},{352,320},{1,225},{97,65},{257,481},{353... | collective-permute-start | bytes 491528 | tf_op jit(solution)/shard_map/ppermute | solution.py:260
  20.6 14.6 %collective-permute-start.5 = (f32[5,8,8,128]{3,2,1,0:T(8,128)S(1)}, f32[5,8,8,128]{3,2,1,0:T(8,128)S(1)}, u32[]{:S(2)}, u32[]{:S(2)}) collective-permute-start(f32[5,8,8,128]{3,2,1,0:T(8,128)S(1)} %get-tuple-element.15), channel_id=1, source_target_pairs={{0,31},{1,2},{2,1},{3,4},{4,3},{5,6},{6,5},{7,8},{8,7},{9,10},{10,... | collective-permute-start | bytes 491528 | tf_op jit(solution)/shard_map/ppermute | solution.py:271
  28.6 6.9 %collective-permute-start.6 = (f32[5,8,8,128]{3,2,1,0:T(8,128)S(1)}, f32[5,8,8,128]{3,2,1,0:T(8,128)S(1)}, u32[]{:S(2)}, u32[]{:S(2)}) collective-permute-start(f32[5,8,8,128]{3,2,1,0:T(8,128)S(1)} %get-tuple-element.16), channel_id=1, source_target_pairs={{0,1},{1,0},{2,3},{3,2},{4,5},{5,4},{6,7},{7,6},{8,9},{9,8},{10,11... | collective-permute-start | bytes 491528 | tf_op jit(solution)/shard_map/ppermute | solution.py:274
  38.5 19.0 %all-to-all-start = ((f32[32,1,128]{2,1,0:T(1,128)}), f32[32,1,128]{2,1,0:T(1,128)S(1)}, u32[]{:S(2)}, u32[]{:S(2)}) async-start(f32[32,1,128]{2,1,0:T(1,128)} %get-tuple-element.21), calls=%async_computation | async-start | bytes 32768 | tf_op jit(solution)/shard_map/all_to_all | solution.py:293
  48.2 5.3 %collective-permute-start.7 = (f32[5,8,128]{2,1,0:T(8,128)S(1)}, f32[5,8,128]{2,1,0:T(8,128)S(1)}, u32[]{:S(2)}, u32[]{:S(2)}) collective-permute-start(f32[5,8,128]{2,1,0:T(8,128)S(1)} %get-tuple-element.19), channel_id=1, source_target_pairs={{0,1},{1,2},{2,3},{3,4},{4,5},{5,6},{6,7},{7,8},{8,9},{9,10},{10,1... | collective-permute-start | bytes 61448 | tf_op jit(solution)/shard_map/ppermute | solution.py:292

commit v4 on v3

--- a/solution.py
+++ b/solution.py
@@ -116,16 +116,18 @@
     return jnp.where(lax.axis_index("run") == 0, 0.0, DT * strength)
 
 
-def pack_kernel(sp_ref, off_ref, own_ref, y_ref, p_ref, q_ref, nat_ref, d_ref, near_ref, far_ref):
+def pack_kernel(sp_ref, off_ref, own_ref, y_ref, u_ref, v_ref, p_ref, e_ref, h_ref, nat_ref, d_ref, near_ref, far_ref):
     spread = Spread(sp_ref, off_ref)
     sub = sub_ids()
     even = lax.rem(lax.axis_index("tile"), 2) == 0
     to_near = (sub >= 4) == even
+    root = lax.axis_index("run") == 0
     for z in range(PLANES):
         keep = spread.plane(z)
         for c in range(5):
             own = own_ref[c, z]
-            nat = y_ref[c, z] + p_ref[c, z] + q_ref[c, z]
+            nat = (y_ref[c, z] + u_ref[c, z] + v_ref[c, z]) + (p_ref[c, z] + e_ref[c, z] + h_ref[c, z])
+            nat = jnp.where(root, own, nat)
             nat_ref[c, z] = nat
             if c > 0:
                 d = spread(own - nat, keep)
@@ -137,7 +139,7 @@
 
 
 def steps_kernel(
-    sp_ref, st_ref, off_ref, own_ref, nat_ref, d_ref, far_ref, near_ref,
+    sp_ref, st_ref, off_ref, own_ref, nat_ref, d_ref, near_ref, far_ref,
     own2_ref, beyond_ref, edge_ref, d2_ref, sum_ref, a_ref, b_ref, a1_ref, b1_ref, far2_ref, total_ref,
 ):
     spread = Spread(sp_ref, off_ref)
@@ -243,30 +245,27 @@
 EXTENDED = (5, PLANES + 2, 32, 128)
 
 
-def twice(pairs):
-    return pairs + [(a + 8, b + 8) for a, b in pairs]
-
-
 def shards(state, spacing_index, strength_index, obs_offsets):
     own = state[0]
-    run = lax.axis_index("run")
-
-    p = lax.ppermute(own, "run", [(0, 8)])
-    y = jnp.where(run == 0, own, p)
-    p = lax.ppermute(y, "run", twice([(0, 3)]))
-    q = lax.ppermute(y, "run", twice([(0, 5)]))
-    y = y + p + q
-    p = lax.ppermute(y, "run", twice([(0, 1), (3, 4), (5, 6)]))
-    q = lax.ppermute(y, "run", twice([(0, 7), (3, 2)]))
+
+    def send(x, pairs):
+        return lax.ppermute(x, "run", pairs)
+
+    p = send(own, [(0, 8)])
+    a, b, e = send(own, [(0, 2)]), send(own, [(0, 6)]), send(own, [(0, 4)])
+    f, g, h = send(p, [(8, 10)]), send(p, [(8, 14)]), send(p, [(8, 12)])
+    y = a + b + f + g
+    u = send(y, [(2, 3), (6, 7), (10, 11), (14, 15)])
+    v = send(y, [(2, 1), (6, 5), (10, 9), (14, 13)])
 
     nat, d, near, far = pl.pallas_call(
         pack_kernel,
         out_shape=(f32(*BLOCK), f32(*BLOCK4), f32(*BLOCK), f32(*BLOCK)),
-        in_specs=[SM, SM, VM, VM, VM, VM],
+        in_specs=[SM, SM] + [VM] * 7,
         out_specs=(VM,) * 4,
         compiler_params=PARAMS,
         name="pack",
-    )(spacing_index, obs_offsets, own, y, p, q)
+    )(spacing_index, obs_offsets, own, y, u, v, p, e, h)
 
     far = lax.ppermute(
         far, "tile", [(i, (i + 1) % TILES if i % 2 else (i - 1) % TILES) for i in range(TILES)]
@@ -287,7 +286,7 @@
         ],
         compiler_params=PARAMS,
         name="steps",
-    )(spacing_index, strength_index, obs_offsets, own, nat, d, far, near)
+    )(spacing_index, strength_index, obs_offsets, own, nat, d, near, far)
 
     edge = lax.ppermute(edge, "tile", [(i, (i + 1) % TILES) for i in range(TILES)])
     sums = lax.all_to_all(sums, "tile", 0, 0)

time: 59.5 us -> 58.2 us (0.978)
  the two profiles are of different devices: /device:TPU:1 before, /device:TPU:105 now
where the time goes in v4:
time: 58.2 us; the launch traced here: 57.8 us
  starting transfers between devices  36.4 us (63%)
  waiting for transfers between devices  14.5 us (25%)
  Pallas kernels  4.64 us (8%)
  between operations  2.14 us (4%)
    all_to_all x1, starting transfers between devices, shards(): sums = lax.all_to_all(sums, 'tile', 0, 0)  10 us
    ppermute x1, starting transfers between devices, shards(): lax.ppermute(far, 'tile', [(i, (i + 1) % TILES if i % 2 else (i - 1) % TI...  9.91 us
    ppermute x9, waiting for transfers between devices, send(): return lax.ppermute(x, 'run', pairs)  9.3 us
    ppermute x9, starting transfers between devices, send(): return lax.ppermute(x, 'run', pairs)  6.79 us
    ppermute x1, starting transfers between devices, shards(): near = lax.ppermute(near, 'tile', [(i, i ^ 1) for i in range(TILES)])  5.25 us
    ppermute x1, starting transfers between devices, shards(): lax.ppermute(edge, 'tile', [(i, (i + 1) % TILES) for i in range(TILES)])  4.44 us
    all_to_all x1, waiting for transfers between devices, shards(): sums = lax.all_to_all(sums, 'tile', 0, 0)  3.96 us
    pallas_call x1, Pallas kernels, shards(): pl.pallas_call(steps_kernel, out_shape=(f32(*BLOCK), f32(5, PLANES, 128),...  3 us
  transfers between devices with their start and end apart: 13, of which 4 were waited for; matrix products, arithmetic and copies ran while one was open for 0% of the time, Pallas kernels for 0%

profile of v4, /device:TPU:105, one launch (start us, length us, event | category | flops | bytes accessed | tf_op | source)
XLA Modules:
  0.0 57.8 jit_solution(2832074406275135161)
XLA Ops:
  0.6 0.0 copy-start.1
  0.6 0.0 copy-start
  0.6 0.8 %collective-permute-start.2 = (f32[5,8,8,128]{3,2,1,0:T(8,128)}, f32[5,8,8,128]{3,2,1,0:T(8,128)S(1)}, u32[]{:S(2)}, u32[]{:S(2)}) collective-permute-start(f32[5,8,8,128]{3,2,1,0:T(8,128)} %bitcast.2), channel_id=1, source_target_pairs={{0,256},{1,257},{2,258},{3,259},{4,260},{5,261},{6,262},{7,263},{8... | collective-permute-start | bytes 491528 | tf_op jit(solution)/shard_map/ppermute | solution.py:252
  1.5 0.7 %collective-permute-start = (f32[5,8,8,128]{3,2,1,0:T(8,128)}, f32[5,8,8,128]{3,2,1,0:T(8,128)S(1)}, u32[]{:S(2)}, u32[]{:S(2)}) collective-permute-start(f32[5,8,8,128]{3,2,1,0:T(8,128)} %bitcast.3), channel_id=1, source_target_pairs={{0,64},{1,65},{2,66},{3,67},{4,68},{5,69},{6,70},{7,71},{8,72},{9,... | collective-permute-start | bytes 491528 | tf_op jit(solution)/shard_map/ppermute | solution.py:252
  2.1 0.7 %collective-permute-start.1 = (f32[5,8,8,128]{3,2,1,0:T(8,128)}, f32[5,8,8,128]{3,2,1,0:T(8,128)S(1)}, u32[]{:S(2)}, u32[]{:S(2)}) collective-permute-start(f32[5,8,8,128]{3,2,1,0:T(8,128)} %bitcast.4), channel_id=1, source_target_pairs={{0,192},{1,193},{2,194},{3,195},{4,196},{5,197},{6,198},{7,199},{8... | collective-permute-start | bytes 491528 | tf_op jit(solution)/shard_map/ppermute | solution.py:252
  2.8 0.0 collective-permute-done.2.p_ref
  2.8 0.7 %collective-permute-start.3 = (f32[5,8,8,128]{3,2,1,0:T(8,128)S(1)}, f32[5,8,8,128]{3,2,1,0:T(8,128)S(1)}, u32[]{:S(2)}, u32[]{:S(2)}) collective-permute-start(f32[5,8,8,128]{3,2,1,0:T(8,128)S(1)} %collective-permute-done.2.p_ref), channel_id=1, source_target_pairs={{256,320},{257,321},{258,322},{259,323},{260,324},{261,325},{262,3... | collective-permute-start | bytes 491528 | tf_op jit(solution)/shard_map/ppermute | solution.py:252
  3.5 0.7 %collective-permute-start.4 = (f32[5,8,8,128]{3,2,1,0:T(8,128)S(1)}, f32[5,8,8,128]{3,2,1,0:T(8,128)S(1)}, u32[]{:S(2)}, u32[]{:S(2)}) collective-permute-start(f32[5,8,8,128]{3,2,1,0:T(8,128)S(1)} %collective-permute-done.2.p_ref), channel_id=1, source_target_pairs={{256,448},{257,449},{258,450},{259,451},{260,452},{261,453},{262,4... | collective-permute-start | bytes 491528 | tf_op jit(solution)/shard_map/ppermute | solution.py:252
  4.2 0.7 %collective-permute-start.7 = (f32[5,8,8,128]{3,2,1,0:T(8,128)}, f32[5,8,8,128]{3,2,1,0:T(8,128)S(1)}, u32[]{:S(2)}, u32[]{:S(2)}) collective-permute-start(f32[5,8,8,128]{3,2,1,0:T(8,128)} %bitcast.5), channel_id=1, source_target_pairs={{0,128},{1,129},{2,130},{3,131},{4,132},{5,133},{6,134},{7,135},{8... | collective-permute-start | bytes 491528 | tf_op jit(solution)/shard_map/ppermute | solution.py:252
  4.9 0.0 collective-permute-done
  4.9 0.7 %collective-permute-start.8 = (f32[5,8,8,128]{3,2,1,0:T(8,128)S(1)}, f32[5,8,8,128]{3,2,1,0:T(8,128)S(1)}, u32[]{:S(2)}, u32[]{:S(2)}) collective-permute-start(f32[5,8,8,128]{3,2,1,0:T(8,128)S(1)} %collective-permute-done.2.p_ref), channel_id=1, source_target_pairs={{256,384},{257,385},{258,386},{259,387},{260,388},{261,389},{262,3... | collective-permute-start | bytes 491528 | tf_op jit(solution)/shard_map/ppermute | solution.py:252
  5.6 0.0 collective-permute-done.1
  5.6 0.0 collective-permute-done.3
  5.6 0.0 collective-permute-done.4
  5.6 0.7 %collective-permute-start.5 = (f32[5,8,8,128]{3,2,1,0:T(8,128)S(1)}, f32[5,8,8,128]{3,2,1,0:T(8,128)S(1)}, u32[]{:S(2)}, u32[]{:S(2)}) collective-permute-start(f32[5,8,8,128]{3,2,1,0:T(8,128)S(1)} %add_add_fusion.y_ref), channel_id=1, source_target_pairs={{64,96},{192,224},{320,352},{448,480},{65,97},{193,225},{321,353},... | collective-permute-start | bytes 491528 | tf_op jit(solution)/shard_map/ppermute | solution.py:252
  6.3 1.3 %collective-permute-start.6 = (f32[5,8,8,128]{3,2,1,0:T(8,128)S(1)}, f32[5,8,8,128]{3,2,1,0:T(8,128)S(1)}, u32[]{:S(2)}, u32[]{:S(2)}) collective-permute-start(f32[5,8,8,128]{3,2,1,0:T(8,128)S(1)} %add_add_fusion.y_ref), channel_id=1, source_target_pairs={{64,32},{192,160},{320,288},{448,416},{65,33},{193,161},{321,289},... | collective-permute-start | bytes 491528 | tf_op jit(solution)/shard_map/ppermute | solution.py:252
  7.6 0.0 copy-done.1
  7.6 0.1 copy.7.off_ref
  8.4 0.0 collective-permute-done.7.e_ref
  8.4 0.0 collective-permute-done.8.h_ref
  8.4 0.0 collective-permute-done.5.u_ref
  8.4 9.3 %collective-permute-done.6.v_ref = f32[5,8,8,128]{3,2,1,0:T(8,128)S(1)} collective-permute-done((f32[5,8,8,128]{3,2,1,0:T(8,128)S(1)}, f32[5,8,8,128]{3,2,1,0:T(8,128)S(1)}, u32[]{:S(2)}, u32[]{:S(2)}) %collective-permute-start.6) | collective-permute-done | bytes 163872 | tf_op jit(solution)/shard_map/ppermute | solution.py:252
  17.7 0.0 copy-done
  17.7 0.7 %pack.1 = (f32[5,8,8,128]{3,2,1,0:T(8,128)S(1)}, f32[4,8,8,128]{3,2,1,0:T(8,128)S(1)}, f32[5,8,8,128]{3,2,1,0:T(8,128)S(1)}, f32[5,8,8,128]{3,2,1,0:T(8,128)S(1)}) custom-call(s32[1]{0:T(128)S(6)} %copy.8.sp_ref, s32[8,2]{1,0:T(8,128)S(1)} %copy.7.off_ref, f32[5,8,8,128]{3,2,1,0:T(8,128)S(1)} %bitcast.6, f32[5,8,8,128]{3,2,1,0:T(8,128)S(1)} %add_add_fusion.y_ref, ...), custom_call_target="tpu_custom_call" | custom-call | tf_op jit(solution)/shard_map/pack/pallas_call | solution.py:261
  18.4 9.9 %collective-permute-start.10 = (f32[5,8,8,128]{3,2,1,0:T(8,128)S(1)}, f32[5,8,8,128]{3,2,1,0:T(8,128)S(1)}, u32[]{:S(2)}, u32[]{:S(2)}) collective-permute-start(f32[5,8,8,128]{3,2,1,0:T(8,128)S(1)} %get-tuple-element.16), channel_id=1, source_target_pairs={{0,31},{1,2},{2,1},{3,4},{4,3},{5,6},{6,5},{7,8},{8,7},{9,10},{10,... | collective-permute-start | bytes 491528 | tf_op jit(solution)/shard_map/ppermute | solution.py:270
  28.3 5.2 %collective-permute-start.9 = (f32[5,8,8,128]{3,2,1,0:T(8,128)S(1)}, f32[5,8,8,128]{3,2,1,0:T(8,128)S(1)}, u32[]{:S(2)}, u32[]{:S(2)}) collective-permute-start(f32[5,8,8,128]{3,2,1,0:T(8,128)S(1)} %get-tuple-element.15), channel_id=1, source_target_pairs={{0,1},{1,0},{2,3},{3,2},{4,5},{5,4},{6,7},{7,6},{8,9},{9,8},{10,11... | collective-permute-start | bytes 491528 | tf_op jit(solution)/shard_map/ppermute | solution.py:273
  34.2 0.0 collective-permute-done.10.far_ref
  34.2 0.3 collective-permute-done.9.near_ref
  34.6 3.0 %steps.1 = (f32[5,8,8,128]{3,2,1,0:T(8,128)S(1)}, f32[5,8,128]{2,1,0:T(8,128)S(1)}, f32[5,8,128]{2,1,0:T(8,128)S(1)}, f32[4,8,8,128]{3,2,1,0:T(8,128)S(1)}, f32[32,1,128]{2,1,0:T(1,128)}) custom-call(s32[1]{0:T(128)S(6)} %copy.8.sp_ref, s32[1]{0:T(128)S(6)} %copy.9.st_ref, s32[8,2]{1,0:T(8,128)S(1)} %copy.7.off_ref, f32[5,8,8,128]{3,2,1,0:T(8,128)S(1)} %bitcast.7, ...), custom_call_target="tpu_custom_call" | custom-call | tf_op jit(solution)/shard_map/steps/pallas_call | solution.py:275
  37.6 10.0 %all-to-all-start = ((f32[32,1,128]{2,1,0:T(1,128)}), f32[32,1,128]{2,1,0:T(1,128)S(1)}, u32[]{:S(2)}, u32[]{:S(2)}) async-start(f32[32,1,128]{2,1,0:T(1,128)} %get-tuple-element.21), calls=%async_computation | async-start | bytes 32768 | tf_op jit(solution)/shard_map/all_to_all | solution.py:292
  47.6 4.4 %collective-permute-start.11 = (f32[5,8,128]{2,1,0:T(8,128)S(1)}, f32[5,8,128]{2,1,0:T(8,128)S(1)}, u32[]{:S(2)}, u32[]{:S(2)}) collective-permute-start(f32[5,8,128]{2,1,0:T(8,128)S(1)} %get-tuple-element.19), channel_id=1, source_target_pairs={{0,1},{1,2},{2,3},{3,4},{4,5},{5,6},{6,7},{7,8},{8,9},{9,10},{10,1... | collective-permute-start | bytes 61448 | tf_op jit(solution)/shard_map/ppermute | solution.py:291
  52.0 0.9 %collective-permute-done.11.edge_ref = f32[5,8,128]{2,1,0:T(8,128)S(1)} collective-permute-done((f32[5,8,128]{2,1,0:T(8,128)S(1)}, f32[5,8,128]{2,1,0:T(8,128)S(1)}, u32[]{:S(2)}, u32[]{:S(2)}) %collective-permute-start.11) | collective-permute-done | bytes 20512 | tf_op jit(solution)/shard_map/ppermute | solution.py:291
  52.9 4.0 %all-to-all-done.sums_ref = f32[32,1,128]{2,1,0:T(1,128)S(1)} async-done(((f32[32,1,128]{2,1,0:T(1,128)}), f32[32,1,128]{2,1,0:T(1,128)S(1)}, u32[]{:S(2)}, u32[]{:S(2)}) %all-to-all-start) | async-done | bytes 16416 | tf_op jit(solution)/shard_map/all_to_all | solution.py:292
  56.9 0.9 %last.1 = (f32[5,8,8,128]{3,2,1,0:T(8,128)}, f32[1]{0:T(128)}) custom-call(s32[1]{0:T(128)S(6)} %copy.9.st_ref, f32[5,8,8,128]{3,2,1,0:T(8,128)S(1)} %get-tuple-element.17.own_ref, f32[5,8,128]{2,1,0:T(8,128)S(1)} %get-tuple-element.18.beyond_ref, f32[5,8,128]{2,1,0:T(8,128)S(1)} %collective-permute-done.11.edge_ref, ...), custom_call_target="tpu_custom_call" | custom-call | tf_op jit(solution)/shard_map/last/pallas_call | solution.py:294
  (1 shorter events, 0.0 us)
Async XLA Ops:
  0.6 7.0 %copy-start.1 = (s32[8,2]{0,1:T(2,128)S(1)}, s32[8,2]{0,1:T(2,128)}, u32[]{:S(2)}) copy-start(s32[8,2]{0,1:T(2,128)} %param.7) | copy-start | bytes 196
  0.6 17.0 %copy-start = (f32[1,5,8,8,128]{4,3,2,1,0:T(8,128)S(1)}, f32[1,5,8,8,128]{4,3,2,1,0:T(8,128)}, u32[]{:S(2)}) copy-start(f32[1,5,8,8,128]{4,3,2,1,0:T(8,128)} %param.4) | copy-start | bytes 491524
  0.6 2.2 %collective-permute-start.2 = (f32[5,8,8,128]{3,2,1,0:T(8,128)}, f32[5,8,8,128]{3,2,1,0:T(8,128)S(1)}, u32[]{:S(2)}, u32[]{:S(2)}) collective-permute-start(f32[5,8,8,128]{3,2,1,0:T(8,128)} %bitcast.2), channel_id=1, source_target_pairs={{0,256},{1,257},{2,258},{3,259},{4,260},{5,261},{6,262},{7,263},{8... | collective-permute-start | bytes 491528 | tf_op jit(solution)/shard_map/ppermute | solution.py:252
  1.5 3.4 %collective-permute-start = (f32[5,8,8,128]{3,2,1,0:T(8,128)}, f32[5,8,8,128]{3,2,1,0:T(8,128)S(1)}, u32[]{:S(2)}, u32[]{:S(2)}) collective-permute-start(f32[5,8,8,128]{3,2,1,0:T(8,128)} %bitcast.3), channel_id=1, source_target_pairs={{0,64},{1,65},{2,66},{3,67},{4,68},{5,69},{6,70},{7,71},{8,72},{9,... | collective-permute-start | bytes 491528 | tf_op jit(solution)/shard_map/ppermute | solution.py:252
  2.1 3.4 %collective-permute-start.1 = (f32[5,8,8,128]{3,2,1,0:T(8,128)}, f32[5,8,8,128]{3,2,1,0:T(8,128)S(1)}, u32[]{:S(2)}, u32[]{:S(2)}) collective-permute-start(f32[5,8,8,128]{3,2,1,0:T(8,128)} %bitcast.4), channel_id=1, source_target_pairs={{0,192},{1,193},{2,194},{3,195},{4,196},{5,197},{6,198},{7,199},{8... | collective-permute-start | bytes 491528 | tf_op jit(solution)/shard_map/ppermute | solution.py:252
  2.8 2.7 %collective-permute-start.3 = (f32[5,8,8,128]{3,2,1,0:T(8,128)S(1)}, f32[5,8,8,128]{3,2,1,0:T(8,128)S(1)}, u32[]{:S(2)}, u32[]{:S(2)}) collective-permute-start(f32[5,8,8,128]{3,2,1,0:T(8,128)S(1)} %collective-permute-done.2.p_ref), channel_id=1, source_target_pairs={{256,320},{257,321},{258,322},{259,323},{260,324},{261,325},{262,3... | collective-permute-start | bytes 491528 | tf_op jit(solution)/shard_map/ppermute | solution.py:252
  3.5 2.1 %collective-permute-start.4 = (f32[5,8,8,128]{3,2,1,0:T(8,128)S(1)}, f32[5,8,8,128]{3,2,1,0:T(8,128)S(1)}, u32[]{:S(2)}, u32[]{:S(2)}) collective-permute-start(f32[5,8,8,128]{3,2,1,0:T(8,128)S(1)} %collective-permute-done.2.p_ref), channel_id=1, source_target_pairs={{256,448},{257,449},{258,450},{259,451},{260,452},{261,453},{262,4... | collective-permute-start | bytes 491528 | tf_op jit(solution)/shard_map/ppermute | solution.py:252
  4.2 4.2 %collective-permute-start.7 = (f32[5,8,8,128]{3,2,1,0:T(8,128)}, f32[5,8,8,128]{3,2,1,0:T(8,128)S(1)}, u32[]{:S(2)}, u32[]{:S(2)}) collective-permute-start(f32[5,8,8,128]{3,2,1,0:T(8,128)} %bitcast.5), channel_id=1, source_target_pairs={{0,128},{1,129},{2,130},{3,131},{4,132},{5,133},{6,134},{7,135},{8... | collective-permute-start | bytes 491528 | tf_op jit(solution)/shard_map/ppermute | solution.py:252
  4.9 3.5 %collective-permute-start.8 = (f32[5,8,8,128]{3,2,1,0:T(8,128)S(1)}, f32[5,8,8,128]{3,2,1,0:T(8,128)S(1)}, u32[]{:S(2)}, u32[]{:S(2)}) collective-permute-start(f32[5,8,8,128]{3,2,1,0:T(8,128)S(1)} %collective-permute-done.2.p_ref), channel_id=1, source_target_pairs={{256,384},{257,385},{258,386},{259,387},{260,388},{261,389},{262,3... | collective-permute-start | bytes 491528 | tf_op jit(solution)/shard_map/ppermute | solution.py:252
  5.6 2.7 %collective-permute-start.5 = (f32[5,8,8,128]{3,2,1,0:T(8,128)S(1)}, f32[5,8,8,128]{3,2,1,0:T(8,128)S(1)}, u32[]{:S(2)}, u32[]{:S(2)}) collective-permute-start(f32[5,8,8,128]{3,2,1,0:T(8,128)S(1)} %add_add_fusion.y_ref), channel_id=1, source_target_pairs={{64,96},{192,224},{320,352},{448,480},{65,97},{193,225},{321,353},... | collective-permute-start | bytes 491528 | tf_op jit(solution)/shard_map/ppermute | solution.py:252
  6.3 11.4 %collective-permute-start.6 = (f32[5,8,8,128]{3,2,1,0:T(8,128)S(1)}, f32[5,8,8,128]{3,2,1,0:T(8,128)S(1)}, u32[]{:S(2)}, u32[]{:S(2)}) collective-permute-start(f32[5,8,8,128]{3,2,1,0:T(8,128)S(1)} %add_add_fusion.y_ref), channel_id=1, source_target_pairs={{64,32},{192,160},{320,288},{448,416},{65,33},{193,161},{321,289},... | collective-permute-start | bytes 491528 | tf_op jit(solution)/shard_map/ppermute | solution.py:252
  18.4 15.8 %collective-permute-start.10 = (f32[5,8,8,128]{3,2,1,0:T(8,128)S(1)}, f32[5,8,8,128]{3,2,1,0:T(8,128)S(1)}, u32[]{:S(2)}, u32[]{:S(2)}) collective-permute-start(f32[5,8,8,128]{3,2,1,0:T(8,128)S(1)} %get-tuple-element.16), channel_id=1, source_target_pairs={{0,31},{1,2},{2,1},{3,4},{4,3},{5,6},{6,5},{7,8},{8,7},{9,10},{10,... | collective-permute-start | bytes 491528 | tf_op jit(solution)/shard_map/ppermute | solution.py:270
  28.3 6.3 %collective-permute-start.9 = (f32[5,8,8,128]{3,2,1,0:T(8,128)S(1)}, f32[5,8,8,128]{3,2,1,0:T(8,128)S(1)}, u32[]{:S(2)}, u32[]{:S(2)}) collective-permute-start(f32[5,8,8,128]{3,2,1,0:T(8,128)S(1)} %get-tuple-element.15), channel_id=1, source_target_pairs={{0,1},{1,0},{2,3},{3,2},{4,5},{5,4},{6,7},{7,6},{8,9},{9,8},{10,11... | collective-permute-start | bytes 491528 | tf_op jit(solution)/shard_map/ppermute | solution.py:273
  37.6 19.3 %all-to-all-start = ((f32[32,1,128]{2,1,0:T(1,128)}), f32[32,1,128]{2,1,0:T(1,128)S(1)}, u32[]{:S(2)}, u32[]{:S(2)}) async-start(f32[32,1,128]{2,1,0:T(1,128)} %get-tuple-element.21), calls=%async_computation | async-start | bytes 32768 | tf_op jit(solution)/shard_map/all_to_all | solution.py:292
  47.6 5.3 %collective-permute-start.11 = (f32[5,8,128]{2,1,0:T(8,128)S(1)}, f32[5,8,128]{2,1,0:T(8,128)S(1)}, u32[]{:S(2)}, u32[]{:S(2)}) collective-permute-start(f32[5,8,128]{2,1,0:T(8,128)S(1)} %get-tuple-element.19), channel_id=1, source_target_pairs={{0,1},{1,2},{2,3},{3,4},{4,5},{5,6},{6,7},{7,8},{8,9},{9,10},{10,1... | collective-permute-start | bytes 61448 | tf_op jit(solution)/shard_map/ppermute | solution.py:291

commit v5 on v4

v5 whole, which is shorter than its diff:
```python
import jax
import jax.numpy as jnp
from jax import lax
from jax.experimental import pallas as pl
from jax.experimental.pallas import tpu as pltpu
from jax.sharding import PartitionSpec as P

RUNS = 16
TILES = 32
PLANES = 8
CELLS = 8 * 256 * 128

DT = 0.05
VISC = 0.05
GAMMA1 = 0.4
GRAVITY = 0.5
HOT = 1.2
COLD = 0.8

ROWS = (8, 128)
UNROLL = 4


def rolled(v, shift, axis):
    return pltpu.roll(v, shift % v.shape[axis], axis)


def sub_ids():
    return lax.broadcasted_iota(jnp.int32, ROWS, 0)


def lane_ids():
    return lax.broadcasted_iota(jnp.int32, ROWS, 1)


class Spread:
    def __init__(self, sp_ref, off_ref):
        k = sp_ref[0]
        self.off = off_ref
        self.base = [lax.shift_left(lax.shift_right_logical(ids, k), k) for ids in (sub_ids(), lane_ids())]

    def plane(self, z):
        return self.base[0] + self.off[z, 0], self.base[1] + self.off[z, 1]

    def __call__(self, e, index):
        for axis in (0, 1):
            e = jnp.take_along_axis(e, index[axis], axis=axis, mode="promise_in_bounds")
        return e


PITCH = 24


def place(z, row):
    return (z + 1) * PITCH + 8 + row


def get(ref, c, z, shift=0):
    return ref[c, pl.ds(place(z, shift), 8)]


def put(ref, c, z, value):
    ref[c, pl.ds(pl.multiple_of(place(z, 0), 8), 8)] = value


def get_edge(ref, c, row):
    return ref[c, pl.ds(place(0, row), PLANES, stride=PITCH)]


def put_edge(ref, c, row, value):
    ref[c, pl.ds(place(0, row), PLANES, stride=PITCH)] = value


def mirrored(c, low, high):
    if c == 3:
        return -low, -high
    if c == 4:
        return 2.0 * HOT - low, 2.0 * COLD - high
    return low, high


def set_ghosts(ref):
    for c in range(5):
        low, high = mirrored(c, get(ref, c, 0), get(ref, c, PLANES - 1))
        put(ref, c, -1, low)
        put(ref, c, PLANES, high)


def advanced(c0, xn, xp, zn, zp):
    yn = [rolled(v, -1, 1) for v in c0]
    yp = [rolled(v, 1, 1) for v in c0]
    flux = (
        (xn[0] * xn[1] - xp[0] * xp[1])
        + (yn[0] * yn[2] - yp[0] * yp[2])
        + (zn[0] * zn[3] - zp[0] * zp[3])
    )
    scale = (0.5 * DT) / c0[0]
    grad = (
        xn[0] * xn[4] - xp[0] * xp[4],
        yn[0] * yn[4] - yp[0] * yp[4],
        zn[0] * zn[4] - zp[0] * zp[4],
    )
    new = [c0[0] - (0.5 * DT) * flux]
    div = None
    for q in range(1, 5):
        dx, dy, dz = xn[q] - xp[q], yn[q] - yp[q], zn[q] - zp[q]
        part = (None, dx, dy, dz, None)[q]
        if part is not None:
            div = part if div is None else div + part
        adv = c0[1] * dx + c0[2] * dy + c0[3] * dz
        six = ((xn[q] + xp[q]) + (yn[q] + yp[q])) + (zn[q] + zp[q])
        change = (DT * VISC) * (six - 6.0 * c0[q]) - (0.5 * DT) * adv
        if q < 4:
            change = change - grad[q - 1] * scale
            if q == 3:
                change = change - DT * GRAVITY
        else:
            change = change - (0.5 * DT * GAMMA1) * (c0[4] * div)
        new.append(c0[q] + change)
    return new


def stepped(ref, z):
    return advanced(
        *([get(ref, c, z + dz, dx) for c in range(5)] for dz, dx in ((0, 0), (0, 1), (0, -1), (1, 0), (-1, 0)))
    )


def edge_stepped(c0, xn, xp):
    sub = sub_ids()
    zn, zp = [], []
    for c in range(5):
        low, high = mirrored(c, c0[c], c0[c])
        zn.append(jnp.where(sub == PLANES - 1, high, rolled(c0[c], -1, 0)))
        zp.append(jnp.where(sub == 0, low, rolled(c0[c], 1, 0)))
    return advanced(c0, xn, xp, zn, zp)


def nudge_factor(st_ref):
    strength = 0.5 * lax.shift_left(jnp.int32(1), st_ref[0]).astype(jnp.float32)
    return jnp.where(lax.axis_index("run") == 0, 0.0, DT * strength)


EDGES = 30


def even_tile():
    return lax.rem(lax.axis_index("tile"), 2) == 0


def tile_of(z):
    return pl.ds(pl.multiple_of(8 * z, 8), 8)


def edge_of(ref, c, row):
    return ref[c, pl.ds(row, PLANES, stride=8)]


def planes(body):
    def several(i, carry):
        for k in range(UNROLL):
            body(i * UNROLL + k)
        return carry

    lax.fori_loop(0, PLANES // UNROLL, several, 0)


def pack_kernel(
    sp_ref, off_ref, own_ref, y_ref, u_ref, v_ref, p_ref, e_ref, h_ref, nat_ref, d_ref, near_ref, far_ref
):
    spread = Spread(sp_ref, off_ref)
    even = even_tile()
    root = lax.axis_index("run") == 0
    for z in range(PLANES):
        index = spread.plane(z)
        here = pl.ds(8 * z, 8)
        for c in range(5):
            own = own_ref[c, here]
            nat = (y_ref[c, here] + u_ref[c, here] + v_ref[c, here]) + (p_ref[c, here] + e_ref[c, here] + h_ref[c, here])
            nat = jnp.where(root, own, nat)
            nat_ref[c, here] = nat
            if c > 0:
                d_ref[c - 1, here] = spread(own - nat, index)
    fields = [(ref, c) for ref in (own_ref, nat_ref) for c in range(5)]
    left = [edge_of(ref, c, row) for ref, c in fields for row in (0, 1, 2)]
    right = [edge_of(ref, c, row) for ref, c in fields for row in (6, 7)] + [edge_of(d_ref, c, 7) for c in range(4)]
    for i in range(EDGES):
        to_right = right[min(i, len(right) - 1)]
        near_ref[i] = jnp.where(even, to_right, left[i])
        far_ref[i] = jnp.where(even, left[i], to_right)


def inner_kernel(st_ref, own_ref, nat_ref, d_ref, own1_ref, nat1_ref, a_ref, b_ref):
    mu = nudge_factor(st_ref)
    for ref, source in ((a_ref, own_ref), (b_ref, nat_ref)):
        for c in range(5):
            for z in range(PLANES):
                put(ref, c, z, source[c, 8 * z : 8 * z + 8])
        set_ghosts(ref)

    def first(z):
        new_a, new_b = stepped(a_ref, z), stepped(b_ref, z)
        for c in range(5):
            own1_ref[c, tile_of(z)] = new_a[c] - mu * d_ref[c - 1, tile_of(z)] if c > 0 else new_a[c]
            nat1_ref[c, tile_of(z)] = new_b[c]

    planes(first)


def steps_kernel(
    sp_ref, st_ref, off_ref, own_ref, nat_ref, d_ref, own1_ref, nat1_ref, near_ref, far_ref,
    own2_ref, beyond_ref, edge_ref, d2_ref, sum_ref, a1_ref, b1_ref, total_ref,
):
    spread = Spread(sp_ref, off_ref)
    even = even_tile()
    mu = nudge_factor(st_ref)
    sub = sub_ids()
    off_x, columns = jnp.zeros(ROWS, jnp.int32), spread.base[1]
    for z in range(PLANES):
        off_x = jnp.where(sub == z, off_ref[z, 0], off_x)
        columns = jnp.where(sub == z, spread.base[1] + off_ref[z, 1], columns)

    def observed(row8, row9):
        return jnp.take_along_axis(
            jnp.where(off_x == 0, row8, row9), columns, axis=1, mode="promise_in_bounds"
        )

    def sent(i, from_left):
        near, far = near_ref[i], far_ref[i]
        return jnp.where(even, far, near) if from_left else jnp.where(even, near, far)

    rows, next_rows = [], []
    for k, ref in ((0, own_ref), (1, nat_ref)):
        row = {
            j: [sent((5 * k + c) * width + i, j < 0) for c in range(5)]
            for j, width, i in ((-2, 2, 0), (-1, 2, 1), (8, 3, 0), (9, 3, 1), (10, 3, 2))
        }
        for j in (0, 1, 6, 7):
            row[j] = [edge_of(ref, c, j) for c in range(5)]
        rows.append(row)
        next_rows.append({j: edge_stepped(row[j], row[j + 1], row[j - 1]) for j in (-1, 0, 7, 8, 9)})
    for c in range(1, 5):
        d = observed(rows[0][8][c] - rows[1][8][c], rows[0][9][c] - rows[1][9][c])
        next_rows[0][-1][c] -= mu * sent(20 + c - 1, True)
        for j in (0, 7):
            next_rows[0][j][c] -= mu * edge_of(d_ref, c - 1, j)
        for j in (8, 9):
            next_rows[0][j][c] -= mu * d
    for ref, source, edge in ((a1_ref, own1_ref, next_rows[0]), (b1_ref, nat1_ref, next_rows[1])):
        for c in range(5):
            for z in range(PLANES):
                put(ref, c, z, source[c, 8 * z : 8 * z + 8])
            for j in (-1, 0, 7, 8):
                put_edge(ref, c, j, edge[j][c])
        set_ghosts(ref)

    def second(z):
        index = spread.plane(z)
        new_a, new_b = stepped(a1_ref, z), stepped(b1_ref, z)
        for c in range(5):
            value = new_a[c]
            if c > 0:
                value = value - mu * spread(get(a1_ref, c, z) - get(b1_ref, c, z), index)
                d = spread(value - new_b[c], index)
                d2_ref[c - 1, z] = d
                if c == 4:
                    total_ref[...] += d * d
            own2_ref[c, tile_of(z)] = value

    total_ref[...] = jnp.zeros(ROWS, jnp.float32)
    planes(second)
    own, nat = next_rows
    new = edge_stepped(own[8], own[9], own[7])
    for c in range(5):
        if c > 0:
            new[c] -= mu * observed(own[8][c] - nat[8][c], own[9][c] - nat[9][c])
        beyond_ref[c] = new[c]
        edge_ref[c] = edge_of(own2_ref, c, 7)
    total = jnp.sum(total_ref[...], axis=0)
    sum_ref[...] = jnp.broadcast_to(total[None, None], sum_ref.shape)


def last_kernel(st_ref, own_ref, beyond_ref, edge_ref, d_ref, sums_ref, out_ref, misfit_ref, a_ref):
    mu = nudge_factor(st_ref)
    for c in range(5):
        for z in range(PLANES):
            put(a_ref, c, z, own_ref[c, 8 * z : 8 * z + 8])
        put_edge(a_ref, c, -1, edge_ref[c])
        put_edge(a_ref, c, 8, beyond_ref[c])
    set_ghosts(a_ref)
    for z in range(PLANES):
        new = stepped(a_ref, z)
        for c in range(5):
            out_ref[c, z] = new[c] - mu * d_ref[c - 1, z] if c > 0 else new[c]
    misfit_ref[0] = jnp.sum(sums_ref[...]) * (1.0 / CELLS)


def f32(*shape):
    return jax.ShapeDtypeStruct(shape, jnp.float32)


VM = pl.BlockSpec(memory_space=pltpu.VMEM)
SM = pl.BlockSpec(memory_space=pltpu.SMEM)
PARAMS = pltpu.CompilerParams(vmem_limit_bytes=12 * 2**20)
BLOCK = (5, PLANES, 8, 128)
BLOCK4 = (4, PLANES, 8, 128)
FLAT = (5, PLANES * 8, 128)
FLAT4 = (4, PLANES * 8, 128)
EXTENDED = (5, (PLANES + 2) * PITCH, 128)


NEAR = [(i, i ^ 1) for i in range(TILES)]
FAR = [(i, (i + 1) % TILES if i % 2 else (i - 1) % TILES) for i in range(TILES)]


def shards(state, spacing_index, strength_index, obs_offsets):
    own = state.reshape(FLAT)

    def send(x, pairs):
        return lax.ppermute(x, "run", pairs)

    p = send(own, [(0, 8)])
    a, b, e = send(own, [(0, 2)]), send(own, [(0, 6)]), send(own, [(0, 4)])
    f, g, h = send(p, [(8, 10)]), send(p, [(8, 14)]), send(p, [(8, 12)])
    y = a + b + f + g
    u = send(y, [(2, 3), (6, 7), (10, 11), (14, 15)])
    v = send(y, [(2, 1), (6, 5), (10, 9), (14, 13)])

    nat, d, near, far = pl.pallas_call(
        pack_kernel,
        out_shape=(f32(*FLAT), f32(*FLAT4), f32(EDGES, 8, 128), f32(EDGES, 8, 128)),
        in_specs=[SM, SM] + [VM] * 7,
        out_specs=(VM,) * 4,
        compiler_params=PARAMS,
        name="pack",
    )(spacing_index, obs_offsets, own, y, u, v, p, e, h)

    near = lax.ppermute(near, "tile", NEAR)
    far = lax.ppermute(far, "tile", FAR)

    own1, nat1 = pl.pallas_call(
        inner_kernel,
        out_shape=(f32(*FLAT), f32(*FLAT)),
        in_specs=[SM] + [VM] * 3,
        out_specs=(VM,) * 2,
        scratch_shapes=[pltpu.VMEM(EXTENDED, jnp.float32)] * 2,
        compiler_params=PARAMS,
        name="inner",
    )(strength_index, own, nat, d)

    own2, beyond, edge, d2, sums = pl.pallas_call(
        steps_kernel,
        out_shape=(
            f32(*FLAT), f32(5, PLANES, 128), f32(5, PLANES, 128), f32(*BLOCK4), f32(TILES, 1, 128)
        ),
        in_specs=[SM, SM, SM] + [VM] * 7,
        out_specs=(VM,) * 5,
        scratch_shapes=[*[pltpu.VMEM(EXTENDED, jnp.float32)] * 2, pltpu.VMEM(ROWS, jnp.float32)],
        compiler_params=PARAMS,
        name="steps",
    )(spacing_index, strength_index, obs_offsets, own, nat, d, own1, nat1, near, far)

    edge = lax.ppermute(edge, "tile", [(i, (i + 1) % TILES) for i in range(TILES)])
    sums = lax.all_to_all(sums, "tile", 0, 0)

    out, misfit = pl.pallas_call(
        last_kernel,
        out_shape=(f32(*BLOCK), f32(1)),
        in_specs=[SM] + [VM] * 5,
        out_specs=(VM, SM),
        scratch_shapes=[pltpu.VMEM(EXTENDED, jnp.float32)],
        compiler_params=PARAMS,
        name="last",
    )(strength_index, own2, beyond, edge, d2, sums)
    return out[None], misfit


def solution(mesh):
    placed = (P("run", None, None, "tile", None), P("run"), P("run"), P())
    return jax.shard_map(
        shards,
        mesh=mesh,
        in_specs=placed,
        out_specs=(P("run", None, None, "tile", None), P("run")),
        check_vma=False,
    )
```

time: 58.2 us -> 56.6 us (0.973)
  the two profiles are of different devices: /device:TPU:105 before, /device:TPU:89 now
where the time goes in v5:
time: 56.6 us; the launch traced here: 56.2 us
  starting transfers between devices  36.5 us (64%)
  waiting for transfers between devices  13.2 us (23%)
  Pallas kernels  4.16 us (7%)
  between operations  2.15 us (4%)
    ppermute x1, starting transfers between devices, shards(): far = lax.ppermute(far, 'tile', FAR)  10.3 us
    ppermute x9, waiting for transfers between devices, send(): return lax.ppermute(x, 'run', pairs)  8.36 us
    ppermute x1, starting transfers between devices, shards(): near = lax.ppermute(near, 'tile', NEAR)  8.07 us
    all_to_all x1, starting transfers between devices, shards(): sums = lax.all_to_all(sums, 'tile', 0, 0)  6.94 us
    ppermute x9, starting transfers between devices, send(): return lax.ppermute(x, 'run', pairs)  6.79 us
    ppermute x1, starting transfers between devices, shards(): lax.ppermute(edge, 'tile', [(i, (i + 1) % TILES) for i in range(TILES)])  4.44 us
    all_to_all x1, waiting for transfers between devices, shards(): sums = lax.all_to_all(sums, 'tile', 0, 0)  3.96 us
    pallas_call x1, Pallas kernels, shards(): pl.pallas_call(steps_kernel, out_shape=(f32(*FLAT), f32(5, PLANES, 128),...  2.13 us
  transfers between devices with their start and end apart: 13, of which 3 were waited for; matrix products, arithmetic and copies ran while one was open for 0% of the time, Pallas kernels for 1%

profile of v5, /device:TPU:89, one launch (start us, length us, event | category | flops | bytes accessed | tf_op | source)
XLA Modules:
  0.0 56.2 jit_solution(4588977548673274942)
XLA Ops:
  0.6 0.0 copy-start.1
  0.6 0.0 copy-start
  0.6 0.8 %collective-permute-start.2 = (f32[5,64,128]{2,1,0:T(8,128)}, f32[5,64,128]{2,1,0:T(8,128)S(1)}, u32[]{:S(2)}, u32[]{:S(2)}) collective-permute-start(f32[5,64,128]{2,1,0:T(8,128)} %bitcast.2), channel_id=1, source_target_pairs={{0,256},{1,257},{2,258},{3,259},{4,260},{5,261},{6,262},{7,263},{8... | collective-permute-start | bytes 491528 | tf_op jit(solution)/shard_map/ppermute | solution.py:320
  1.5 0.7 %collective-permute-start = (f32[5,64,128]{2,1,0:T(8,128)}, f32[5,64,128]{2,1,0:T(8,128)S(1)}, u32[]{:S(2)}, u32[]{:S(2)}) collective-permute-start(f32[5,64,128]{2,1,0:T(8,128)} %bitcast.3), channel_id=1, source_target_pairs={{0,64},{1,65},{2,66},{3,67},{4,68},{5,69},{6,70},{7,71},{8,72},{9,... | collective-permute-start | bytes 491528 | tf_op jit(solution)/shard_map/ppermute | solution.py:320
  2.1 0.7 %collective-permute-start.1 = (f32[5,64,128]{2,1,0:T(8,128)}, f32[5,64,128]{2,1,0:T(8,128)S(1)}, u32[]{:S(2)}, u32[]{:S(2)}) collective-permute-start(f32[5,64,128]{2,1,0:T(8,128)} %bitcast.4), channel_id=1, source_target_pairs={{0,192},{1,193},{2,194},{3,195},{4,196},{5,197},{6,198},{7,199},{8... | collective-permute-start | bytes 491528 | tf_op jit(solution)/shard_map/ppermute | solution.py:320
  2.8 0.0 collective-permute-done.2.p_ref
  2.8 0.7 %collective-permute-start.3 = (f32[5,64,128]{2,1,0:T(8,128)S(1)}, f32[5,64,128]{2,1,0:T(8,128)S(1)}, u32[]{:S(2)}, u32[]{:S(2)}) collective-permute-start(f32[5,64,128]{2,1,0:T(8,128)S(1)} %collective-permute-done.2.p_ref), channel_id=1, source_target_pairs={{256,320},{257,321},{258,322},{259,323},{260,324},{261,325},{262,3... | collective-permute-start | bytes 491528 | tf_op jit(solution)/shard_map/ppermute | solution.py:320
  3.5 0.7 %collective-permute-start.4 = (f32[5,64,128]{2,1,0:T(8,128)S(1)}, f32[5,64,128]{2,1,0:T(8,128)S(1)}, u32[]{:S(2)}, u32[]{:S(2)}) collective-permute-start(f32[5,64,128]{2,1,0:T(8,128)S(1)} %collective-permute-done.2.p_ref), channel_id=1, source_target_pairs={{256,448},{257,449},{258,450},{259,451},{260,452},{261,453},{262,4... | collective-permute-start | bytes 491528 | tf_op jit(solution)/shard_map/ppermute | solution.py:320
  4.2 0.7 %collective-permute-start.7 = (f32[5,64,128]{2,1,0:T(8,128)}, f32[5,64,128]{2,1,0:T(8,128)S(1)}, u32[]{:S(2)}, u32[]{:S(2)}) collective-permute-start(f32[5,64,128]{2,1,0:T(8,128)} %bitcast.5), channel_id=1, source_target_pairs={{0,128},{1,129},{2,130},{3,131},{4,132},{5,133},{6,134},{7,135},{8... | collective-permute-start | bytes 491528 | tf_op jit(solution)/shard_map/ppermute | solution.py:320
  4.9 0.0 collective-permute-done
  4.9 0.7 %collective-permute-start.8 = (f32[5,64,128]{2,1,0:T(8,128)S(1)}, f32[5,64,128]{2,1,0:T(8,128)S(1)}, u32[]{:S(2)}, u32[]{:S(2)}) collective-permute-start(f32[5,64,128]{2,1,0:T(8,128)S(1)} %collective-permute-done.2.p_ref), channel_id=1, source_target_pairs={{256,384},{257,385},{258,386},{259,387},{260,388},{261,389},{262,3... | collective-permute-start | bytes 491528 | tf_op jit(solution)/shard_map/ppermute | solution.py:320
  5.6 0.0 collective-permute-done.1
  5.6 0.0 collective-permute-done.3
  5.6 0.0 collective-permute-done.4
  5.6 1.3 %collective-permute-start.5 = (f32[5,64,128]{2,1,0:T(8,128)S(1)}, f32[5,64,128]{2,1,0:T(8,128)S(1)}, u32[]{:S(2)}, u32[]{:S(2)}) collective-permute-start(f32[5,64,128]{2,1,0:T(8,128)S(1)} %add_add_fusion.y_ref), channel_id=1, source_target_pairs={{64,96},{192,224},{320,352},{448,480},{65,97},{193,225},{321,353},... | collective-permute-start | bytes 491528 | tf_op jit(solution)/shard_map/ppermute | solution.py:320
  6.9 0.7 %collective-permute-start.6 = (f32[5,64,128]{2,1,0:T(8,128)S(1)}, f32[5,64,128]{2,1,0:T(8,128)S(1)}, u32[]{:S(2)}, u32[]{:S(2)}) collective-permute-start(f32[5,64,128]{2,1,0:T(8,128)S(1)} %add_add_fusion.y_ref), channel_id=1, source_target_pairs={{64,32},{192,160},{320,288},{448,416},{65,33},{193,161},{321,289},... | collective-permute-start | bytes 491528 | tf_op jit(solution)/shard_map/ppermute | solution.py:320
  7.6 0.0 copy-done.1
  7.6 0.1 copy.7.off_ref
  8.4 0.0 collective-permute-done.7.e_ref
  8.4 0.0 collective-permute-done.8.h_ref
  8.4 8.3 %collective-permute-done.5.u_ref = f32[5,64,128]{2,1,0:T(8,128)S(1)} collective-permute-done((f32[5,64,128]{2,1,0:T(8,128)S(1)}, f32[5,64,128]{2,1,0:T(8,128)S(1)}, u32[]{:S(2)}, u32[]{:S(2)}) %collective-permute-start.5) | collective-permute-done | bytes 163872 | tf_op jit(solution)/shard_map/ppermute | solution.py:320
  16.7 0.0 collective-permute-done.6.v_ref
  16.7 0.0 copy-done
  16.7 0.8 %pack.1 = (f32[5,64,128]{2,1,0:T(8,128)S(1)}, f32[4,64,128]{2,1,0:T(8,128)S(1)}, f32[30,8,128]{2,1,0:T(8,128)S(1)}, f32[30,8,128]{2,1,0:T(8,128)S(1)}) custom-call(s32[1]{0:T(128)S(6)} %copy.8.sp_ref, s32[8,2]{1,0:T(8,128)S(1)} %copy.7.off_ref, f32[5,64,128]{2,1,0:T(8,128)S(1)} %bitcast.6, f32[5,64,128]{2,1,0:T(8,128)S(1)} %add_add_fusion.y_ref, ...), custom_call_target="tpu_custom_call" | custom-call | tf_op jit(solution)/shard_map/pack/pallas_call | solution.py:329
  17.5 10.3 %collective-permute-start.10 = (f32[30,8,128]{2,1,0:T(8,128)S(1)}, f32[30,8,128]{2,1,0:T(8,128)S(1)}, u32[]{:S(2)}, u32[]{:S(2)}) collective-permute-start(f32[30,8,128]{2,1,0:T(8,128)S(1)} %get-tuple-element.20), channel_id=1, source_target_pairs={{0,31},{1,2},{2,1},{3,4},{4,3},{5,6},{6,5},{7,8},{8,7},{9,10},{10,... | collective-permute-start | bytes 368648 | tf_op jit(solution)/shard_map/ppermute | solution.py:339
  27.8 8.1 %collective-permute-start.9 = (f32[30,8,128]{2,1,0:T(8,128)S(1)}, f32[30,8,128]{2,1,0:T(8,128)S(1)}, u32[]{:S(2)}, u32[]{:S(2)}) collective-permute-start(f32[30,8,128]{2,1,0:T(8,128)S(1)} %get-tuple-element.19), channel_id=1, source_target_pairs={{0,1},{1,0},{2,3},{3,2},{4,5},{5,4},{6,7},{7,6},{8,9},{9,8},{10,11... | collective-permute-start | bytes 368648 | tf_op jit(solution)/shard_map/ppermute | solution.py:338
  36.5 0.4 inner.1
  36.9 0.0 collective-permute-done.10.far_ref
  36.9 0.0 collective-permute-done.9.near_ref
  36.9 2.1 %steps.1 = (f32[5,64,128]{2,1,0:T(8,128)S(1)}, f32[5,8,128]{2,1,0:T(8,128)S(1)}, f32[5,8,128]{2,1,0:T(8,128)S(1)}, f32[4,8,8,128]{3,2,1,0:T(8,128)S(1)}, f32[32,1,128]{2,1,0:T(1,128)}) custom-call(s32[1]{0:T(128)S(6)} %copy.8.sp_ref, s32[1]{0:T(128)S(6)} %copy.9.st_ref, s32[8,2]{1,0:T(8,128)S(1)} %copy.7.off_ref, f32[5,64,128]{2,1,0:T(8,128)S(1)} %bitcast.8, ...), custom_call_target="tpu_custom_call" | custom-call | tf_op jit(solution)/shard_map/steps/pallas_call | solution.py:351
  39.1 6.9 %all-to-all-start = ((f32[32,1,128]{2,1,0:T(1,128)}), f32[32,1,128]{2,1,0:T(1,128)S(1)}, u32[]{:S(2)}, u32[]{:S(2)}) async-start(f32[32,1,128]{2,1,0:T(1,128)} %get-tuple-element.25), calls=%async_computation | async-start | bytes 32768 | tf_op jit(solution)/shard_map/all_to_all | solution.py:364
  46.0 4.4 %collective-permute-start.11 = (f32[5,8,128]{2,1,0:T(8,128)S(1)}, f32[5,8,128]{2,1,0:T(8,128)S(1)}, u32[]{:S(2)}, u32[]{:S(2)}) collective-permute-start(f32[5,8,128]{2,1,0:T(8,128)S(1)} %get-tuple-element.23), channel_id=1, source_target_pairs={{0,1},{1,2},{2,3},{3,4},{4,5},{5,6},{6,7},{7,8},{8,9},{9,10},{10,1... | collective-permute-start | bytes 61448 | tf_op jit(solution)/shard_map/ppermute | solution.py:363
  50.5 0.9 %collective-permute-done.11.edge_ref = f32[5,8,128]{2,1,0:T(8,128)S(1)} collective-permute-done((f32[5,8,128]{2,1,0:T(8,128)S(1)}, f32[5,8,128]{2,1,0:T(8,128)S(1)}, u32[]{:S(2)}, u32[]{:S(2)}) %collective-permute-start.11) | collective-permute-done | bytes 20512 | tf_op jit(solution)/shard_map/ppermute | solution.py:363
  51.4 4.0 %all-to-all-done.sums_ref = f32[32,1,128]{2,1,0:T(1,128)S(1)} async-done(((f32[32,1,128]{2,1,0:T(1,128)}), f32[32,1,128]{2,1,0:T(1,128)S(1)}, u32[]{:S(2)}, u32[]{:S(2)}) %all-to-all-start) | async-done | bytes 16416 | tf_op jit(solution)/shard_map/all_to_all | solution.py:364
  55.3 0.9 %last.1 = (f32[5,8,8,128]{3,2,1,0:T(8,128)}, f32[1]{0:T(128)}) custom-call(s32[1]{0:T(128)S(6)} %copy.9.st_ref, f32[5,64,128]{2,1,0:T(8,128)S(1)} %get-tuple-element.21.own_ref, f32[5,8,128]{2,1,0:T(8,128)S(1)} %get-tuple-element.22.beyond_ref, f32[5,8,128]{2,1,0:T(8,128)S(1)} %collective-permute-done.11.edge_ref, ...), custom_call_target="tpu_custom_call" | custom-call | tf_op jit(solution)/shard_map/last/pallas_call | solution.py:366
  (1 shorter events, 0.0 us)
Async XLA Ops:
  0.6 7.0 %copy-start.1 = (s32[8,2]{0,1:T(2,128)S(1)}, s32[8,2]{0,1:T(2,128)}, u32[]{:S(2)}) copy-start(s32[8,2]{0,1:T(2,128)} %param.7) | copy-start | bytes 196
  0.6 16.1 %copy-start = (f32[1,5,8,8,128]{4,3,2,1,0:T(8,128)S(1)}, f32[1,5,8,8,128]{4,3,2,1,0:T(8,128)}, u32[]{:S(2)}) copy-start(f32[1,5,8,8,128]{4,3,2,1,0:T(8,128)} %param.4) | copy-start | bytes 491524
  0.6 2.2 %collective-permute-start.2 = (f32[5,64,128]{2,1,0:T(8,128)}, f32[5,64,128]{2,1,0:T(8,128)S(1)}, u32[]{:S(2)}, u32[]{:S(2)}) collective-permute-start(f32[5,64,128]{2,1,0:T(8,128)} %bitcast.2), channel_id=1, source_target_pairs={{0,256},{1,257},{2,258},{3,259},{4,260},{5,261},{6,262},{7,263},{8... | collective-permute-start | bytes 491528 | tf_op jit(solution)/shard_map/ppermute | solution.py:320
  1.5 3.4 %collective-permute-start = (f32[5,64,128]{2,1,0:T(8,128)}, f32[5,64,128]{2,1,0:T(8,128)S(1)}, u32[]{:S(2)}, u32[]{:S(2)}) collective-permute-start(f32[5,64,128]{2,1,0:T(8,128)} %bitcast.3), channel_id=1, source_target_pairs={{0,64},{1,65},{2,66},{3,67},{4,68},{5,69},{6,70},{7,71},{8,72},{9,... | collective-permute-start | bytes 491528 | tf_op jit(solution)/shard_map/ppermute | solution.py:320
  2.1 3.4 %collective-permute-start.1 = (f32[5,64,128]{2,1,0:T(8,128)}, f32[5,64,128]{2,1,0:T(8,128)S(1)}, u32[]{:S(2)}, u32[]{:S(2)}) collective-permute-start(f32[5,64,128]{2,1,0:T(8,128)} %bitcast.4), channel_id=1, source_target_pairs={{0,192},{1,193},{2,194},{3,195},{4,196},{5,197},{6,198},{7,199},{8... | collective-permute-start | bytes 491528 | tf_op jit(solution)/shard_map/ppermute | solution.py:320
  2.8 2.7 %collective-permute-start.3 = (f32[5,64,128]{2,1,0:T(8,128)S(1)}, f32[5,64,128]{2,1,0:T(8,128)S(1)}, u32[]{:S(2)}, u32[]{:S(2)}) collective-permute-start(f32[5,64,128]{2,1,0:T(8,128)S(1)} %collective-permute-done.2.p_ref), channel_id=1, source_target_pairs={{256,320},{257,321},{258,322},{259,323},{260,324},{261,325},{262,3... | collective-permute-start | bytes 491528 | tf_op jit(solution)/shard_map/ppermute | solution.py:320
  3.5 2.1 %collective-permute-start.4 = (f32[5,64,128]{2,1,0:T(8,128)S(1)}, f32[5,64,128]{2,1,0:T(8,128)S(1)}, u32[]{:S(2)}, u32[]{:S(2)}) collective-permute-start(f32[5,64,128]{2,1,0:T(8,128)S(1)} %collective-permute-done.2.p_ref), channel_id=1, source_target_pairs={{256,448},{257,449},{258,450},{259,451},{260,452},{261,453},{262,4... | collective-permute-start | bytes 491528 | tf_op jit(solution)/shard_map/ppermute | solution.py:320
  4.2 4.2 %collective-permute-start.7 = (f32[5,64,128]{2,1,0:T(8,128)}, f32[5,64,128]{2,1,0:T(8,128)S(1)}, u32[]{:S(2)}, u32[]{:S(2)}) collective-permute-start(f32[5,64,128]{2,1,0:T(8,128)} %bitcast.5), channel_id=1, source_target_pairs={{0,128},{1,129},{2,130},{3,131},{4,132},{5,133},{6,134},{7,135},{8... | collective-permute-start | bytes 491528 | tf_op jit(solution)/shard_map/ppermute | solution.py:320
  4.9 3.5 %collective-permute-start.8 = (f32[5,64,128]{2,1,0:T(8,128)S(1)}, f32[5,64,128]{2,1,0:T(8,128)S(1)}, u32[]{:S(2)}, u32[]{:S(2)}) collective-permute-start(f32[5,64,128]{2,1,0:T(8,128)S(1)} %collective-permute-done.2.p_ref), channel_id=1, source_target_pairs={{256,384},{257,385},{258,386},{259,387},{260,388},{261,389},{262,3... | collective-permute-start | bytes 491528 | tf_op jit(solution)/shard_map/ppermute | solution.py:320
  5.6 11.1 %collective-permute-start.5 = (f32[5,64,128]{2,1,0:T(8,128)S(1)}, f32[5,64,128]{2,1,0:T(8,128)S(1)}, u32[]{:S(2)}, u32[]{:S(2)}) collective-permute-start(f32[5,64,128]{2,1,0:T(8,128)S(1)} %add_add_fusion.y_ref), channel_id=1, source_target_pairs={{64,96},{192,224},{320,352},{448,480},{65,97},{193,225},{321,353},... | collective-permute-start | bytes 491528 | tf_op jit(solution)/shard_map/ppermute | solution.py:320
  6.9 9.8 %collective-permute-start.6 = (f32[5,64,128]{2,1,0:T(8,128)S(1)}, f32[5,64,128]{2,1,0:T(8,128)S(1)}, u32[]{:S(2)}, u32[]{:S(2)}) collective-permute-start(f32[5,64,128]{2,1,0:T(8,128)S(1)} %add_add_fusion.y_ref), channel_id=1, source_target_pairs={{64,32},{192,160},{320,288},{448,416},{65,33},{193,161},{321,289},... | collective-permute-start | bytes 491528 | tf_op jit(solution)/shard_map/ppermute | solution.py:320
  17.5 19.4 %collective-permute-start.10 = (f32[30,8,128]{2,1,0:T(8,128)S(1)}, f32[30,8,128]{2,1,0:T(8,128)S(1)}, u32[]{:S(2)}, u32[]{:S(2)}) collective-permute-start(f32[30,8,128]{2,1,0:T(8,128)S(1)} %get-tuple-element.20), channel_id=1, source_target_pairs={{0,31},{1,2},{2,1},{3,4},{4,3},{5,6},{6,5},{7,8},{8,7},{9,10},{10,... | collective-permute-start | bytes 368648 | tf_op jit(solution)/shard_map/ppermute | solution.py:339
  27.8 9.1 %collective-permute-start.9 = (f32[30,8,128]{2,1,0:T(8,128)S(1)}, f32[30,8,128]{2,1,0:T(8,128)S(1)}, u32[]{:S(2)}, u32[]{:S(2)}) collective-permute-start(f32[30,8,128]{2,1,0:T(8,128)S(1)} %get-tuple-element.19), channel_id=1, source_target_pairs={{0,1},{1,0},{2,3},{3,2},{4,5},{5,4},{6,7},{7,6},{8,9},{9,8},{10,11... | collective-permute-start | bytes 368648 | tf_op jit(solution)/shard_map/ppermute | solution.py:338
  39.1 16.2 %all-to-all-start = ((f32[32,1,128]{2,1,0:T(1,128)}), f32[32,1,128]{2,1,0:T(1,128)S(1)}, u32[]{:S(2)}, u32[]{:S(2)}) async-start(f32[32,1,128]{2,1,0:T(1,128)} %get-tuple-element.25), calls=%async_computation | async-start | bytes 32768 | tf_op jit(solution)/shard_map/all_to_all | solution.py:364
  46.0 5.3 %collective-permute-start.11 = (f32[5,8,128]{2,1,0:T(8,128)S(1)}, f32[5,8,128]{2,1,0:T(8,128)S(1)}, u32[]{:S(2)}, u32[]{:S(2)}) collective-permute-start(f32[5,8,128]{2,1,0:T(8,128)S(1)} %get-tuple-element.23), channel_id=1, source_target_pairs={{0,1},{1,2},{2,3},{3,4},{4,5},{5,6},{6,7},{7,8},{8,9},{9,10},{10,1... | collective-permute-start | bytes 61448 | tf_op jit(solution)/shard_map/ppermute | solution.py:363

commit v6 on v5

--- a/solution.py
+++ b/solution.py
@@ -166,7 +166,7 @@
 
 
 def pack_kernel(
-    sp_ref, off_ref, own_ref, y_ref, u_ref, v_ref, p_ref, e_ref, h_ref, nat_ref, d_ref, near_ref, far_ref
+    sp_ref, off_ref, own_ref, y_ref, u_ref, v_ref, w_ref, p_ref, nat_ref, d_ref, near_ref, far_ref
 ):
     spread = Spread(sp_ref, off_ref)
     even = even_tile()
@@ -176,7 +176,7 @@
         here = pl.ds(8 * z, 8)
         for c in range(5):
             own = own_ref[c, here]
-            nat = (y_ref[c, here] + u_ref[c, here] + v_ref[c, here]) + (p_ref[c, here] + e_ref[c, here] + h_ref[c, here])
+            nat = (y_ref[c, here] + u_ref[c, here]) + (v_ref[c, here] + w_ref[c, here]) + p_ref[c, here]
             nat = jnp.where(root, own, nat)
             nat_ref[c, here] = nat
             if c > 0:
@@ -208,7 +208,7 @@
 
 
 def steps_kernel(
-    sp_ref, st_ref, off_ref, own_ref, nat_ref, d_ref, own1_ref, nat1_ref, near_ref, far_ref,
+    sp_ref, st_ref, off_ref, own_ref, nat_ref, d_ref, own1_ref, nat1_ref, far_ref, near_ref,
     own2_ref, beyond_ref, edge_ref, d2_ref, sum_ref, a1_ref, b1_ref, total_ref,
 ):
     spread = Spread(sp_ref, off_ref)
@@ -320,20 +320,21 @@
         return lax.ppermute(x, "run", pairs)
 
     p = send(own, [(0, 8)])
-    a, b, e = send(own, [(0, 2)]), send(own, [(0, 6)]), send(own, [(0, 4)])
-    f, g, h = send(p, [(8, 10)]), send(p, [(8, 14)]), send(p, [(8, 12)])
+    a, b = send(own, [(0, 2)]), send(own, [(0, 6)])
+    f, g = send(p, [(8, 10)]), send(p, [(8, 14)])
     y = a + b + f + g
     u = send(y, [(2, 3), (6, 7), (10, 11), (14, 15)])
     v = send(y, [(2, 1), (6, 5), (10, 9), (14, 13)])
+    w = send(y, [(2, 4), (10, 12)])
 
     nat, d, near, far = pl.pallas_call(
         pack_kernel,
         out_shape=(f32(*FLAT), f32(*FLAT4), f32(EDGES, 8, 128), f32(EDGES, 8, 128)),
-        in_specs=[SM, SM] + [VM] * 7,
+        in_specs=[SM, SM] + [VM] * 6,
         out_specs=(VM,) * 4,
         compiler_params=PARAMS,
         name="pack",
-    )(spacing_index, obs_offsets, own, y, u, v, p, e, h)
+    )(spacing_index, obs_offsets, own, y, u, v, w, p)
 
     near = lax.ppermute(near, "tile", NEAR)
     far = lax.ppermute(far, "tile", FAR)
@@ -358,7 +359,7 @@
         scratch_shapes=[*[pltpu.VMEM(EXTENDED, jnp.float32)] * 2, pltpu.VMEM(ROWS, jnp.float32)],
         compiler_params=PARAMS,
         name="steps",
-    )(spacing_index, strength_index, obs_offsets, own, nat, d, own1, nat1, near, far)
+    )(spacing_index, strength_index, obs_offsets, own, nat, d, own1, nat1, far, near)
 
     edge = lax.ppermute(edge, "tile", [(i, (i + 1) % TILES) for i in range(TILES)])
     sums = lax.all_to_all(sums, "tile", 0, 0)

time: 56.6 us -> 56.6 us (level)
  the two profiles are of different devices: /device:TPU:89 before, /device:TPU:97 now
where the time goes in v6:
time: 56.6 us; the launch traced here: 56.2 us
  starting transfers between devices  34.9 us (62%)
  waiting for transfers between devices  15 us (27%)
  Pallas kernels  4.15 us (7%)
  between operations  2.14 us (4%)
    ppermute x1, starting transfers between devices, shards(): far = lax.ppermute(far, 'tile', FAR)  10.8 us
    ppermute x8, waiting for transfers between devices, send(): return lax.ppermute(x, 'run', pairs)  10.1 us
    all_to_all x1, starting transfers between devices, shards(): sums = lax.all_to_all(sums, 'tile', 0, 0)  7.42 us
    ppermute x8, starting transfers between devices, send(): return lax.ppermute(x, 'run', pairs)  6.12 us
    ppermute x1, starting transfers between devices, shards(): near = lax.ppermute(near, 'tile', NEAR)  6.11 us
    ppermute x1, starting transfers between devices, shards(): lax.ppermute(edge, 'tile', [(i, (i + 1) % TILES) for i in range(TILES)])  4.44 us
    all_to_all x1, waiting for transfers between devices, shards(): sums = lax.all_to_all(sums, 'tile', 0, 0)  3.96 us
    pallas_call x1, Pallas kernels, shards(): pl.pallas_call(steps_kernel, out_shape=(f32(*FLAT), f32(5, PLANES, 128),...  2.13 us
  transfers between devices with their start and end apart: 12, of which 3 were waited for; matrix products, arithmetic and copies ran while one was open for 0% of the time, Pallas kernels for 1%

profile of v6, /device:TPU:97, one launch (start us, length us, event | category | flops | bytes accessed | tf_op | source)
XLA Modules:
  0.0 56.2 jit_solution(11155409501276317341)
XLA Ops:
  0.6 0.0 copy-start.1
  0.6 0.0 copy-start
  0.6 0.8 %collective-permute-start.2 = (f32[5,64,128]{2,1,0:T(8,128)}, f32[5,64,128]{2,1,0:T(8,128)S(1)}, u32[]{:S(2)}, u32[]{:S(2)}) collective-permute-start(f32[5,64,128]{2,1,0:T(8,128)} %bitcast.2), channel_id=1, source_target_pairs={{0,256},{1,257},{2,258},{3,259},{4,260},{5,261},{6,262},{7,263},{8... | collective-permute-start | bytes 491528 | tf_op jit(solution)/shard_map/ppermute | solution.py:320
  1.5 0.7 %collective-permute-start = (f32[5,64,128]{2,1,0:T(8,128)}, f32[5,64,128]{2,1,0:T(8,128)S(1)}, u32[]{:S(2)}, u32[]{:S(2)}) collective-permute-start(f32[5,64,128]{2,1,0:T(8,128)} %bitcast.3), channel_id=1, source_target_pairs={{0,64},{1,65},{2,66},{3,67},{4,68},{5,69},{6,70},{7,71},{8,72},{9,... | collective-permute-start | bytes 491528 | tf_op jit(solution)/shard_map/ppermute | solution.py:320
  2.1 0.7 %collective-permute-start.1 = (f32[5,64,128]{2,1,0:T(8,128)}, f32[5,64,128]{2,1,0:T(8,128)S(1)}, u32[]{:S(2)}, u32[]{:S(2)}) collective-permute-start(f32[5,64,128]{2,1,0:T(8,128)} %bitcast.4), channel_id=1, source_target_pairs={{0,192},{1,193},{2,194},{3,195},{4,196},{5,197},{6,198},{7,199},{8... | collective-permute-start | bytes 491528 | tf_op jit(solution)/shard_map/ppermute | solution.py:320
  2.8 0.0 collective-permute-done.2.p_ref
  2.8 0.7 %collective-permute-start.3 = (f32[5,64,128]{2,1,0:T(8,128)S(1)}, f32[5,64,128]{2,1,0:T(8,128)S(1)}, u32[]{:S(2)}, u32[]{:S(2)}) collective-permute-start(f32[5,64,128]{2,1,0:T(8,128)S(1)} %collective-permute-done.2.p_ref), channel_id=1, source_target_pairs={{256,320},{257,321},{258,322},{259,323},{260,324},{261,325},{262,3... | collective-permute-start | bytes 491528 | tf_op jit(solution)/shard_map/ppermute | solution.py:320
  3.5 0.7 %collective-permute-start.4 = (f32[5,64,128]{2,1,0:T(8,128)S(1)}, f32[5,64,128]{2,1,0:T(8,128)S(1)}, u32[]{:S(2)}, u32[]{:S(2)}) collective-permute-start(f32[5,64,128]{2,1,0:T(8,128)S(1)} %collective-permute-done.2.p_ref), channel_id=1, source_target_pairs={{256,448},{257,449},{258,450},{259,451},{260,452},{261,453},{262,4... | collective-permute-start | bytes 491528 | tf_op jit(solution)/shard_map/ppermute | solution.py:320
  4.2 0.0 collective-permute-done
  4.2 0.0 collective-permute-done.1
  4.2 0.0 collective-permute-done.3
  4.2 0.0 collective-permute-done.4
  4.3 0.7 %collective-permute-start.5 = (f32[5,64,128]{2,1,0:T(8,128)S(1)}, f32[5,64,128]{2,1,0:T(8,128)S(1)}, u32[]{:S(2)}, u32[]{:S(2)}) collective-permute-start(f32[5,64,128]{2,1,0:T(8,128)S(1)} %add_add_fusion.y_ref), channel_id=1, source_target_pairs={{64,96},{192,224},{320,352},{448,480},{65,97},{193,225},{321,353},... | collective-permute-start | bytes 491528 | tf_op jit(solution)/shard_map/ppermute | solution.py:320
  5.0 0.7 %collective-permute-start.6 = (f32[5,64,128]{2,1,0:T(8,128)S(1)}, f32[5,64,128]{2,1,0:T(8,128)S(1)}, u32[]{:S(2)}, u32[]{:S(2)}) collective-permute-start(f32[5,64,128]{2,1,0:T(8,128)S(1)} %add_add_fusion.y_ref), channel_id=1, source_target_pairs={{64,32},{192,160},{320,288},{448,416},{65,33},{193,161},{321,289},... | collective-permute-start | bytes 491528 | tf_op jit(solution)/shard_map/ppermute | solution.py:320
  5.6 1.3 %collective-permute-start.7 = (f32[5,64,128]{2,1,0:T(8,128)S(1)}, f32[5,64,128]{2,1,0:T(8,128)S(1)}, u32[]{:S(2)}, u32[]{:S(2)}) collective-permute-start(f32[5,64,128]{2,1,0:T(8,128)S(1)} %add_add_fusion.y_ref), channel_id=1, source_target_pairs={{64,128},{320,384},{65,129},{321,385},{66,130},{322,386},{67,131},... | collective-permute-start | bytes 491528 | tf_op jit(solution)/shard_map/ppermute | solution.py:320
  6.9 0.0 copy-done.1
  6.9 0.1 copy.7.off_ref
  7.7 0.0 collective-permute-done.5.u_ref
  7.7 0.0 collective-permute-done.6.v_ref
  7.7 10.1 %collective-permute-done.7.w_ref = f32[5,64,128]{2,1,0:T(8,128)S(1)} collective-permute-done((f32[5,64,128]{2,1,0:T(8,128)S(1)}, f32[5,64,128]{2,1,0:T(8,128)S(1)}, u32[]{:S(2)}, u32[]{:S(2)}) %collective-permute-start.7) | collective-permute-done | bytes 163872 | tf_op jit(solution)/shard_map/ppermute | solution.py:320
  17.8 0.0 copy-done
  17.8 0.8 %pack.1 = (f32[5,64,128]{2,1,0:T(8,128)S(1)}, f32[4,64,128]{2,1,0:T(8,128)S(1)}, f32[30,8,128]{2,1,0:T(8,128)S(1)}, f32[30,8,128]{2,1,0:T(8,128)S(1)}) custom-call(s32[1]{0:T(128)S(6)} %copy.8.sp_ref, s32[8,2]{1,0:T(8,128)S(1)} %copy.7.off_ref, f32[5,64,128]{2,1,0:T(8,128)S(1)} %bitcast.5, f32[5,64,128]{2,1,0:T(8,128)S(1)} %add_add_fusion.y_ref, ...), custom_call_target="tpu_custom_call" | custom-call | tf_op jit(solution)/shard_map/pack/pallas_call | solution.py:330
  18.5 10.8 %collective-permute-start.8 = (f32[30,8,128]{2,1,0:T(8,128)S(1)}, f32[30,8,128]{2,1,0:T(8,128)S(1)}, u32[]{:S(2)}, u32[]{:S(2)}) collective-permute-start(f32[30,8,128]{2,1,0:T(8,128)S(1)} %get-tuple-element.19), channel_id=1, source_target_pairs={{0,31},{1,2},{2,1},{3,4},{4,3},{5,6},{6,5},{7,8},{8,7},{9,10},{10,... | collective-permute-start | bytes 368648 | tf_op jit(solution)/shard_map/ppermute | solution.py:340
  29.3 6.1 %collective-permute-start.9 = (f32[30,8,128]{2,1,0:T(8,128)S(1)}, f32[30,8,128]{2,1,0:T(8,128)S(1)}, u32[]{:S(2)}, u32[]{:S(2)}) collective-permute-start(f32[30,8,128]{2,1,0:T(8,128)S(1)} %get-tuple-element.20), channel_id=1, source_target_pairs={{0,1},{1,0},{2,3},{3,2},{4,5},{5,4},{6,7},{7,6},{8,9},{9,8},{10,11... | collective-permute-start | bytes 368648 | tf_op jit(solution)/shard_map/ppermute | solution.py:339
  36.1 0.4 inner.1
  36.5 0.0 collective-permute-done.8.far_ref
  36.5 0.0 collective-permute-done.9.near_ref
  36.5 2.1 %steps.1 = (f32[5,64,128]{2,1,0:T(8,128)S(1)}, f32[5,8,128]{2,1,0:T(8,128)S(1)}, f32[5,8,128]{2,1,0:T(8,128)S(1)}, f32[4,8,8,128]{3,2,1,0:T(8,128)S(1)}, f32[32,1,128]{2,1,0:T(1,128)}) custom-call(s32[1]{0:T(128)S(6)} %copy.8.sp_ref, s32[1]{0:T(128)S(6)} %copy.9.st_ref, s32[8,2]{1,0:T(8,128)S(1)} %copy.7.off_ref, f32[5,64,128]{2,1,0:T(8,128)S(1)} %bitcast.7, ...), custom_call_target="tpu_custom_call" | custom-call | tf_op jit(solution)/shard_map/steps/pallas_call | solution.py:352
  38.6 7.4 %all-to-all-start = ((f32[32,1,128]{2,1,0:T(1,128)}), f32[32,1,128]{2,1,0:T(1,128)S(1)}, u32[]{:S(2)}, u32[]{:S(2)}) async-start(f32[32,1,128]{2,1,0:T(1,128)} %get-tuple-element.25), calls=%async_computation | async-start | bytes 32768 | tf_op jit(solution)/shard_map/all_to_all | solution.py:365
  46.1 4.4 %collective-permute-start.10 = (f32[5,8,128]{2,1,0:T(8,128)S(1)}, f32[5,8,128]{2,1,0:T(8,128)S(1)}, u32[]{:S(2)}, u32[]{:S(2)}) collective-permute-start(f32[5,8,128]{2,1,0:T(8,128)S(1)} %get-tuple-element.23), channel_id=1, source_target_pairs={{0,1},{1,2},{2,3},{3,4},{4,5},{5,6},{6,7},{7,8},{8,9},{9,10},{10,1... | collective-permute-start | bytes 61448 | tf_op jit(solution)/shard_map/ppermute | solution.py:364
  50.5 0.9 %collective-permute-done.10.edge_ref = f32[5,8,128]{2,1,0:T(8,128)S(1)} collective-permute-done((f32[5,8,128]{2,1,0:T(8,128)S(1)}, f32[5,8,128]{2,1,0:T(8,128)S(1)}, u32[]{:S(2)}, u32[]{:S(2)}) %collective-permute-start.10) | collective-permute-done | bytes 20512 | tf_op jit(solution)/shard_map/ppermute | solution.py:364
  51.4 4.0 %all-to-all-done.sums_ref = f32[32,1,128]{2,1,0:T(1,128)S(1)} async-done(((f32[32,1,128]{2,1,0:T(1,128)}), f32[32,1,128]{2,1,0:T(1,128)S(1)}, u32[]{:S(2)}, u32[]{:S(2)}) %all-to-all-start) | async-done | bytes 16416 | tf_op jit(solution)/shard_map/all_to_all | solution.py:365
  55.4 0.9 %last.1 = (f32[5,8,8,128]{3,2,1,0:T(8,128)}, f32[1]{0:T(128)}) custom-call(s32[1]{0:T(128)S(6)} %copy.9.st_ref, f32[5,64,128]{2,1,0:T(8,128)S(1)} %get-tuple-element.21.own_ref, f32[5,8,128]{2,1,0:T(8,128)S(1)} %get-tuple-element.22.beyond_ref, f32[5,8,128]{2,1,0:T(8,128)S(1)} %collective-permute-done.10.edge_ref, ...), custom_call_target="tpu_custom_call" | custom-call | tf_op jit(solution)/shard_map/last/pallas_call | solution.py:367
  (1 shorter events, 0.0 us)
Async XLA Ops:
  0.6 6.3 %copy-start.1 = (s32[8,2]{0,1:T(2,128)S(1)}, s32[8,2]{0,1:T(2,128)}, u32[]{:S(2)}) copy-start(s32[8,2]{0,1:T(2,128)} %param.7) | copy-start | bytes 196
  0.6 17.1 %copy-start = (f32[1,5,8,8,128]{4,3,2,1,0:T(8,128)S(1)}, f32[1,5,8,8,128]{4,3,2,1,0:T(8,128)}, u32[]{:S(2)}) copy-start(f32[1,5,8,8,128]{4,3,2,1,0:T(8,128)} %param.4) | copy-start | bytes 491524
  0.6 2.2 %collective-permute-start.2 = (f32[5,64,128]{2,1,0:T(8,128)}, f32[5,64,128]{2,1,0:T(8,128)S(1)}, u32[]{:S(2)}, u32[]{:S(2)}) collective-permute-start(f32[5,64,128]{2,1,0:T(8,128)} %bitcast.2), channel_id=1, source_target_pairs={{0,256},{1,257},{2,258},{3,259},{4,260},{5,261},{6,262},{7,263},{8... | collective-permute-start | bytes 491528 | tf_op jit(solution)/shard_map/ppermute | solution.py:320
  1.5 2.7 %collective-permute-start = (f32[5,64,128]{2,1,0:T(8,128)}, f32[5,64,128]{2,1,0:T(8,128)S(1)}, u32[]{:S(2)}, u32[]{:S(2)}) collective-permute-start(f32[5,64,128]{2,1,0:T(8,128)} %bitcast.3), channel_id=1, source_target_pairs={{0,64},{1,65},{2,66},{3,67},{4,68},{5,69},{6,70},{7,71},{8,72},{9,... | collective-permute-start | bytes 491528 | tf_op jit(solution)/shard_map/ppermute | solution.py:320
  2.1 2.1 %collective-permute-start.1 = (f32[5,64,128]{2,1,0:T(8,128)}, f32[5,64,128]{2,1,0:T(8,128)S(1)}, u32[]{:S(2)}, u32[]{:S(2)}) collective-permute-start(f32[5,64,128]{2,1,0:T(8,128)} %bitcast.4), channel_id=1, source_target_pairs={{0,192},{1,193},{2,194},{3,195},{4,196},{5,197},{6,198},{7,199},{8... | collective-permute-start | bytes 491528 | tf_op jit(solution)/shard_map/ppermute | solution.py:320
  2.8 1.4 %collective-permute-start.3 = (f32[5,64,128]{2,1,0:T(8,128)S(1)}, f32[5,64,128]{2,1,0:T(8,128)S(1)}, u32[]{:S(2)}, u32[]{:S(2)}) collective-permute-start(f32[5,64,128]{2,1,0:T(8,128)S(1)} %collective-permute-done.2.p_ref), channel_id=1, source_target_pairs={{256,320},{257,321},{258,322},{259,323},{260,324},{261,325},{262,3... | collective-permute-start | bytes 491528 | tf_op jit(solution)/shard_map/ppermute | solution.py:320
  3.5 0.7 %collective-permute-start.4 = (f32[5,64,128]{2,1,0:T(8,128)S(1)}, f32[5,64,128]{2,1,0:T(8,128)S(1)}, u32[]{:S(2)}, u32[]{:S(2)}) collective-permute-start(f32[5,64,128]{2,1,0:T(8,128)S(1)} %collective-permute-done.2.p_ref), channel_id=1, source_target_pairs={{256,448},{257,449},{258,450},{259,451},{260,452},{261,453},{262,4... | collective-permute-start | bytes 491528 | tf_op jit(solution)/shard_map/ppermute | solution.py:320
  4.3 3.4 %collective-permute-start.5 = (f32[5,64,128]{2,1,0:T(8,128)S(1)}, f32[5,64,128]{2,1,0:T(8,128)S(1)}, u32[]{:S(2)}, u32[]{:S(2)}) collective-permute-start(f32[5,64,128]{2,1,0:T(8,128)S(1)} %add_add_fusion.y_ref), channel_id=1, source_target_pairs={{64,96},{192,224},{320,352},{448,480},{65,97},{193,225},{321,353},... | collective-permute-start | bytes 491528 | tf_op jit(solution)/shard_map/ppermute | solution.py:320
  5.0 2.7 %collective-permute-start.6 = (f32[5,64,128]{2,1,0:T(8,128)S(1)}, f32[5,64,128]{2,1,0:T(8,128)S(1)}, u32[]{:S(2)}, u32[]{:S(2)}) collective-permute-start(f32[5,64,128]{2,1,0:T(8,128)S(1)} %add_add_fusion.y_ref), channel_id=1, source_target_pairs={{64,32},{192,160},{320,288},{448,416},{65,33},{193,161},{321,289},... | collective-permute-start | bytes 491528 | tf_op jit(solution)/shard_map/ppermute | solution.py:320
  5.6 12.1 %collective-permute-start.7 = (f32[5,64,128]{2,1,0:T(8,128)S(1)}, f32[5,64,128]{2,1,0:T(8,128)S(1)}, u32[]{:S(2)}, u32[]{:S(2)}) collective-permute-start(f32[5,64,128]{2,1,0:T(8,128)S(1)} %add_add_fusion.y_ref), channel_id=1, source_target_pairs={{64,128},{320,384},{65,129},{321,385},{66,130},{322,386},{67,131},... | collective-permute-start | bytes 491528 | tf_op jit(solution)/shard_map/ppermute | solution.py:320
  18.5 18.0 %collective-permute-start.8 = (f32[30,8,128]{2,1,0:T(8,128)S(1)}, f32[30,8,128]{2,1,0:T(8,128)S(1)}, u32[]{:S(2)}, u32[]{:S(2)}) collective-permute-start(f32[30,8,128]{2,1,0:T(8,128)S(1)} %get-tuple-element.19), channel_id=1, source_target_pairs={{0,31},{1,2},{2,1},{3,4},{4,3},{5,6},{6,5},{7,8},{8,7},{9,10},{10,... | collective-permute-start | bytes 368648 | tf_op jit(solution)/shard_map/ppermute | solution.py:340
  29.3 7.2 %collective-permute-start.9 = (f32[30,8,128]{2,1,0:T(8,128)S(1)}, f32[30,8,128]{2,1,0:T(8,128)S(1)}, u32[]{:S(2)}, u32[]{:S(2)}) collective-permute-start(f32[30,8,128]{2,1,0:T(8,128)S(1)} %get-tuple-element.20), channel_id=1, source_target_pairs={{0,1},{1,0},{2,3},{3,2},{4,5},{5,4},{6,7},{7,6},{8,9},{9,8},{10,11... | collective-permute-start | bytes 368648 | tf_op jit(solution)/shard_map/ppermute | solution.py:339
  38.6 16.7 %all-to-all-start = ((f32[32,1,128]{2,1,0:T(1,128)}), f32[32,1,128]{2,1,0:T(1,128)S(1)}, u32[]{:S(2)}, u32[]{:S(2)}) async-start(f32[32,1,128]{2,1,0:T(1,128)} %get-tuple-element.25), calls=%async_computation | async-start | bytes 32768 | tf_op jit(solution)/shard_map/all_to_all | solution.py:365
  46.1 5.3 %collective-permute-start.10 = (f32[5,8,128]{2,1,0:T(8,128)S(1)}, f32[5,8,128]{2,1,0:T(8,128)S(1)}, u32[]{:S(2)}, u32[]{:S(2)}) collective-permute-start(f32[5,8,128]{2,1,0:T(8,128)S(1)} %get-tuple-element.23), channel_id=1, source_target_pairs={{0,1},{1,2},{2,3},{3,4},{4,5},{5,6},{6,7},{7,8},{8,9},{9,10},{10,1... | collective-permute-start | bytes 61448 | tf_op jit(solution)/shard_map/ppermute | solution.py:364

commit v7 on v6

--- a/solution.py
+++ b/solution.py
@@ -277,7 +277,7 @@
         beyond_ref[c] = new[c]
         edge_ref[c] = edge_of(own2_ref, c, 7)
     total = jnp.sum(total_ref[...], axis=0)
-    sum_ref[...] = jnp.broadcast_to(total[None, None], sum_ref.shape)
+    sum_ref[...] = jnp.broadcast_to(total[None], sum_ref.shape)
 
 
 def last_kernel(st_ref, own_ref, beyond_ref, edge_ref, d_ref, sums_ref, out_ref, misfit_ref, a_ref):
@@ -352,7 +352,7 @@
     own2, beyond, edge, d2, sums = pl.pallas_call(
         steps_kernel,
         out_shape=(
-            f32(*FLAT), f32(5, PLANES, 128), f32(5, PLANES, 128), f32(*BLOCK4), f32(TILES, 1, 128)
+            f32(*FLAT), f32(5, PLANES, 128), f32(5, PLANES, 128), f32(*BLOCK4), f32(TILES, 128)
         ),
         in_specs=[SM, SM, SM] + [VM] * 7,
         out_specs=(VM,) * 5,
@@ -362,7 +362,7 @@
     )(spacing_index, strength_index, obs_offsets, own, nat, d, own1, nat1, far, near)
 
     edge = lax.ppermute(edge, "tile", [(i, (i + 1) % TILES) for i in range(TILES)])
-    sums = lax.all_to_all(sums, "tile", 0, 0)
+    sums = lax.all_to_all(sums, "tile", 0, 0, tiled=True)
 
     out, misfit = pl.pallas_call(
         last_kernel,

time: 56.6 us -> 56.6 us (level)
  no operation moved by 1% of the time
where the time goes in v7:
time: 56.6 us; the launch traced here: 56.2 us
  starting transfers between devices  34.9 us (62%)
  waiting for transfers between devices  15 us (27%)
  Pallas kernels  4.15 us (7%)
  between operations  2.14 us (4%)
    ppermute x1, starting transfers between devices, shards(): far = lax.ppermute(far, 'tile', FAR)  10.8 us
    ppermute x8, waiting for transfers between devices, send(): return lax.ppermute(x, 'run', pairs)  10.1 us
    all_to_all x1, starting transfers between devices, shards(): sums = lax.all_to_all(sums, 'tile', 0, 0, tiled=True)  7.42 us
    ppermute x8, starting transfers between devices, send(): return lax.ppermute(x, 'run', pairs)  6.12 us
    ppermute x1, starting transfers between devices, shards(): near = lax.ppermute(near, 'tile', NEAR)  6.11 us
    ppermute x1, starting transfers between devices, shards(): lax.ppermute(edge, 'tile', [(i, (i + 1) % TILES) for i in range(TILES)])  4.44 us
    all_to_all x1, waiting for transfers between devices, shards(): sums = lax.all_to_all(sums, 'tile', 0, 0, tiled=True)  3.96 us
    pallas_call x1, Pallas kernels, shards(): pl.pallas_call(steps_kernel, out_shape=(f32(*FLAT), f32(5, PLANES, 128),...  2.12 us
  transfers between devices with their start and end apart: 12, of which 3 were waited for; matrix products, arithmetic and copies ran while one was open for 0% of the time, Pallas kernels for 1%

profile of v7, /device:TPU:97, one launch (start us, length us, event | category | flops | bytes accessed | tf_op | source)
XLA Modules:
  0.0 56.2 jit_solution(17515090995424569458)
XLA Ops:
  0.6 0.0 copy-start.1
  0.6 0.0 copy-start
  0.6 0.8 %collective-permute-start.2 = (f32[5,64,128]{2,1,0:T(8,128)}, f32[5,64,128]{2,1,0:T(8,128)S(1)}, u32[]{:S(2)}, u32[]{:S(2)}) collective-permute-start(f32[5,64,128]{2,1,0:T(8,128)} %bitcast.6), channel_id=1, source_target_pairs={{0,256},{1,257},{2,258},{3,259},{4,260},{5,261},{6,262},{7,263},{8... | collective-permute-start | bytes 491528 | tf_op jit(solution)/shard_map/ppermute | solution.py:320
  1.5 0.7 %collective-permute-start = (f32[5,64,128]{2,1,0:T(8,128)}, f32[5,64,128]{2,1,0:T(8,128)S(1)}, u32[]{:S(2)}, u32[]{:S(2)}) collective-permute-start(f32[5,64,128]{2,1,0:T(8,128)} %bitcast.7), channel_id=1, source_target_pairs={{0,64},{1,65},{2,66},{3,67},{4,68},{5,69},{6,70},{7,71},{8,72},{9,... | collective-permute-start | bytes 491528 | tf_op jit(solution)/shard_map/ppermute | solution.py:320
  2.1 0.7 %collective-permute-start.1 = (f32[5,64,128]{2,1,0:T(8,128)}, f32[5,64,128]{2,1,0:T(8,128)S(1)}, u32[]{:S(2)}, u32[]{:S(2)}) collective-permute-start(f32[5,64,128]{2,1,0:T(8,128)} %bitcast.8), channel_id=1, source_target_pairs={{0,192},{1,193},{2,194},{3,195},{4,196},{5,197},{6,198},{7,199},{8... | collective-permute-start | bytes 491528 | tf_op jit(solution)/shard_map/ppermute | solution.py:320
  2.8 0.0 collective-permute-done.2.p_ref
  2.8 0.7 %collective-permute-start.3 = (f32[5,64,128]{2,1,0:T(8,128)S(1)}, f32[5,64,128]{2,1,0:T(8,128)S(1)}, u32[]{:S(2)}, u32[]{:S(2)}) collective-permute-start(f32[5,64,128]{2,1,0:T(8,128)S(1)} %collective-permute-done.2.p_ref), channel_id=1, source_target_pairs={{256,320},{257,321},{258,322},{259,323},{260,324},{261,325},{262,3... | collective-permute-start | bytes 491528 | tf_op jit(solution)/shard_map/ppermute | solution.py:320
  3.5 0.7 %collective-permute-start.4 = (f32[5,64,128]{2,1,0:T(8,128)S(1)}, f32[5,64,128]{2,1,0:T(8,128)S(1)}, u32[]{:S(2)}, u32[]{:S(2)}) collective-permute-start(f32[5,64,128]{2,1,0:T(8,128)S(1)} %collective-permute-done.2.p_ref), channel_id=1, source_target_pairs={{256,448},{257,449},{258,450},{259,451},{260,452},{261,453},{262,4... | collective-permute-start | bytes 491528 | tf_op jit(solution)/shard_map/ppermute | solution.py:320
  4.2 0.0 collective-permute-done
  4.2 0.0 collective-permute-done.1
  4.2 0.0 collective-permute-done.3
  4.2 0.0 collective-permute-done.4
  4.3 0.7 %collective-permute-start.5 = (f32[5,64,128]{2,1,0:T(8,128)S(1)}, f32[5,64,128]{2,1,0:T(8,128)S(1)}, u32[]{:S(2)}, u32[]{:S(2)}) collective-permute-start(f32[5,64,128]{2,1,0:T(8,128)S(1)} %add_add_fusion.y_ref), channel_id=1, source_target_pairs={{64,96},{192,224},{320,352},{448,480},{65,97},{193,225},{321,353},... | collective-permute-start | bytes 491528 | tf_op jit(solution)/shard_map/ppermute | solution.py:320
  5.0 0.7 %collective-permute-start.6 = (f32[5,64,128]{2,1,0:T(8,128)S(1)}, f32[5,64,128]{2,1,0:T(8,128)S(1)}, u32[]{:S(2)}, u32[]{:S(2)}) collective-permute-start(f32[5,64,128]{2,1,0:T(8,128)S(1)} %add_add_fusion.y_ref), channel_id=1, source_target_pairs={{64,32},{192,160},{320,288},{448,416},{65,33},{193,161},{321,289},... | collective-permute-start | bytes 491528 | tf_op jit(solution)/shard_map/ppermute | solution.py:320
  5.6 1.3 %collective-permute-start.7 = (f32[5,64,128]{2,1,0:T(8,128)S(1)}, f32[5,64,128]{2,1,0:T(8,128)S(1)}, u32[]{:S(2)}, u32[]{:S(2)}) collective-permute-start(f32[5,64,128]{2,1,0:T(8,128)S(1)} %add_add_fusion.y_ref), channel_id=1, source_target_pairs={{64,128},{320,384},{65,129},{321,385},{66,130},{322,386},{67,131},... | collective-permute-start | bytes 491528 | tf_op jit(solution)/shard_map/ppermute | solution.py:320
  6.9 0.0 copy-done.1
  6.9 0.1 copy.9.off_ref
  7.7 0.0 collective-permute-done.5.u_ref
  7.7 0.0 collective-permute-done.6.v_ref
  7.7 10.1 %collective-permute-done.7.w_ref = f32[5,64,128]{2,1,0:T(8,128)S(1)} collective-permute-done((f32[5,64,128]{2,1,0:T(8,128)S(1)}, f32[5,64,128]{2,1,0:T(8,128)S(1)}, u32[]{:S(2)}, u32[]{:S(2)}) %collective-permute-start.7) | collective-permute-done | bytes 163872 | tf_op jit(solution)/shard_map/ppermute | solution.py:320
  17.8 0.0 copy-done
  17.8 0.8 %pack.1 = (f32[5,64,128]{2,1,0:T(8,128)S(1)}, f32[4,64,128]{2,1,0:T(8,128)S(1)}, f32[30,8,128]{2,1,0:T(8,128)S(1)}, f32[30,8,128]{2,1,0:T(8,128)S(1)}) custom-call(s32[1]{0:T(128)S(6)} %copy.11.sp_ref, s32[8,2]{1,0:T(8,128)S(1)} %copy.9.off_ref, f32[5,64,128]{2,1,0:T(8,128)S(1)} %bitcast.9, f32[5,64,128]{2,1,0:T(8,128)S(1)} %add_add_fusion.y_ref, ...), custom_call_target="tpu_custom_call" | custom-call | tf_op jit(solution)/shard_map/pack/pallas_call | solution.py:330
  18.5 10.8 %collective-permute-start.8 = (f32[30,8,128]{2,1,0:T(8,128)S(1)}, f32[30,8,128]{2,1,0:T(8,128)S(1)}, u32[]{:S(2)}, u32[]{:S(2)}) collective-permute-start(f32[30,8,128]{2,1,0:T(8,128)S(1)} %get-tuple-element.19), channel_id=1, source_target_pairs={{0,31},{1,2},{2,1},{3,4},{4,3},{5,6},{6,5},{7,8},{8,7},{9,10},{10,... | collective-permute-start | bytes 368648 | tf_op jit(solution)/shard_map/ppermute | solution.py:340
  29.3 6.1 %collective-permute-start.9 = (f32[30,8,128]{2,1,0:T(8,128)S(1)}, f32[30,8,128]{2,1,0:T(8,128)S(1)}, u32[]{:S(2)}, u32[]{:S(2)}) collective-permute-start(f32[30,8,128]{2,1,0:T(8,128)S(1)} %get-tuple-element.20), channel_id=1, source_target_pairs={{0,1},{1,0},{2,3},{3,2},{4,5},{5,4},{6,7},{7,6},{8,9},{9,8},{10,11... | collective-permute-start | bytes 368648 | tf_op jit(solution)/shard_map/ppermute | solution.py:339
  36.1 0.4 inner.1
  36.5 0.0 collective-permute-done.8.far_ref
  36.5 0.0 collective-permute-done.9.near_ref
  36.5 2.1 %steps.1 = (f32[5,64,128]{2,1,0:T(8,128)S(1)}, f32[5,8,128]{2,1,0:T(8,128)S(1)}, f32[5,8,128]{2,1,0:T(8,128)S(1)}, f32[4,8,8,128]{3,2,1,0:T(8,128)S(1)}, f32[32,128]{1,0:T(8,128)}) custom-call(s32[1]{0:T(128)S(6)} %copy.11.sp_ref, s32[1]{0:T(128)S(6)} %copy.12.st_ref, s32[8,2]{1,0:T(8,128)S(1)} %copy.9.off_ref, f32[5,64,128]{2,1,0:T(8,128)S(1)} %bitcast.11, ...), custom_call_target="tpu_custom_call" | custom-call | tf_op jit(solution)/shard_map/steps/pallas_call | solution.py:352
  38.6 7.4 %all-to-all-start = ((f32[32,1,128]{2,1,0:T(1,128)}), f32[32,1,128]{2,1,0:T(1,128)S(1)}, u32[]{:S(2)}, u32[]{:S(2)}) async-start(f32[32,1,128]{2,1,0:T(1,128)} %bitcast.2), calls=%async_computation | async-start | bytes 32768 | tf_op jit(solution)/shard_map/all_to_all | solution.py:365
  46.1 4.4 %collective-permute-start.10 = (f32[5,8,128]{2,1,0:T(8,128)S(1)}, f32[5,8,128]{2,1,0:T(8,128)S(1)}, u32[]{:S(2)}, u32[]{:S(2)}) collective-permute-start(f32[5,8,128]{2,1,0:T(8,128)S(1)} %get-tuple-element.23), channel_id=1, source_target_pairs={{0,1},{1,2},{2,3},{3,4},{4,5},{5,6},{6,7},{7,8},{8,9},{9,10},{10,1... | collective-permute-start | bytes 61448 | tf_op jit(solution)/shard_map/ppermute | solution.py:364
  50.5 0.9 %collective-permute-done.10.edge_ref = f32[5,8,128]{2,1,0:T(8,128)S(1)} collective-permute-done((f32[5,8,128]{2,1,0:T(8,128)S(1)}, f32[5,8,128]{2,1,0:T(8,128)S(1)}, u32[]{:S(2)}, u32[]{:S(2)}) %collective-permute-start.10) | collective-permute-done | bytes 20512 | tf_op jit(solution)/shard_map/ppermute | solution.py:364
  51.4 4.0 %all-to-all-done = f32[32,1,128]{2,1,0:T(1,128)S(1)} async-done(((f32[32,1,128]{2,1,0:T(1,128)}), f32[32,1,128]{2,1,0:T(1,128)S(1)}, u32[]{:S(2)}, u32[]{:S(2)}) %all-to-all-start) | async-done | bytes 16416 | tf_op jit(solution)/shard_map/all_to_all | solution.py:365
  55.4 0.9 %last.1 = (f32[5,8,8,128]{3,2,1,0:T(8,128)}, f32[1]{0:T(128)}) custom-call(s32[1]{0:T(128)S(6)} %copy.12.st_ref, f32[5,64,128]{2,1,0:T(8,128)S(1)} %get-tuple-element.21.own_ref, f32[5,8,128]{2,1,0:T(8,128)S(1)} %get-tuple-element.22.beyond_ref, f32[5,8,128]{2,1,0:T(8,128)S(1)} %collective-permute-done.10.edge_ref, ...), custom_call_target="tpu_custom_call" | custom-call | tf_op jit(solution)/shard_map/last/pallas_call | solution.py:367
  (1 shorter events, 0.0 us)
Async XLA Ops:
  0.6 6.3 %copy-start.1 = (s32[8,2]{0,1:T(2,128)S(1)}, s32[8,2]{0,1:T(2,128)}, u32[]{:S(2)}) copy-start(s32[8,2]{0,1:T(2,128)} %param.7) | copy-start | bytes 196
  0.6 17.1 %copy-start = (f32[1,5,8,8,128]{4,3,2,1,0:T(8,128)S(1)}, f32[1,5,8,8,128]{4,3,2,1,0:T(8,128)}, u32[]{:S(2)}) copy-start(f32[1,5,8,8,128]{4,3,2,1,0:T(8,128)} %param.4) | copy-start | bytes 491524
  0.6 2.2 %collective-permute-start.2 = (f32[5,64,128]{2,1,0:T(8,128)}, f32[5,64,128]{2,1,0:T(8,128)S(1)}, u32[]{:S(2)}, u32[]{:S(2)}) collective-permute-start(f32[5,64,128]{2,1,0:T(8,128)} %bitcast.6), channel_id=1, source_target_pairs={{0,256},{1,257},{2,258},{3,259},{4,260},{5,261},{6,262},{7,263},{8... | collective-permute-start | bytes 491528 | tf_op jit(solution)/shard_map/ppermute | solution.py:320
  1.5 2.7 %collective-permute-start = (f32[5,64,128]{2,1,0:T(8,128)}, f32[5,64,128]{2,1,0:T(8,128)S(1)}, u32[]{:S(2)}, u32[]{:S(2)}) collective-permute-start(f32[5,64,128]{2,1,0:T(8,128)} %bitcast.7), channel_id=1, source_target_pairs={{0,64},{1,65},{2,66},{3,67},{4,68},{5,69},{6,70},{7,71},{8,72},{9,... | collective-permute-start | bytes 491528 | tf_op jit(solution)/shard_map/ppermute | solution.py:320
  2.1 2.1 %collective-permute-start.1 = (f32[5,64,128]{2,1,0:T(8,128)}, f32[5,64,128]{2,1,0:T(8,128)S(1)}, u32[]{:S(2)}, u32[]{:S(2)}) collective-permute-start(f32[5,64,128]{2,1,0:T(8,128)} %bitcast.8), channel_id=1, source_target_pairs={{0,192},{1,193},{2,194},{3,195},{4,196},{5,197},{6,198},{7,199},{8... | collective-permute-start | bytes 491528 | tf_op jit(solution)/shard_map/ppermute | solution.py:320
  2.8 1.4 %collective-permute-start.3 = (f32[5,64,128]{2,1,0:T(8,128)S(1)}, f32[5,64,128]{2,1,0:T(8,128)S(1)}, u32[]{:S(2)}, u32[]{:S(2)}) collective-permute-start(f32[5,64,128]{2,1,0:T(8,128)S(1)} %collective-permute-done.2.p_ref), channel_id=1, source_target_pairs={{256,320},{257,321},{258,322},{259,323},{260,324},{261,325},{262,3... | collective-permute-start | bytes 491528 | tf_op jit(solution)/shard_map/ppermute | solution.py:320
  3.5 0.7 %collective-permute-start.4 = (f32[5,64,128]{2,1,0:T(8,128)S(1)}, f32[5,64,128]{2,1,0:T(8,128)S(1)}, u32[]{:S(2)}, u32[]{:S(2)}) collective-permute-start(f32[5,64,128]{2,1,0:T(8,128)S(1)} %collective-permute-done.2.p_ref), channel_id=1, source_target_pairs={{256,448},{257,449},{258,450},{259,451},{260,452},{261,453},{262,4... | collective-permute-start | bytes 491528 | tf_op jit(solution)/shard_map/ppermute | solution.py:320
  4.3 3.4 %collective-permute-start.5 = (f32[5,64,128]{2,1,0:T(8,128)S(1)}, f32[5,64,128]{2,1,0:T(8,128)S(1)}, u32[]{:S(2)}, u32[]{:S(2)}) collective-permute-start(f32[5,64,128]{2,1,0:T(8,128)S(1)} %add_add_fusion.y_ref), channel_id=1, source_target_pairs={{64,96},{192,224},{320,352},{448,480},{65,97},{193,225},{321,353},... | collective-permute-start | bytes 491528 | tf_op jit(solution)/shard_map/ppermute | solution.py:320
  5.0 2.7 %collective-permute-start.6 = (f32[5,64,128]{2,1,0:T(8,128)S(1)}, f32[5,64,128]{2,1,0:T(8,128)S(1)}, u32[]{:S(2)}, u32[]{:S(2)}) collective-permute-start(f32[5,64,128]{2,1,0:T(8,128)S(1)} %add_add_fusion.y_ref), channel_id=1, source_target_pairs={{64,32},{192,160},{320,288},{448,416},{65,33},{193,161},{321,289},... | collective-permute-start | bytes 491528 | tf_op jit(solution)/shard_map/ppermute | solution.py:320
  5.6 12.1 %collective-permute-start.7 = (f32[5,64,128]{2,1,0:T(8,128)S(1)}, f32[5,64,128]{2,1,0:T(8,128)S(1)}, u32[]{:S(2)}, u32[]{:S(2)}) collective-permute-start(f32[5,64,128]{2,1,0:T(8,128)S(1)} %add_add_fusion.y_ref), channel_id=1, source_target_pairs={{64,128},{320,384},{65,129},{321,385},{66,130},{322,386},{67,131},... | collective-permute-start | bytes 491528 | tf_op jit(solution)/shard_map/ppermute | solution.py:320
  18.5 18.0 %collective-permute-start.8 = (f32[30,8,128]{2,1,0:T(8,128)S(1)}, f32[30,8,128]{2,1,0:T(8,128)S(1)}, u32[]{:S(2)}, u32[]{:S(2)}) collective-permute-start(f32[30,8,128]{2,1,0:T(8,128)S(1)} %get-tuple-element.19), channel_id=1, source_target_pairs={{0,31},{1,2},{2,1},{3,4},{4,3},{5,6},{6,5},{7,8},{8,7},{9,10},{10,... | collective-permute-start | bytes 368648 | tf_op jit(solution)/shard_map/ppermute | solution.py:340
  29.3 7.2 %collective-permute-start.9 = (f32[30,8,128]{2,1,0:T(8,128)S(1)}, f32[30,8,128]{2,1,0:T(8,128)S(1)}, u32[]{:S(2)}, u32[]{:S(2)}) collective-permute-start(f32[30,8,128]{2,1,0:T(8,128)S(1)} %get-tuple-element.20), channel_id=1, source_target_pairs={{0,1},{1,0},{2,3},{3,2},{4,5},{5,4},{6,7},{7,6},{8,9},{9,8},{10,11... | collective-permute-start | bytes 368648 | tf_op jit(solution)/shard_map/ppermute | solution.py:339
  38.6 16.7 %all-to-all-start = ((f32[32,1,128]{2,1,0:T(1,128)}), f32[32,1,128]{2,1,0:T(1,128)S(1)}, u32[]{:S(2)}, u32[]{:S(2)}) async-start(f32[32,1,128]{2,1,0:T(1,128)} %bitcast.2), calls=%async_computation | async-start | bytes 32768 | tf_op jit(solution)/shard_map/all_to_all | solution.py:365
  46.1 5.3 %collective-permute-start.10 = (f32[5,8,128]{2,1,0:T(8,128)S(1)}, f32[5,8,128]{2,1,0:T(8,128)S(1)}, u32[]{:S(2)}, u32[]{:S(2)}) collective-permute-start(f32[5,8,128]{2,1,0:T(8,128)S(1)} %get-tuple-element.23), channel_id=1, source_target_pairs={{0,1},{1,2},{2,3},{3,4},{4,5},{5,6},{6,7},{7,8},{8,9},{9,10},{10,1... | collective-permute-start | bytes 61448 | tf_op jit(solution)/shard_map/ppermute | solution.py:364

commit v8 on v7

--- a/solution.py
+++ b/solution.py
@@ -166,7 +166,7 @@
 
 
 def pack_kernel(
-    sp_ref, off_ref, own_ref, y_ref, u_ref, v_ref, w_ref, p_ref, nat_ref, d_ref, near_ref, far_ref
+    sp_ref, off_ref, own_ref, y_ref, u_ref, v_ref, w_ref, p_ref, e_ref, nat_ref, d_ref, near_ref, far_ref
 ):
     spread = Spread(sp_ref, off_ref)
     even = even_tile()
@@ -176,7 +176,7 @@
         here = pl.ds(8 * z, 8)
         for c in range(5):
             own = own_ref[c, here]
-            nat = (y_ref[c, here] + u_ref[c, here]) + (v_ref[c, here] + w_ref[c, here]) + p_ref[c, here]
+            nat = (y_ref[c, here] + u_ref[c, here]) + (v_ref[c, here] + w_ref[c, here]) + (p_ref[c, here] + e_ref[c, here])
             nat = jnp.where(root, own, nat)
             nat_ref[c, here] = nat
             if c > 0:
@@ -320,21 +320,21 @@
         return lax.ppermute(x, "run", pairs)
 
     p = send(own, [(0, 8)])
-    a, b = send(own, [(0, 2)]), send(own, [(0, 6)])
+    a, b, e = send(own, [(0, 2)]), send(own, [(0, 6)]), send(own, [(0, 4)])
     f, g = send(p, [(8, 10)]), send(p, [(8, 14)])
     y = a + b + f + g
     u = send(y, [(2, 3), (6, 7), (10, 11), (14, 15)])
     v = send(y, [(2, 1), (6, 5), (10, 9), (14, 13)])
-    w = send(y, [(2, 4), (10, 12)])
+    w = send(y, [(10, 12)])
 
     nat, d, near, far = pl.pallas_call(
         pack_kernel,
         out_shape=(f32(*FLAT), f32(*FLAT4), f32(EDGES, 8, 128), f32(EDGES, 8, 128)),
-        in_specs=[SM, SM] + [VM] * 6,
+        in_specs=[SM, SM] + [VM] * 7,
         out_specs=(VM,) * 4,
         compiler_params=PARAMS,
         name="pack",
-    )(spacing_index, obs_offsets, own, y, u, v, w, p)
+    )(spacing_index, obs_offsets, own, y, u, v, w, p, e)
 
     near = lax.ppermute(near, "tile", NEAR)
     far = lax.ppermute(far, "tile", FAR)

time: 56.6 us -> 60.5 us (1.069)
  starting transfers between devices: 34.9 us -> 38 us
  waiting for transfers between devices: 15 us -> 15.7 us
    all_to_all x1, starting transfers between devices: 7.42 us -> 14 us  [shards(): sums = lax.all_to_all(sums, 'tile', 0, 0, tiled=True)]
    ppermute x1, starting transfers between devices: 10.8 us -> 4.85 us  [shards(): far = lax.ppermute(far, 'tile', FAR)]
    ppermute x1, starting transfers between devices: 6.11 us -> 7.85 us  [shards(): near = lax.ppermute(near, 'tile', NEAR)]
    ppermute x1, waiting for transfers between devices: 0.01 us -> 1.49 us  [shards(): far = lax.ppermute(far, 'tile', FAR)]
    ppermute x8 -> x9, waiting for transfers between devices: 10.1 us -> 9.41 us  [send(): return lax.ppermute(x, 'run', pairs)]
    ppermute x8 -> x9, starting transfers between devices: 6.12 us -> 6.79 us  [send(): return lax.ppermute(x, 'run', pairs)]
  transfers between devices with their start and end apart: 12 -> 13, of which waited for: 3 -> 4; matrix products, arithmetic and copies ran while one was open for 0% -> 0% of each run, Pallas kernels for 1% -> 1%
where the time goes in v8:
time: 60.5 us; the launch traced here: 60.1 us
  starting transfers between devices  38 us (63%)
  waiting for transfers between devices  15.7 us (26%)
  Pallas kernels  4.15 us (7%)
  between operations  2.15 us (4%)
    all_to_all x1, starting transfers between devices, shards(): sums = lax.all_to_all(sums, 'tile', 0, 0, tiled=True)  14 us
    ppermute x9, waiting for transfers between devices, send(): return lax.ppermute(x, 'run', pairs)  9.41 us
    ppermute x1, starting transfers between devices, shards(): near = lax.ppermute(near, 'tile', NEAR)  7.85 us
    ppermute x9, starting transfers between devices, send(): return lax.ppermute(x, 'run', pairs)  6.79 us
    ppermute x1, starting transfers between devices, shards(): far = lax.ppermute(far, 'tile', FAR)  4.85 us
    ppermute x1, starting transfers between devices, shards(): lax.ppermute(edge, 'tile', [(i, (i + 1) % TILES) for i in range(TILES)])  4.44 us
    all_to_all x1, waiting for transfers between devices, shards(): sums = lax.all_to_all(sums, 'tile', 0, 0, tiled=True)  3.96 us
    pallas_call x1, Pallas kernels, shards(): pl.pallas_call(steps_kernel, out_shape=(f32(*FLAT), f32(5, PLANES, 128),...  2.12 us
  transfers between devices with their start and end apart: 13, of which 4 were waited for; matrix products, arithmetic and copies ran while one was open for 0% of the time, Pallas kernels for 1%

profile of v8, /device:TPU:97, one launch (start us, length us, event | category | flops | bytes accessed | tf_op | source)
XLA Modules:
  0.0 60.1 jit_solution(11738230465554809418)
XLA Ops:
  0.6 0.0 copy-start.1
  0.6 0.0 copy-start
  0.6 0.8 %collective-permute-start.2 = (f32[5,64,128]{2,1,0:T(8,128)}, f32[5,64,128]{2,1,0:T(8,128)S(1)}, u32[]{:S(2)}, u32[]{:S(2)}) collective-permute-start(f32[5,64,128]{2,1,0:T(8,128)} %bitcast.6), channel_id=1, source_target_pairs={{0,256},{1,257},{2,258},{3,259},{4,260},{5,261},{6,262},{7,263},{8... | collective-permute-start | bytes 491528 | tf_op jit(solution)/shard_map/ppermute | solution.py:320
  1.5 0.7 %collective-permute-start = (f32[5,64,128]{2,1,0:T(8,128)}, f32[5,64,128]{2,1,0:T(8,128)S(1)}, u32[]{:S(2)}, u32[]{:S(2)}) collective-permute-start(f32[5,64,128]{2,1,0:T(8,128)} %bitcast.7), channel_id=1, source_target_pairs={{0,64},{1,65},{2,66},{3,67},{4,68},{5,69},{6,70},{7,71},{8,72},{9,... | collective-permute-start | bytes 491528 | tf_op jit(solution)/shard_map/ppermute | solution.py:320
  2.1 0.7 %collective-permute-start.1 = (f32[5,64,128]{2,1,0:T(8,128)}, f32[5,64,128]{2,1,0:T(8,128)S(1)}, u32[]{:S(2)}, u32[]{:S(2)}) collective-permute-start(f32[5,64,128]{2,1,0:T(8,128)} %bitcast.8), channel_id=1, source_target_pairs={{0,192},{1,193},{2,194},{3,195},{4,196},{5,197},{6,198},{7,199},{8... | collective-permute-start | bytes 491528 | tf_op jit(solution)/shard_map/ppermute | solution.py:320
  2.8 0.0 collective-permute-done.2.p_ref
  2.8 0.7 %collective-permute-start.3 = (f32[5,64,128]{2,1,0:T(8,128)S(1)}, f32[5,64,128]{2,1,0:T(8,128)S(1)}, u32[]{:S(2)}, u32[]{:S(2)}) collective-permute-start(f32[5,64,128]{2,1,0:T(8,128)S(1)} %collective-permute-done.2.p_ref), channel_id=1, source_target_pairs={{256,320},{257,321},{258,322},{259,323},{260,324},{261,325},{262,3... | collective-permute-start | bytes 491528 | tf_op jit(solution)/shard_map/ppermute | solution.py:320
  3.5 0.7 %collective-permute-start.4 = (f32[5,64,128]{2,1,0:T(8,128)S(1)}, f32[5,64,128]{2,1,0:T(8,128)S(1)}, u32[]{:S(2)}, u32[]{:S(2)}) collective-permute-start(f32[5,64,128]{2,1,0:T(8,128)S(1)} %collective-permute-done.2.p_ref), channel_id=1, source_target_pairs={{256,448},{257,449},{258,450},{259,451},{260,452},{261,453},{262,4... | collective-permute-start | bytes 491528 | tf_op jit(solution)/shard_map/ppermute | solution.py:320
  4.2 0.7 %collective-permute-start.8 = (f32[5,64,128]{2,1,0:T(8,128)}, f32[5,64,128]{2,1,0:T(8,128)S(1)}, u32[]{:S(2)}, u32[]{:S(2)}) collective-permute-start(f32[5,64,128]{2,1,0:T(8,128)} %bitcast.9), channel_id=1, source_target_pairs={{0,128},{1,129},{2,130},{3,131},{4,132},{5,133},{6,134},{7,135},{8... | collective-permute-start | bytes 491528 | tf_op jit(solution)/shard_map/ppermute | solution.py:320
  4.9 0.0 collective-permute-done
  4.9 0.0 collective-permute-done.1
  4.9 0.0 collective-permute-done.3
  4.9 0.0 collective-permute-done.4
  5.0 0.7 %collective-permute-start.5 = (f32[5,64,128]{2,1,0:T(8,128)S(1)}, f32[5,64,128]{2,1,0:T(8,128)S(1)}, u32[]{:S(2)}, u32[]{:S(2)}) collective-permute-start(f32[5,64,128]{2,1,0:T(8,128)S(1)} %add_add_fusion.y_ref), channel_id=1, source_target_pairs={{64,96},{192,224},{320,352},{448,480},{65,97},{193,225},{321,353},... | collective-permute-start | bytes 491528 | tf_op jit(solution)/shard_map/ppermute | solution.py:320
  5.6 0.7 %collective-permute-start.6 = (f32[5,64,128]{2,1,0:T(8,128)S(1)}, f32[5,64,128]{2,1,0:T(8,128)S(1)}, u32[]{:S(2)}, u32[]{:S(2)}) collective-permute-start(f32[5,64,128]{2,1,0:T(8,128)S(1)} %add_add_fusion.y_ref), channel_id=1, source_target_pairs={{64,32},{192,160},{320,288},{448,416},{65,33},{193,161},{321,289},... | collective-permute-start | bytes 491528 | tf_op jit(solution)/shard_map/ppermute | solution.py:320
  6.3 1.3 %collective-permute-start.7 = (f32[5,64,128]{2,1,0:T(8,128)S(1)}, f32[5,64,128]{2,1,0:T(8,128)S(1)}, u32[]{:S(2)}, u32[]{:S(2)}) collective-permute-start(f32[5,64,128]{2,1,0:T(8,128)S(1)} %add_add_fusion.y_ref), channel_id=1, source_target_pairs={{320,384},{321,385},{322,386},{323,387},{324,388},{325,389},{326,3... | collective-permute-start | bytes 491528 | tf_op jit(solution)/shard_map/ppermute | solution.py:320
  7.6 0.0 copy-done.1
  7.6 0.1 copy.9.off_ref
  8.4 0.0 collective-permute-done.8.e_ref
  8.4 0.0 collective-permute-done.5.u_ref
  8.4 0.0 collective-permute-done.6.v_ref
  8.4 9.4 %collective-permute-done.7.w_ref = f32[5,64,128]{2,1,0:T(8,128)S(1)} collective-permute-done((f32[5,64,128]{2,1,0:T(8,128)S(1)}, f32[5,64,128]{2,1,0:T(8,128)S(1)}, u32[]{:S(2)}, u32[]{:S(2)}) %collective-permute-start.7) | collective-permute-done | bytes 163872 | tf_op jit(solution)/shard_map/ppermute | solution.py:320
  17.8 0.0 copy-done
  17.8 0.8 %pack.1 = (f32[5,64,128]{2,1,0:T(8,128)S(1)}, f32[4,64,128]{2,1,0:T(8,128)S(1)}, f32[30,8,128]{2,1,0:T(8,128)S(1)}, f32[30,8,128]{2,1,0:T(8,128)S(1)}) custom-call(s32[1]{0:T(128)S(6)} %copy.11.sp_ref, s32[8,2]{1,0:T(8,128)S(1)} %copy.9.off_ref, f32[5,64,128]{2,1,0:T(8,128)S(1)} %bitcast.10, f32[5,64,128]{2,1,0:T(8,128)S(1)} %add_add_fusion.y_ref, ...), custom_call_target="tpu_custom_call" | custom-call | tf_op jit(solution)/shard_map/pack/pallas_call | solution.py:330
  18.5 7.9 %collective-permute-start.10 = (f32[30,8,128]{2,1,0:T(8,128)S(1)}, f32[30,8,128]{2,1,0:T(8,128)S(1)}, u32[]{:S(2)}, u32[]{:S(2)}) collective-permute-start(f32[30,8,128]{2,1,0:T(8,128)S(1)} %get-tuple-element.20), channel_id=1, source_target_pairs={{0,1},{1,0},{2,3},{3,2},{4,5},{5,4},{6,7},{7,6},{8,9},{9,8},{10,11... | collective-permute-start | bytes 368648 | tf_op jit(solution)/shard_map/ppermute | solution.py:339
  26.4 4.9 %collective-permute-start.9 = (f32[30,8,128]{2,1,0:T(8,128)S(1)}, f32[30,8,128]{2,1,0:T(8,128)S(1)}, u32[]{:S(2)}, u32[]{:S(2)}) collective-permute-start(f32[30,8,128]{2,1,0:T(8,128)S(1)} %get-tuple-element.19), channel_id=1, source_target_pairs={{0,31},{1,2},{2,1},{3,4},{4,3},{5,6},{6,5},{7,8},{8,7},{9,10},{10,... | collective-permute-start | bytes 368648 | tf_op jit(solution)/shard_map/ppermute | solution.py:340
  31.9 0.4 inner.1
  32.3 0.0 collective-permute-done.10.near_ref
  32.3 1.5 %collective-permute-done.9.far_ref = f32[30,8,128]{2,1,0:T(8,128)S(1)} collective-permute-done((f32[30,8,128]{2,1,0:T(8,128)S(1)}, f32[30,8,128]{2,1,0:T(8,128)S(1)}, u32[]{:S(2)}, u32[]{:S(2)}) %collective-permute-start.9) | collective-permute-done | bytes 122912 | tf_op jit(solution)/shard_map/ppermute | solution.py:340
  33.8 2.1 %steps.1 = (f32[5,64,128]{2,1,0:T(8,128)S(1)}, f32[5,8,128]{2,1,0:T(8,128)S(1)}, f32[5,8,128]{2,1,0:T(8,128)S(1)}, f32[4,8,8,128]{3,2,1,0:T(8,128)S(1)}, f32[32,128]{1,0:T(8,128)}) custom-call(s32[1]{0:T(128)S(6)} %copy.11.sp_ref, s32[1]{0:T(128)S(6)} %copy.12.st_ref, s32[8,2]{1,0:T(8,128)S(1)} %copy.9.off_ref, f32[5,64,128]{2,1,0:T(8,128)S(1)} %bitcast.12, ...), custom_call_target="tpu_custom_call" | custom-call | tf_op jit(solution)/shard_map/steps/pallas_call | solution.py:352
  35.9 14.0 %all-to-all-start = ((f32[32,1,128]{2,1,0:T(1,128)}), f32[32,1,128]{2,1,0:T(1,128)S(1)}, u32[]{:S(2)}, u32[]{:S(2)}) async-start(f32[32,1,128]{2,1,0:T(1,128)} %bitcast.2), calls=%async_computation | async-start | bytes 32768 | tf_op jit(solution)/shard_map/all_to_all | solution.py:365
  50.0 4.4 %collective-permute-start.11 = (f32[5,8,128]{2,1,0:T(8,128)S(1)}, f32[5,8,128]{2,1,0:T(8,128)S(1)}, u32[]{:S(2)}, u32[]{:S(2)}) collective-permute-start(f32[5,8,128]{2,1,0:T(8,128)S(1)} %get-tuple-element.23), channel_id=1, source_target_pairs={{0,1},{1,2},{2,3},{3,4},{4,5},{5,6},{6,7},{7,8},{8,9},{9,10},{10,1... | collective-permute-start | bytes 61448 | tf_op jit(solution)/shard_map/ppermute | solution.py:364
  54.4 0.9 %collective-permute-done.11.edge_ref = f32[5,8,128]{2,1,0:T(8,128)S(1)} collective-permute-done((f32[5,8,128]{2,1,0:T(8,128)S(1)}, f32[5,8,128]{2,1,0:T(8,128)S(1)}, u32[]{:S(2)}, u32[]{:S(2)}) %collective-permute-start.11) | collective-permute-done | bytes 20512 | tf_op jit(solution)/shard_map/ppermute | solution.py:364
  55.3 4.0 %all-to-all-done = f32[32,1,128]{2,1,0:T(1,128)S(1)} async-done(((f32[32,1,128]{2,1,0:T(1,128)}), f32[32,1,128]{2,1,0:T(1,128)S(1)}, u32[]{:S(2)}, u32[]{:S(2)}) %all-to-all-start) | async-done | bytes 16416 | tf_op jit(solution)/shard_map/all_to_all | solution.py:365
  59.3 0.9 %last.1 = (f32[5,8,8,128]{3,2,1,0:T(8,128)}, f32[1]{0:T(128)}) custom-call(s32[1]{0:T(128)S(6)} %copy.12.st_ref, f32[5,64,128]{2,1,0:T(8,128)S(1)} %get-tuple-element.21.own_ref, f32[5,8,128]{2,1,0:T(8,128)S(1)} %get-tuple-element.22.beyond_ref, f32[5,8,128]{2,1,0:T(8,128)S(1)} %collective-permute-done.11.edge_ref, ...), custom_call_target="tpu_custom_call" | custom-call | tf_op jit(solution)/shard_map/last/pallas_call | solution.py:367
  (1 shorter events, 0.0 us)
Async XLA Ops:
  0.6 7.0 %copy-start.1 = (s32[8,2]{0,1:T(2,128)S(1)}, s32[8,2]{0,1:T(2,128)}, u32[]{:S(2)}) copy-start(s32[8,2]{0,1:T(2,128)} %param.7) | copy-start | bytes 196
  0.6 17.1 %copy-start = (f32[1,5,8,8,128]{4,3,2,1,0:T(8,128)S(1)}, f32[1,5,8,8,128]{4,3,2,1,0:T(8,128)}, u32[]{:S(2)}) copy-start(f32[1,5,8,8,128]{4,3,2,1,0:T(8,128)} %param.4) | copy-start | bytes 491524
  0.6 2.2 %collective-permute-start.2 = (f32[5,64,128]{2,1,0:T(8,128)}, f32[5,64,128]{2,1,0:T(8,128)S(1)}, u32[]{:S(2)}, u32[]{:S(2)}) collective-permute-start(f32[5,64,128]{2,1,0:T(8,128)} %bitcast.6), channel_id=1, source_target_pairs={{0,256},{1,257},{2,258},{3,259},{4,260},{5,261},{6,262},{7,263},{8... | collective-permute-start | bytes 491528 | tf_op jit(solution)/shard_map/ppermute | solution.py:320
  1.5 3.4 %collective-permute-start = (f32[5,64,128]{2,1,0:T(8,128)}, f32[5,64,128]{2,1,0:T(8,128)S(1)}, u32[]{:S(2)}, u32[]{:S(2)}) collective-permute-start(f32[5,64,128]{2,1,0:T(8,128)} %bitcast.7), channel_id=1, source_target_pairs={{0,64},{1,65},{2,66},{3,67},{4,68},{5,69},{6,70},{7,71},{8,72},{9,... | collective-permute-start | bytes 491528 | tf_op jit(solution)/shard_map/ppermute | solution.py:320
  2.1 2.7 %collective-permute-start.1 = (f32[5,64,128]{2,1,0:T(8,128)}, f32[5,64,128]{2,1,0:T(8,128)S(1)}, u32[]{:S(2)}, u32[]{:S(2)}) collective-permute-start(f32[5,64,128]{2,1,0:T(8,128)} %bitcast.8), channel_id=1, source_target_pairs={{0,192},{1,193},{2,194},{3,195},{4,196},{5,197},{6,198},{7,199},{8... | collective-permute-start | bytes 491528 | tf_op jit(solution)/shard_map/ppermute | solution.py:320
  2.8 2.1 %collective-permute-start.3 = (f32[5,64,128]{2,1,0:T(8,128)S(1)}, f32[5,64,128]{2,1,0:T(8,128)S(1)}, u32[]{:S(2)}, u32[]{:S(2)}) collective-permute-start(f32[5,64,128]{2,1,0:T(8,128)S(1)} %collective-permute-done.2.p_ref), channel_id=1, source_target_pairs={{256,320},{257,321},{258,322},{259,323},{260,324},{261,325},{262,3... | collective-permute-start | bytes 491528 | tf_op jit(solution)/shard_map/ppermute | solution.py:320
  3.5 1.4 %collective-permute-start.4 = (f32[5,64,128]{2,1,0:T(8,128)S(1)}, f32[5,64,128]{2,1,0:T(8,128)S(1)}, u32[]{:S(2)}, u32[]{:S(2)}) collective-permute-start(f32[5,64,128]{2,1,0:T(8,128)S(1)} %collective-permute-done.2.p_ref), channel_id=1, source_target_pairs={{256,448},{257,449},{258,450},{259,451},{260,452},{261,453},{262,4... | collective-permute-start | bytes 491528 | tf_op jit(solution)/shard_map/ppermute | solution.py:320
  4.2 4.2 %collective-permute-start.8 = (f32[5,64,128]{2,1,0:T(8,128)}, f32[5,64,128]{2,1,0:T(8,128)S(1)}, u32[]{:S(2)}, u32[]{:S(2)}) collective-permute-start(f32[5,64,128]{2,1,0:T(8,128)} %bitcast.9), channel_id=1, source_target_pairs={{0,128},{1,129},{2,130},{3,131},{4,132},{5,133},{6,134},{7,135},{8... | collective-permute-start | bytes 491528 | tf_op jit(solution)/shard_map/ppermute | solution.py:320
  5.0 3.4 %collective-permute-start.5 = (f32[5,64,128]{2,1,0:T(8,128)S(1)}, f32[5,64,128]{2,1,0:T(8,128)S(1)}, u32[]{:S(2)}, u32[]{:S(2)}) collective-permute-start(f32[5,64,128]{2,1,0:T(8,128)S(1)} %add_add_fusion.y_ref), channel_id=1, source_target_pairs={{64,96},{192,224},{320,352},{448,480},{65,97},{193,225},{321,353},... | collective-permute-start | bytes 491528 | tf_op jit(solution)/shard_map/ppermute | solution.py:320
  5.6 2.7 %collective-permute-start.6 = (f32[5,64,128]{2,1,0:T(8,128)S(1)}, f32[5,64,128]{2,1,0:T(8,128)S(1)}, u32[]{:S(2)}, u32[]{:S(2)}) collective-permute-start(f32[5,64,128]{2,1,0:T(8,128)S(1)} %add_add_fusion.y_ref), channel_id=1, source_target_pairs={{64,32},{192,160},{320,288},{448,416},{65,33},{193,161},{321,289},... | collective-permute-start | bytes 491528 | tf_op jit(solution)/shard_map/ppermute | solution.py:320
  6.3 11.5 %collective-permute-start.7 = (f32[5,64,128]{2,1,0:T(8,128)S(1)}, f32[5,64,128]{2,1,0:T(8,128)S(1)}, u32[]{:S(2)}, u32[]{:S(2)}) collective-permute-start(f32[5,64,128]{2,1,0:T(8,128)S(1)} %add_add_fusion.y_ref), channel_id=1, source_target_pairs={{320,384},{321,385},{322,386},{323,387},{324,388},{325,389},{326,3... | collective-permute-start | bytes 491528 | tf_op jit(solution)/shard_map/ppermute | solution.py:320
  18.5 13.8 %collective-permute-start.10 = (f32[30,8,128]{2,1,0:T(8,128)S(1)}, f32[30,8,128]{2,1,0:T(8,128)S(1)}, u32[]{:S(2)}, u32[]{:S(2)}) collective-permute-start(f32[30,8,128]{2,1,0:T(8,128)S(1)} %get-tuple-element.20), channel_id=1, source_target_pairs={{0,1},{1,0},{2,3},{3,2},{4,5},{5,4},{6,7},{7,6},{8,9},{9,8},{10,11... | collective-permute-start | bytes 368648 | tf_op jit(solution)/shard_map/ppermute | solution.py:339
  26.4 7.4 %collective-permute-start.9 = (f32[30,8,128]{2,1,0:T(8,128)S(1)}, f32[30,8,128]{2,1,0:T(8,128)S(1)}, u32[]{:S(2)}, u32[]{:S(2)}) collective-permute-start(f32[30,8,128]{2,1,0:T(8,128)S(1)} %get-tuple-element.19), channel_id=1, source_target_pairs={{0,31},{1,2},{2,1},{3,4},{4,3},{5,6},{6,5},{7,8},{8,7},{9,10},{10,... | collective-permute-start | bytes 368648 | tf_op jit(solution)/shard_map/ppermute | solution.py:340
  35.9 23.3 %all-to-all-start = ((f32[32,1,128]{2,1,0:T(1,128)}), f32[32,1,128]{2,1,0:T(1,128)S(1)}, u32[]{:S(2)}, u32[]{:S(2)}) async-start(f32[32,1,128]{2,1,0:T(1,128)} %bitcast.2), calls=%async_computation | async-start | bytes 32768 | tf_op jit(solution)/shard_map/all_to_all | solution.py:365
  50.0 5.3 %collective-permute-start.11 = (f32[5,8,128]{2,1,0:T(8,128)S(1)}, f32[5,8,128]{2,1,0:T(8,128)S(1)}, u32[]{:S(2)}, u32[]{:S(2)}) collective-permute-start(f32[5,8,128]{2,1,0:T(8,128)S(1)} %get-tuple-element.23), channel_id=1, source_target_pairs={{0,1},{1,2},{2,3},{3,4},{4,5},{5,6},{6,7},{7,8},{8,9},{9,10},{10,1... | collective-permute-start | bytes 61448 | tf_op jit(solution)/shard_map/ppermute | solution.py:364
